TPU v7x, 256 devices: a whole 4x4x8 slice. The times are simulated.
256 devices in a mesh: gx: 16 (over y_hi, x, core), gy: 16 (over y_lo, z).
Axes of the slice: x: 4, y: 4 (y_hi: 2, y_lo: 2; y = y_hi * 2 + y_lo), z: 8, core: 2. Of those that a mesh axis runs over, the one named last changes fastest.
Arguments:
- nodes: bfloat16 [16, 16, 64, 512], P('gx', 'gy'), may hold values from -6 to 6
- edges: bfloat16 [16, 16, 384, 512], P('gx', 'gy'), may hold values from -6 to 6
- senders: int32 [16, 16, 384], P('gx', 'gy'), may hold values from 0 to 127, as said below
- segments: int32 [16, 16, 384], P('gx', 'gy'), may hold values from 0 to 63, never falling along the last dimension, each value on 1 to 12 neighbouring positions
- send_lists: int32 [16, 16, 4, 16], P('gx', 'gy'), may hold values from 0 to 63
- cot_nodes: bfloat16 [16, 16, 64, 512], P('gx', 'gy'), may hold values from -6 to 6
- cot_edges: bfloat16 [16, 16, 384, 512], P('gx', 'gy'), may hold values from -6 to 6
- w_edge1: bfloat16 [1536, 512], replicated, may hold values from -0.15625 to 0.15625
- w_edge2: bfloat16 [512, 512], replicated, may hold values from -0.25 to 0.25
- w_node1: bfloat16 [1024, 512], replicated, may hold values from -0.1875 to 0.1875
- w_node2: bfloat16 [512, 512], replicated, may hold values from -0.25 to 0.25
Outputs:
- node_next: bfloat16 [16, 16, 64, 512], P('gx', 'gy')
- grad_nodes: bfloat16 [16, 16, 64, 512], P('gx', 'gy')
- grad_edges: bfloat16 [16, 16, 384, 512], P('gx', 'gy')
- grad_we1: bfloat16 [1536, 512], replicated
- grad_we2: bfloat16 [512, 512], replicated
- grad_wn1: bfloat16 [1024, 512], replicated
- grad_wn2: bfloat16 [512, 512], replicated
Inputs may be any that keep to these rules, and one draw needn't show every extreme that they name: `senders`: below 64 an edge's sender is an owned node; a value 64 + k * 16 + r names row r of halo block k (lower row, upper row, lower column, upper column neighbour); blocks of neighbours outside the grid are never named. `segments`: never falls along a tile's edge list; every owned node receives 1 to 12 edges. `send_lists`: entries may repeat; not every sent row need be named by a receiving edge.
All inputs are finite; a program needn't handle non-finite values.
Results may differ from a plain program's by a relative error of at most 0.012.
Values may be sent and summed in bfloat16 or wider, within the bound.
No kernel may reach another device: no remote copies, remote signals or barrier semaphores. Data moves between devices by JAX's collectives and lax.ppermute only.
A program may use at most 64 MiB of HBM per device.

v0:
```python
import jax
import jax.numpy as jnp
from jax import lax
from jax.sharding import PartitionSpec as P


def with_halo(block, sides, width):
    for axis, dim in sides:
        count = lax.axis_size(axis)
        forward = [(i, i + 1) for i in range(count - 1)]
        backward = [(target, source) for source, target in forward]
        low = lax.ppermute(
            lax.slice_in_dim(block, block.shape[dim] - width, None, axis=dim), axis, forward
        )
        high = lax.ppermute(lax.slice_in_dim(block, 0, width, axis=dim), axis, backward)
        block = jnp.concatenate([low, block, high], axis=dim)
    return block


def layer_norm(values):
    mean = jnp.mean(values, axis=-1, keepdims=True)
    centred = values - mean
    scale = lax.rsqrt(jnp.mean(centred * centred, axis=-1, keepdims=True) + 1e-05)
    return (centred * scale, scale)


def norm_back(grad, normed, scale):
    first = jnp.mean(grad, axis=-1, keepdims=True)
    second = jnp.mean(grad * normed, axis=-1, keepdims=True)
    return scale * (grad - first - normed * second)


def silu_slope(values):
    sig = jax.nn.sigmoid(values)
    return sig * (1.0 + values * (1.0 - sig))


def inner_rows(left, right):
    return lax.dot_general(
        left, right, (((0,), (0,)), ((), ())), preferred_element_type=jnp.float32
    )


def outer_cols(left, right):
    return lax.dot_general(
        left, right, (((1,), (1,)), ((), ())), preferred_element_type=jnp.float32
    )


def local_pass(
    edge_lat,
    node_lat,
    ext,
    senders,
    segments,
    cot_node,
    cot_edge,
    w_edge1,
    w_edge2,
    w_node1,
    w_node2,
):
    count = node_lat.shape[0]
    width = node_lat.shape[1]
    sent = jnp.take(ext, senders, axis=0)
    recv = jnp.take(node_lat, segments, axis=0)
    x_edge = jnp.concatenate([edge_lat, sent, recv], axis=1)
    z_one = jnp.dot(x_edge, w_edge1, preferred_element_type=jnp.float32)
    a_one = jax.nn.silu(z_one).astype(jnp.bfloat16)
    z_two = jnp.dot(a_one, w_edge2, preferred_element_type=jnp.float32)
    n_two, s_two = layer_norm(z_two)
    e_new = (edge_lat.astype(jnp.float32) + n_two).astype(jnp.bfloat16)
    onehot = segments[None, :] == jnp.arange(count, dtype=jnp.int32)[:, None]
    agg = jnp.dot(onehot.astype(jnp.bfloat16), e_new, preferred_element_type=jnp.float32).astype(
        jnp.bfloat16
    )
    y_node = jnp.concatenate([node_lat, agg], axis=1)
    z_three = jnp.dot(y_node, w_node1, preferred_element_type=jnp.float32)
    a_three = jax.nn.silu(z_three).astype(jnp.bfloat16)
    z_four = jnp.dot(a_three, w_node2, preferred_element_type=jnp.float32)
    n_four, s_four = layer_norm(z_four)
    node_new = (node_lat.astype(jnp.float32) + n_four).astype(jnp.bfloat16)
    g_node = cot_node.astype(jnp.float32)
    dz_four = norm_back(g_node, n_four, s_four).astype(jnp.bfloat16)
    dw_node2 = inner_rows(a_three, dz_four)
    da_three = outer_cols(dz_four, w_node2)
    dz_three = (da_three * silu_slope(z_three)).astype(jnp.bfloat16)
    dw_node1 = inner_rows(y_node, dz_three)
    d_ynode = outer_cols(dz_three, w_node1)
    de_new = cot_edge.astype(jnp.float32) + jnp.take(d_ynode[:, width:], segments, axis=0)
    dz_two = norm_back(de_new, n_two, s_two).astype(jnp.bfloat16)
    dw_edge2 = inner_rows(a_one, dz_two)
    da_one = outer_cols(dz_two, w_edge2)
    dz_one = (da_one * silu_slope(z_one)).astype(jnp.bfloat16)
    dw_edge1 = inner_rows(x_edge, dz_one)
    d_xedge = outer_cols(dz_one, w_edge1)
    grad_edge = (de_new + d_xedge[:, :width]).astype(jnp.bfloat16)
    by_recv = jnp.dot(
        onehot.astype(jnp.float32), d_xedge[:, 2 * width :], precision=lax.Precision.HIGHEST
    )
    by_send = jax.ops.segment_sum(d_xedge[:, width : 2 * width], senders, num_segments=ext.shape[0])
    d_node = g_node + d_ynode[:, :width] + by_recv + by_send[:count]
    return (node_new, grad_edge, d_node, by_send[count:], (dw_edge1, dw_edge2, dw_node1, dw_node2))


def local(
    nodes,
    edges,
    senders,
    segments,
    send_lists,
    cot_nodes,
    cot_edges,
    w_edge1,
    w_edge2,
    w_node1,
    w_node2,
):
    node_lat = nodes[0, 0]
    width = node_lat.shape[1]
    lists = send_lists[0, 0]
    rows = lists.shape[1]
    packs = jnp.take(node_lat, lists.reshape(-1), axis=0).reshape(4, rows, width)
    along_x = with_halo(packs[0:2], (("gx", 0),), 1)
    along_y = with_halo(packs[2:4], (("gy", 0),), 1)
    ext = jnp.concatenate([node_lat, along_x[0], along_x[3], along_y[0], along_y[3]], axis=0)
    node_new, grad_edge, d_node, halo_grad, weights = local_pass(
        edges[0, 0],
        node_lat,
        ext,
        senders[0, 0],
        segments[0, 0],
        cot_nodes[0, 0],
        cot_edges[0, 0],
        w_edge1,
        w_edge2,
        w_node1,
        w_node2,
    )
    halo_grad = halo_grad.reshape(4, rows, width)
    back_rows = with_halo(halo_grad[0:2].astype(jnp.bfloat16), (("gx", 0),), 1).astype(jnp.float32)
    back_cols = with_halo(halo_grad[2:4].astype(jnp.bfloat16), (("gy", 0),), 1).astype(jnp.float32)
    returned = jnp.stack([back_rows[0], back_rows[3], back_cols[0], back_cols[3]], axis=0)
    d_node = d_node.at[lists.reshape(-1)].add(returned.reshape(-1, width))
    devices = lax.axis_size("gx") * lax.axis_size("gy")
    factor = 1.0 / jnp.sqrt(jnp.float32(edges.shape[2] * devices))
    sums = lax.psum((weights[0], weights[1], weights[2], weights[3]), ("gx", "gy"))
    grads = tuple(((total * factor).astype(jnp.bfloat16) for total in sums))
    return (
        node_new[None, None],
        d_node.astype(jnp.bfloat16)[None, None],
        grad_edge[None, None],
        grads[0],
        grads[1],
        grads[2],
        grads[3],
    )


def solution(mesh):
    return jax.shard_map(
        local,
        mesh=mesh,
        in_specs=(
            P("gx", "gy", None, None),
            P("gx", "gy", None, None),
            P("gx", "gy", None),
            P("gx", "gy", None),
            P("gx", "gy", None, None),
            P("gx", "gy", None, None),
            P("gx", "gy", None, None),
            P(),
            P(),
            P(),
            P(),
        ),
        out_specs=(
            P("gx", "gy", None, None),
            P("gx", "gy", None, None),
            P("gx", "gy", None, None),
            P(),
            P(),
            P(),
            P(),
        ),
        check_vma=False,
    )
```

profile of v0, /device:TPU:1, one launch (start us, length us, event | category | flops | bytes accessed | tf_op | source)
XLA Modules:
  0.0 345.6 jit_solution(4363664120618757388)
XLA Ops:
  9.6 1.6 gather_fusion
  11.3 1.3 collective-permute-start.3
  12.6 5.0 %collective-permute-start.2 = (bf16[1,16,512]{2,1,0:T(8,128)(2,1)S(1)}, bf16[1,16,512]{2,1,0:T(8,128)(2,1)S(1)}, u32[]{:S(2)}, u32[]{:S(2)}) collective-permute-start(bf16[1,16,512]{2,1,0:T(8,128)(2,1)S(1)} %get-tuple-element.26), channel_id=1, source_target_pairs={{0,1},{1,2},{2,3},{3,4},{4,5},{5,6},{6,7},{7,8},{8,9},{9,10},{10,1... | collective-permute-start | bytes 49160 | tf_op jit(solution)/shard_map/ppermute | solution.py:12
  17.6 4.7 %collective-permute-start.1 = (bf16[1,16,512]{2,1,0:T(8,128)(2,1)S(1)}, bf16[1,16,512]{2,1,0:T(8,128)(2,1)S(1)}, u32[]{:S(2)}, u32[]{:S(2)}) collective-permute-start(bf16[1,16,512]{2,1,0:T(8,128)(2,1)S(1)} %get-tuple-element.27), channel_id=1, source_target_pairs={{16,0},{32,16},{48,32},{64,48},{80,64},{96,80},{112,96},{128,112},... | collective-permute-start | bytes 49160 | tf_op jit(solution)/shard_map/ppermute | solution.py:15
  22.3 1.9 collective-permute-start
  28.2 2.1 gather_fusion.2
  30.5 2.1 gather_fusion.1
  40.5 1.6 gather_fusion.3
  42.2 1.6 fusion.41
  45.3 1.5 fusion.39
  46.9 1.3 fusion.35
  48.2 1.8 fusion.20
  50.1 2.7 fusion.7
  53.7 2.3 fusion.46
  56.0 3.6 %scatter_custom_fusion = f32[128,512]{1,0:T(8,128)S(1)} fusion(s32[384]{0:T(512)} %copy-done.28, f32[384,1536]{1,0:T(8,128)} %fusion.46, f32[]{:T(128)} %constant.80.clone.1), kind=kCustom, calls=%fused_computation.20 | custom fusion | flops 196608 | bytes 1049088 | tf_op jit(solution)/shard_map/scatter-add | solution.py:101
  59.7 1.3 collective-permute-start.7
  61.0 4.0 %collective-permute-start.6 = (bf16[1,16,512]{2,1,0:T(8,128)(2,1)S(1)}, bf16[1,16,512]{2,1,0:T(8,128)(2,1)S(1)}, u32[]{:S(2)}, u32[]{:S(2)}) collective-permute-start(bf16[1,16,512]{2,1,0:T(8,128)(2,1)S(1)} %get-tuple-element.17), channel_id=1, source_target_pairs={{0,1},{1,2},{2,3},{3,4},{4,5},{5,6},{6,7},{7,8},{8,9},{9,10},{10,1... | collective-permute-start | bytes 49160 | tf_op jit(solution)/shard_map/ppermute | solution.py:12
  65.0 1.6 fusion.1
  66.6 2.3 fusion.9
  68.8 2.1 collective-permute-start.4
  71.0 2.2 collective-permute-start.5
  73.2 3.3 collective-permute-done.5
  78.3 253.7 %all-reduce.3.cloned.1.call-done = (f32[1536,512]{1,0:T(8,128)}, f32[512,512]{1,0:T(8,128)}, f32[1024,512]{1,0:T(8,128)}, f32[512,512]{1,0:T(8,128)}) async-done(((f32[1536,512]{1,0:T(8,128)}, f32[512,512]{1,0:T(8,128)}, f32[1024,512]{1,0:T(8,128)}, f32[512,512]{1,0:T(8,128)}), (f32[1536,512]{1,0:T(8,128)}, f32[512,512]{1,0:T(8,128)}, f32[1024,512]{1,0:T(8,128)}, ...) | async-done | bytes 7340048 | tf_op jit(solution)/shard_map/psum | solution.py:147
  332.0 3.6 %multiply_convert_fusion = bf16[1536,512]{1,0:T(8,128)(2,1)} fusion(f32[1536,512]{1,0:T(8,128)} %get-tuple-element.9), kind=kLoop, calls=%fused_computation.6 | loop fusion | flops 1572864 | bytes 4718592 | tf_op jit(solution)/shard_map/convert_element_type | solution.py:148
  (151 shorter events, 21.6 us)
Async XLA Ops:
  7.2 25.6 %copy-start = (bf16[1536,512]{1,0:T(8,128)(2,1)S(1)}, bf16[1536,512]{1,0:T(8,128)(2,1)}, u32[]{:S(2)}) copy-start(bf16[1536,512]{1,0:T(8,128)(2,1)} %param.18) | copy-start | bytes 4718596
  7.2 21.0 %copy-start.1 = (bf16[1,1,64,512]{3,2,1,0:T(8,128)(2,1)S(1)}, bf16[1,1,64,512]{3,2,1,0:T(8,128)(2,1)}, u32[]{:S(2)}) copy-start(bf16[1,1,64,512]{3,2,1,0:T(8,128)(2,1)} %param.11) | copy-start | bytes 196612
  7.2 324.8 %all-reduce.3.cloned.1.call-start = ((), (), s32[]{:S(2)}) async-start(), calls=%async_computation | async-start | bytes 14680064 | tf_op jit(solution)/shard_map/psum | solution.py:147
  11.3 19.2 %collective-permute-start.3 = (bf16[1,16,512]{2,1,0:T(8,128)(2,1)S(1)}, bf16[1,16,512]{2,1,0:T(8,128)(2,1)S(1)}, u32[]{:S(2)}, u32[]{:S(2)}) collective-permute-start(bf16[1,16,512]{2,1,0:T(8,128)(2,1)S(1)} %get-tuple-element.25), channel_id=1, source_target_pairs={{1,0},{2,1},{3,2},{4,3},{5,4},{6,5},{7,6},{8,7},{9,8},{10,9},{11,1... | collective-permute-start | bytes 49160 | tf_op jit(solution)/shard_map/ppermute | solution.py:15
  12.6 17.9 %collective-permute-start.2 = (bf16[1,16,512]{2,1,0:T(8,128)(2,1)S(1)}, bf16[1,16,512]{2,1,0:T(8,128)(2,1)S(1)}, u32[]{:S(2)}, u32[]{:S(2)}) collective-permute-start(bf16[1,16,512]{2,1,0:T(8,128)(2,1)S(1)} %get-tuple-element.26), channel_id=1, source_target_pairs={{0,1},{1,2},{2,3},{3,4},{4,5},{5,6},{6,7},{7,8},{8,9},{9,10},{10,1... | collective-permute-start | bytes 49160 | tf_op jit(solution)/shard_map/ppermute | solution.py:12
  17.6 12.9 %collective-permute-start.1 = (bf16[1,16,512]{2,1,0:T(8,128)(2,1)S(1)}, bf16[1,16,512]{2,1,0:T(8,128)(2,1)S(1)}, u32[]{:S(2)}, u32[]{:S(2)}) collective-permute-start(bf16[1,16,512]{2,1,0:T(8,128)(2,1)S(1)} %get-tuple-element.27), channel_id=1, source_target_pairs={{16,0},{32,16},{48,32},{64,48},{80,64},{96,80},{112,96},{128,112},... | collective-permute-start | bytes 49160 | tf_op jit(solution)/shard_map/ppermute | solution.py:15
  22.3 8.1 %collective-permute-start = (bf16[1,16,512]{2,1,0:T(8,128)(2,1)S(1)}, bf16[1,16,512]{2,1,0:T(8,128)(2,1)S(1)}, u32[]{:S(2)}, u32[]{:S(2)}) collective-permute-start(bf16[1,16,512]{2,1,0:T(8,128)(2,1)S(1)} %get-tuple-element.28), channel_id=1, source_target_pairs={{0,16},{16,32},{32,48},{48,64},{64,80},{80,96},{96,112},{112,128},... | collective-permute-start | bytes 49160 | tf_op jit(solution)/shard_map/ppermute | solution.py:12
  28.1 9.7 %copy-start.35 = (f32[64]{0:T(128)}, f32[64]{0:T(128)S(1)}, u32[]{:S(2)}) copy-start(f32[64]{0:T(128)S(1)} %broadcast_multiply_fusion.4) | copy-start | bytes 772
  45.2 4.8 %copy-start.18 = (bf16[384,512]{1,0:T(8,128)(2,1)}, bf16[384,512]{1,0:T(8,128)(2,1)S(1)}, u32[]{:S(2)}) copy-start(bf16[384,512]{1,0:T(8,128)(2,1)S(1)} %fusion) | copy-start | bytes 1179652
  45.3 2.9 copy-start.12
  45.3 2.9 copy-start.25
  46.8 3.2 copy-start.17
  46.9 3.2 copy-start.21
  46.9 3.2 copy-start.23
  53.7 11.2 %copy-start.9 = (f32[64,1024]{1,0:T(8,128)S(1)}, f32[64,1024]{1,0:T(8,128)}, u32[]{:S(2)}) copy-start(f32[64,1024]{1,0:T(8,128)} %copy-done.8) | copy-start | bytes 786436
  56.0 10.5 %copy-start.4 = (bf16[1,1,384,512]{3,2,1,0:T(8,128)(2,1)S(1)}, bf16[1,1,384,512]{3,2,1,0:T(8,128)(2,1)}, u32[]{:S(2)}) copy-start(bf16[1,1,384,512]{3,2,1,0:T(8,128)(2,1)} %param.17) | copy-start | bytes 1179652
  56.0 10.5 %copy-start.27 = (pred[384]{0:T(512)(128)(4,1)S(1)}, pred[384]{0:T(512)(128)(4,1)}, u32[]{:S(2)}) copy-start(pred[384]{0:T(512)(128)(4,1)} %copy-done.26) | copy-start | bytes 1156
  59.7 13.5 %collective-permute-start.7 = (bf16[1,16,512]{2,1,0:T(8,128)(2,1)S(1)}, bf16[1,16,512]{2,1,0:T(8,128)(2,1)S(1)}, u32[]{:S(2)}, u32[]{:S(2)}) collective-permute-start(bf16[1,16,512]{2,1,0:T(8,128)(2,1)S(1)} %get-tuple-element.16), channel_id=1, source_target_pairs={{1,0},{2,1},{3,2},{4,3},{5,4},{6,5},{7,6},{8,7},{9,8},{10,9},{11,1... | collective-permute-start | bytes 49160 | tf_op jit(solution)/shard_map/ppermute | solution.py:15
  61.0 15.6 %copy-start.34 = (s32[64]{0:T(128)S(1)}, s32[64]{0:T(128)}, u32[]{:S(2)}) copy-start(s32[64]{0:T(128)} %copy-done.33) | copy-start | bytes 772
  61.0 12.2 %collective-permute-start.6 = (bf16[1,16,512]{2,1,0:T(8,128)(2,1)S(1)}, bf16[1,16,512]{2,1,0:T(8,128)(2,1)S(1)}, u32[]{:S(2)}, u32[]{:S(2)}) collective-permute-start(bf16[1,16,512]{2,1,0:T(8,128)(2,1)S(1)} %get-tuple-element.17), channel_id=1, source_target_pairs={{0,1},{1,2},{2,3},{3,4},{4,5},{5,6},{6,7},{7,8},{8,9},{9,10},{10,1... | collective-permute-start | bytes 49160 | tf_op jit(solution)/shard_map/ppermute | solution.py:12
  68.8 4.4 %collective-permute-start.4 = (bf16[1,16,512]{2,1,0:T(8,128)(2,1)S(1)}, bf16[1,16,512]{2,1,0:T(8,128)(2,1)S(1)}, u32[]{:S(2)}, u32[]{:S(2)}) collective-permute-start(bf16[1,16,512]{2,1,0:T(8,128)(2,1)S(1)} %get-tuple-element.15), channel_id=1, source_target_pairs={{0,16},{16,32},{32,48},{48,64},{64,80},{80,96},{96,112},{112,128},... | collective-permute-start | bytes 49160 | tf_op jit(solution)/shard_map/ppermute | solution.py:12
  71.0 5.6 %collective-permute-start.5 = (bf16[1,16,512]{2,1,0:T(8,128)(2,1)S(1)}, bf16[1,16,512]{2,1,0:T(8,128)(2,1)S(1)}, u32[]{:S(2)}, u32[]{:S(2)}) collective-permute-start(bf16[1,16,512]{2,1,0:T(8,128)(2,1)S(1)} %get-tuple-element.18), channel_id=1, source_target_pairs={{16,0},{32,16},{48,32},{64,48},{80,64},{96,80},{112,96},{128,112},... | collective-permute-start | bytes 49160 | tf_op jit(solution)/shard_map/ppermute | solution.py:15
  332.0 3.6 %copy-start.7 = (f32[512,512]{1,0:T(8,128)S(1)}, f32[512,512]{1,0:T(8,128)}, u32[]{:S(2)}) copy-start(f32[512,512]{1,0:T(8,128)} %get-tuple-element.10) | copy-start | bytes 3145732
  332.0 4.5 %copy-start.6 = (f32[512,512]{1,0:T(8,128)S(1)}, f32[512,512]{1,0:T(8,128)}, u32[]{:S(2)}) copy-start(f32[512,512]{1,0:T(8,128)} %get-tuple-element.12) | copy-start | bytes 3145732
  (29 other events, 44.4 us)
Sparse Core Ops, SparseCore 0:
  52.9 279.0 all-reduce.2
where the time goes:
time: 347 us; the launch traced here: 346 us
  waiting for transfers between devices  257 us (74%)
  starting transfers between devices  22.5 us (6%)
  other arithmetic  22.2 us (6%)
  between operations  14.9 us (4%)
  matrix products  14.5 us (4%)
  local copies, waits for them, and re-layouts  14.3 us (4%)
    psum x1, waiting for transfers between devices, local(): lax.psum((weights[0], weights[1], weights[2], weights[3]), ('gx', 'gy'))  254 us
    ppermute x4, starting transfers between devices, with_halo(): lax.ppermute(lax.slice_in_dim(block, block.shape[dim] - width, None, axis...  13 us
    ppermute x4, starting transfers between devices, with_halo(): lax.ppermute(lax.slice_in_dim(block, 0, width, axis=dim), axis, backward)  9.47 us
    dot_general x4, matrix products, inner_rows(): lax.dot_general(left, right, (((0,), (0,)), ((), ())), preferred_element_...  7.33 us
  transfers between devices with their start and end apart: 9, of which 2 were waited for; matrix products, arithmetic and copies ran while one was open for 5% of the time, Pallas kernels for 0%

commit v1 on v0

v1 whole, which is shorter than its diff:
```python
import jax
import jax.numpy as jnp
from jax import lax
from jax.experimental import pallas as pl
from jax.experimental.pallas import tpu as pltpu
from jax.sharding import Mesh
from jax.sharding import PartitionSpec as P

BF = jnp.bfloat16
F32 = jnp.float32
GX = ("yh", "x", "c")
GY = ("yl", "z")
PLANE = ("yh", "x", "yl")
VMEM = pl.BlockSpec(memory_space=pltpu.VMEM)
ANY = pl.BlockSpec(memory_space=pl.ANY)


def dot(left, right):
    return jnp.dot(left, right, preferred_element_type=F32)


def dot_rows(left, right):
    return lax.dot_general(left, right, (((0,), (0,)), ((), ())), preferred_element_type=F32)


def dot_cols(left, right):
    return lax.dot_general(left, right, (((1,), (1,)), ((), ())), preferred_element_type=F32)


def hi_lo(values):
    high = values.astype(BF)
    low = (values - high.astype(F32)).astype(BF)
    return jnp.concatenate([high, low], axis=0)


def fold(values):
    half = values.shape[0] // 2
    return values[:half] + values[half:]


def layer_norm(values):
    mean = jnp.mean(values, axis=-1, keepdims=True)
    centred = values - mean
    scale = lax.rsqrt(jnp.mean(centred * centred, axis=-1, keepdims=True) + 1e-05)
    return centred * scale, scale


def norm_back(grad, normed, scale):
    first = jnp.mean(grad, axis=-1, keepdims=True)
    second = jnp.mean(grad * normed, axis=-1, keepdims=True)
    return scale * (grad - first - normed * second)


def silu_and_slope(values):
    sig = 1.0 / (1.0 + jnp.exp(-values))
    return values * sig, sig * (1.0 + values * (1.0 - sig))


def pick(row, count):
    rows = lax.broadcasted_iota(jnp.int32, (count, row.shape[-1]), 0)
    return jnp.where(rows == row, 1.0, 0.0)


def pack_kernel(nodes, lists, *packs):
    lat = nodes[0, 0]
    for side in range(4):
        chosen = pick(lists[0, 0, side : side + 1, :], lat.shape[0]).astype(BF)
        packs[side][...] = dot_rows(chosen, lat).astype(BF)


def layer_kernel(
    nodes,
    edges,
    halo0,
    halo1,
    halo2,
    halo3,
    senders,
    segments,
    cot_nodes,
    cot_edges,
    w_edge1,
    w_edge2,
    w_node1,
    w_node2,
    node_next,
    grad_edges,
    d_node,
    back0,
    back1,
    back2,
    back3,
    keep,
    send,
):
    core = lax.axis_index("c")
    node = nodes[0, 0]
    edge = edges[0, 0]
    width = node.shape[1]
    count = node.shape[0]
    half = keep.shape[0]

    def put(start, value):
        stop = start + value.shape[0]
        value = value.astype(BF)
        for side in range(2):
            low, high = max(start, side * half), min(stop, (side + 1) * half)
            if low >= high:
                continue
            part = value[low - start : high - start]

            @pl.when(core == side)
            def _():
                keep[low - side * half : high - side * half, :] = part

            @pl.when(core != side)
            def _():
                send[low - side * half : high - side * half, :] = part

    ext = jnp.concatenate([node, halo0[...], halo1[...], halo2[...], halo3[...]], axis=0)
    by_send = pick(senders[0], ext.shape[0])
    by_recv = pick(segments[0], count)
    from_ext = by_send.T.astype(BF)
    from_node = by_recv.T.astype(BF)
    to_ext = by_send.astype(BF)
    to_node = by_recv.astype(BF)

    wide = jnp.concatenate([from_ext, from_ext, from_node, from_node], axis=1)
    terms = jnp.concatenate(
        [
            hi_lo(dot(ext, w_edge1[width : 2 * width, :])),
            hi_lo(dot(node, w_edge1[2 * width :, :])),
        ],
        axis=0,
    )
    z_one = dot(edge, w_edge1[:width, :]) + dot(wide, terms)
    act, slope_one = silu_and_slope(z_one)
    a_one = act.astype(BF)
    n_two, s_two = layer_norm(dot(a_one, w_edge2[...]))
    e_new = (edge.astype(F32) + n_two).astype(BF)
    agg = dot(to_node, e_new).astype(BF)
    z_three = dot(node, w_node1[:width, :]) + dot(agg, w_node1[width:, :])
    act, slope_three = silu_and_slope(z_three)
    a_three = act.astype(BF)
    n_four, s_four = layer_norm(dot(a_three, w_node2[...]))
    node_next[0, 0] = (node.astype(F32) + n_four).astype(BF)

    g_node = cot_nodes[0, 0].astype(F32)
    dz_four = norm_back(g_node, n_four, s_four).astype(BF)
    dz_three = (dot_cols(dz_four, w_node2[...]) * slope_three).astype(BF)
    dy_node = dot_cols(dz_three, w_node1[:width, :])
    dy_agg = dot_cols(dz_three, w_node1[width:, :])
    put(4 * width, dot_rows(node, dz_three))
    put(5 * width, dot_rows(agg, dz_three))
    put(6 * width, dot_rows(a_three, dz_four))

    twice = jnp.concatenate([from_node, from_node], axis=1)
    de_new = cot_edges[0, 0].astype(F32) + dot(twice, hi_lo(dy_agg))
    dz_two = norm_back(de_new, n_two, s_two).astype(BF)
    dz_one = (dot_cols(dz_two, w_edge2[...]) * slope_one).astype(BF)
    put(3 * width, dot_rows(a_one, dz_two))
    put(0, dot_rows(edge, dz_one))
    grad_edges[0, 0] = (de_new + dot_cols(dz_one, w_edge1[:width, :])).astype(BF)

    sum_send = hi_lo(dot(to_ext, dz_one))
    sum_recv = hi_lo(dot(to_node, dz_one))
    put(width, dot_rows(jnp.concatenate([ext, ext], axis=0), sum_send))
    put(2 * width, dot_rows(jnp.concatenate([node, node], axis=0), sum_recv))
    d_ext = fold(dot_cols(sum_send, w_edge1[width : 2 * width, :]))
    d_recv = fold(dot_cols(sum_recv, w_edge1[2 * width :, :]))
    d_node[...] = g_node + dy_node + d_recv + d_ext[:count]
    rows = back0.shape[0]
    for side, back in enumerate((back0, back1, back2, back3)):
        back[...] = d_ext[count + side * rows : count + (side + 1) * rows].astype(BF)


def return_kernel(d_node, lists, ret0, ret1, ret2, ret3, out):
    total = d_node[...]
    for side, ret in enumerate((ret0, ret1, ret2, ret3)):
        chosen = pick(lists[0, 0, side : side + 1, :], total.shape[0]).astype(BF)
        total = total + dot(chosen, ret[...])
    out[0, 0] = total.astype(BF)


def pair_sum_kernel(mine, other, out):
    out[...] = (mine[...].astype(F32) + other[...].astype(F32)).astype(BF)


def plane_sum_kernel(parts, out):
    rows, lanes = out.shape[1], out.shape[2]
    for block in range(out.shape[0]):
        r, c = block % 2 * rows, block // 2 * lanes
        total = parts[0, r : r + rows, c : c + lanes].astype(F32)
        for part in range(1, parts.shape[0]):
            total = total + parts[part, r : r + rows, c : c + lanes].astype(F32)
        out[block] = total


def line_sum_kernel(factor, parts, out):
    total = parts[0]
    for part in range(1, parts.shape[0]):
        total = total + parts[part]
    total = (total * factor).astype(BF)
    for part in range(out.shape[0]):
        out[part] = total


def spread_kernel(blocks, out):
    rows, lanes = blocks.shape[1], blocks.shape[2]
    tops = jnp.concatenate([blocks[2 * i] for i in range(4)], axis=1)
    ends = jnp.concatenate([blocks[2 * i + 1] for i in range(4)], axis=1)
    whole = jnp.concatenate([tops, ends], axis=0)
    for part in range(out.shape[0]):
        out[part] = whole


def finish_kernel(mine, other, *refs):
    outs, sem = refs[:4], refs[4]
    core = lax.axis_index("c")
    half = mine.shape[0]

    def copies(low_half, high_half):
        made = []
        start = 0
        for out in outs:
            stop = start + out.shape[0]
            for side, source in enumerate((low_half, high_half)):
                low, high = max(start, side * half), min(stop, (side + 1) * half)
                if low < high:
                    made.append(
                        pltpu.make_async_copy(
                            source.at[pl.ds(low - side * half, high - low)],
                            out.at[pl.ds(low - start, high - low)],
                            sem.at[len(made)],
                        )
                    )
            start = stop
        for copy in made:
            copy.start()
        for copy in made:
            copy.wait()

    @pl.when(core == 0)
    def _():
        copies(mine, other)

    @pl.when(core != 0)
    def _():
        copies(other, mine)


def call(kernel, outs, n_in, limit=32, **kwargs):
    return pl.pallas_call(
        kernel,
        out_shape=outs,
        in_specs=[VMEM] * n_in,
        out_specs=jax.tree.map(lambda _: VMEM, outs),
        compiler_params=pltpu.CompilerParams(vmem_limit_bytes=limit << 20),
        **kwargs,
    )


def shape(dims, kind=BF):
    return jax.ShapeDtypeStruct(dims, kind)


def cycle(count, step):
    return [(i, (i + step) % count) for i in range(count)]


def local(
    nodes,
    edges,
    senders,
    segments,
    send_lists,
    cot_nodes,
    cot_edges,
    w_edge1,
    w_edge2,
    w_node1,
    w_node2,
):
    width = nodes.shape[3]
    rows = send_lists.shape[3]
    nx, ny = lax.axis_size(GX), lax.axis_size(GY)
    block = [shape((rows, width))] * 4
    packs = call(pack_kernel, block, 2)(nodes, send_lists)
    halo0 = lax.ppermute(packs[1], GX, cycle(nx, 1))
    halo1 = lax.ppermute(packs[0], GX, cycle(nx, -1))
    halo2 = lax.ppermute(packs[3], GY, cycle(ny, 1))
    halo3 = lax.ppermute(packs[2], GY, cycle(ny, -1))
    total = w_edge1.shape[0] + w_edge2.shape[0] + w_node1.shape[0] + w_node2.shape[0]
    half = shape((total // 2, width))
    node_next, grad_edges, d_node, back0, back1, back2, back3, keep, send = call(
        layer_kernel,
        [shape(nodes.shape), shape(edges.shape), shape((nodes.shape[2], width), F32)]
        + block
        + [half, half],
        14,
        limit=48,
    )(
        nodes,
        edges,
        halo0,
        halo1,
        halo2,
        halo3,
        senders,
        segments,
        cot_nodes,
        cot_edges,
        w_edge1,
        w_edge2,
        w_node1,
        w_node2,
    )

    got = lax.ppermute(send, "c", cycle(2, 1))
    pair = call(pair_sum_kernel, half, 2)(keep, got)
    ret0 = lax.ppermute(back1, GX, cycle(nx, 1))
    ret1 = lax.ppermute(back0, GX, cycle(nx, -1))
    ret2 = lax.ppermute(back3, GY, cycle(ny, 1))
    ret3 = lax.ppermute(back2, GY, cycle(ny, -1))
    grad_nodes = call(return_kernel, shape(nodes.shape), 6)(
        d_node, send_lists, ret0, ret1, ret2, ret3
    )

    plane, line = lax.axis_size(PLANE), lax.axis_size("z")
    strip = total // 2 // plane
    cut = (line, strip // 2, width * 2 // line)
    pieces = lax.all_to_all(pair, PLANE, 0, 0, tiled=True).reshape(plane, strip, width)
    pieces = call(plane_sum_kernel, shape(cut, F32), 1)(pieces)
    pieces = lax.all_to_all(pieces, "z", 0, 0, tiled=True)
    factor = float(edges.shape[2] * nx * ny) ** -0.5
    pieces = call(lambda a, b: line_sum_kernel(factor, a, b), shape(cut), 1)(pieces)
    pieces = lax.all_to_all(pieces, "z", 0, 0, tiled=True)
    pieces = call(spread_kernel, shape((plane, strip, width)), 1)(pieces)
    mine = lax.all_to_all(pieces, PLANE, 0, 0, tiled=True).reshape(total // 2, width)
    other = lax.ppermute(mine, "c", cycle(2, 1))
    grads = pl.pallas_call(
        finish_kernel,
        out_shape=[shape(w.shape) for w in (w_edge1, w_edge2, w_node1, w_node2)],
        in_specs=[ANY] * 2,
        out_specs=[ANY] * 4,
        scratch_shapes=[pltpu.SemaphoreType.DMA((5,))],
    )(mine, other)
    return (node_next, grad_nodes, grad_edges, *grads)


def solution(mesh):
    fine = Mesh(mesh.devices.reshape(2, 4, 2, 2, 8), ("yh", "x", "c", "yl", "z"))
    tile = P(GX, GY)
    return jax.shard_map(
        local,
        mesh=fine,
        in_specs=(tile,) * 7 + (P(),) * 4,
        out_specs=(tile,) * 3 + (P(),) * 4,
        check_vma=False,
    )
```

time: 347 us -> 247 us (0.71)
  waiting for transfers between devices: 257 us -> 6.17 us
  Pallas kernels: 0 us -> 123 us
  blocking collectives: 0 us -> 76.7 us
  other arithmetic: 22.2 us -> 0 us
  matrix products: 14.5 us -> 0 us
  between operations: 14.9 us -> 0.7 us
    psum x1 -> x0, waiting for transfers between devices: 254 us -> none  [local(): lax.psum((weights[0], weights[1], weights[2], weights[3]), ('gx', 'gy'))]
    pallas_call x0 -> x8, Pallas kernels: none -> 123 us  [the longest x1 112 us: local(): pl.pallas_call(finish_kernel, out_shape=[shape(w.shape) for w in (w_edge1...]
    all_to_all x0 -> x4, blocking collectives: none -> 76.7 us  [the longest x1 28.3 us: local(): lax.all_to_all(pair, PLANE, 0, 0, tiled=True).reshape(plane, strip, width)]
    dot_general x14 -> x0, matrix products: 14.5 us -> none  [the longest x4 7.33 us: inner_rows(): lax.dot_general(left, right, (((0,), (0,)), ((), ())), preferred_element_...]
    convert_element_type x5 -> x0, other arithmetic: 7.65 us -> none  [the longest x4 6.7 us: local(): grads = tuple(((total * factor).astype(jnp.bfloat16) for total in sums))]
    unnamed x92 -> x30, local copies, waits for them, and re-layouts: 5.35 us -> 12.8 us
    gather x4 -> x0, local copies, waits for them, and re-layouts: 7.32 us -> none  [the longest x1 2.06 us: local_pass(): recv = jnp.take(node_lat, segments, axis=0)]
    scatter-add x2 -> x0, other arithmetic: 4.63 us -> none  [the longest x1 3.58 us: local_pass(): jax.ops.segment_sum(d_xedge[:, width:2 * width], senders, num_segments=ex...]
  transfers between devices with their start and end apart: 9 -> 10, of which waited for: 2 -> 3; matrix products, arithmetic and copies ran while one was open for 5% -> 0% of each run, Pallas kernels for 0% -> 0%
where the time goes in v1:
time: 247 us; the launch traced here: 243 us
  Pallas kernels  123 us (50%)
  blocking collectives  76.7 us (31%)
  starting transfers between devices  24.1 us (10%)
  local copies, waits for them, and re-layouts  12.8 us (5%)
  waiting for transfers between devices  6.17 us (2%)
    pallas_call x1, Pallas kernels, local(): pl.pallas_call(finish_kernel, out_shape=[shape(w.shape) for w in (w_edge1...  112 us
    all_to_all x1, blocking collectives, local(): lax.all_to_all(pair, PLANE, 0, 0, tiled=True).reshape(plane, strip, width)  28.3 us
    all_to_all x2, blocking collectives, local(): pieces = lax.all_to_all(pieces, 'z', 0, 0, tiled=True)  24.5 us
    all_to_all x1, blocking collectives, local(): lax.all_to_all(pieces, PLANE, 0, 0, tiled=True).reshape(total // 2, width)  24 us
    unnamed x30, local copies, waits for them, and re-layouts  12.8 us
    pallas_call x1, Pallas kernels, local(): call(layer_kernel, [shape(nodes.shape), shape(edges.shape), shape((nodes....  8.71 us
    ppermute x1, starting transfers between devices, local(): other = lax.ppermute(mine, 'c', cycle(2, 1))  5.63 us
    ppermute x1, starting transfers between devices, local(): got = lax.ppermute(send, 'c', cycle(2, 1))  5.12 us
  transfers between devices with their start and end apart: 10, of which 3 were waited for; matrix products, arithmetic and copies ran while one was open for 0% of the time, Pallas kernels for 0%

profile of v1, /device:TPU:1, one launch (start us, length us, event | category | flops | bytes accessed | tf_op | source)
XLA Modules:
  0.0 243.4 jit_solution(9962228042443303266)
XLA Ops:
  2.3 2.7 %collective-permute-start = (bf16[16,512]{1,0:T(8,128)(2,1)S(1)}, bf16[16,512]{1,0:T(8,128)(2,1)S(1)}, u32[]{:S(2)}, u32[]{:S(2)}) collective-permute-start(bf16[16,512]{1,0:T(8,128)(2,1)S(1)} %get-tuple-element.24), channel_id=1, source_target_pairs={{0,16},{16,32},{32,48},{48,64},{64,80},{80,96},{96,112},{112,128},... | collective-permute-start | bytes 49160 | tf_op jit(solution)/shard_map/ppermute | solution.py:289
  5.8 0.9 collective-permute-start.2
  6.7 5.0 %collective-permute-start.3 = (bf16[16,512]{1,0:T(8,128)(2,1)S(1)}, bf16[16,512]{1,0:T(8,128)(2,1)S(1)}, u32[]{:S(2)}, u32[]{:S(2)}) collective-permute-start(bf16[16,512]{1,0:T(8,128)(2,1)S(1)} %get-tuple-element.27), channel_id=1, source_target_pairs={{0,15},{1,0},{2,1},{3,2},{4,3},{5,4},{6,5},{7,6},{8,7},{9,8},{10,9... | collective-permute-start | bytes 49160 | tf_op jit(solution)/shard_map/ppermute | solution.py:292
  11.6 1.1 collective-permute-done.2.halo2
  12.7 1.4 copy-done.1
  14.2 1.2 copy-done.2
  15.4 1.0 copy-done.3
  16.4 1.0 copy-done.4
  17.5 1.0 copy-done.5
  18.5 1.0 copy-done.6
  19.5 0.8 copy-done.8
  20.3 0.8 copy-done.9
  22.5 8.7 %shard_map.163 = (bf16[1,1,64,512]{3,2,1,0:T(8,128)(2,1)}, bf16[1,1,384,512]{3,2,1,0:T(8,128)(2,1)}, f32[64,512]{1,0:T(8,128)S(1)}, bf16[16,512]{1,0:T(8,128)(2,...) custom-call(bf16[1,1,64,512]{3,2,1,0:T(8,128)(2,1)S(1)} %copy-done.8, ...), custom_call_target="tpu_custom_call" | custom-call | tf_op jit(solution)/shard_map/pallas_call | solution.py:295
  31.2 5.1 %collective-permute-start.8 = (bf16[1792,512]{1,0:T(8,128)(2,1)}, bf16[1792,512]{1,0:T(8,128)(2,1)S(1)}, u32[]{:S(2)}, u32[]{:S(2)}) collective-permute-start(bf16[1792,512]{1,0:T(8,128)(2,1)} %get-tuple-element.36), channel_id=1, source_target_pairs={{0,16},{16,0},{1,17},{17,1},{2,18},{18,2},{3,19},{19,3},{4,20},{20... | collective-permute-start | bytes 5505032 | tf_op jit(solution)/shard_map/ppermute | solution.py:319
  36.3 3.6 %collective-permute-done.8.other = bf16[1792,512]{1,0:T(8,128)(2,1)S(1)} collective-permute-done((bf16[1792,512]{1,0:T(8,128)(2,1)}, bf16[1792,512]{1,0:T(8,128)(2,1)S(1)}, u32[]{:S(2)}, u32[]{:S(2)}) %collective-permute-start.8) | collective-permute-done | bytes 1835040 | tf_op jit(solution)/shard_map/ppermute | solution.py:319
  40.0 1.5 copy-done
  41.9 28.3 %all_to_all.24.parts = bf16[16,112,512]{2,1,0:T(8,128)(2,1)S(1)} all-to-all(bf16[16,112,512]{2,1,0:T(8,128)(2,1)S(1)} %bitcast.2), channel_id=1, replica_groups=mesh['yh'=2,'x'=4,'c'=2,'yl'=2,'z'=8] {'yh','x','yl'}, dimensions={0} | all-to-all | bytes 3670016 | tf_op jit(solution)/shard_map/all_to_all | solution.py:332
  70.4 14.3 %all_to_all.25.a = f32[8,56,128]{2,1,0:T(8,128)S(1)} all-to-all(f32[8,56,128]{2,1,0:T(8,128)S(1)} %shard_map.166), channel_id=1, replica_groups=mesh['yh'=2,'x'=4,'c'=2,'yl'=2,'z'=8] {'z'}, dimensions={0} | all-to-all | bytes 458752 | tf_op jit(solution)/shard_map/all_to_all | solution.py:334
  84.7 10.2 %all_to_all.26.blocks = bf16[8,56,128]{2,1,0:T(8,128)(2,1)S(1)} all-to-all(bf16[8,56,128]{2,1,0:T(8,128)(2,1)S(1)} %shard_map.167), channel_id=1, replica_groups=mesh['yh'=2,'x'=4,'c'=2,'yl'=2,'z'=8] {'z'}, dimensions={0} | all-to-all | bytes 229376 | tf_op jit(solution)/shard_map/all_to_all | solution.py:337
  95.1 24.0 %all_to_all.27 = bf16[16,112,512]{2,1,0:T(8,128)(2,1)S(1)} all-to-all(bf16[16,112,512]{2,1,0:T(8,128)(2,1)S(1)} %shard_map.168), channel_id=1, replica_groups=mesh['yh'=2,'x'=4,'c'=2,'yl'=2,'z'=8] {'yh','x','yl'}, dimensions={0} | all-to-all | bytes 3670016 | tf_op jit(solution)/shard_map/all_to_all | solution.py:339
  119.1 5.6 %collective-permute-start.9 = (bf16[1792,512]{1,0:T(8,128)(2,1)S(1)}, bf16[1792,512]{1,0:T(8,128)(2,1)}, u32[]{:S(2)}, u32[]{:S(2)}) collective-permute-start(bf16[1792,512]{1,0:T(8,128)(2,1)S(1)} %bitcast.3), channel_id=1, source_target_pairs={{0,16},{16,0},{1,17},{17,1},{2,18},{18,2},{3,19},{19,3},{4,20},{20... | collective-permute-start | bytes 5505032 | tf_op jit(solution)/shard_map/ppermute | solution.py:340
  125.4 3.4 %collective-permute-start.7 = (bf16[16,512]{1,0:T(8,128)(2,1)S(1)}, bf16[16,512]{1,0:T(8,128)(2,1)S(1)}, u32[]{:S(2)}, u32[]{:S(2)}) collective-permute-start(bf16[16,512]{1,0:T(8,128)(2,1)S(1)} %get-tuple-element.33), channel_id=1, source_target_pairs={{0,15},{1,0},{2,1},{3,2},{4,3},{5,4},{6,5},{7,6},{8,7},{9,8},{10,9... | collective-permute-start | bytes 49160 | tf_op jit(solution)/shard_map/ppermute | solution.py:324
  128.8 1.4 collective-permute-done.6.ret2
  131.0 112.3 %shard_map.169 = (bf16[1536,512]{1,0:T(8,128)(2,1)}, bf16[512,512]{1,0:T(8,128)(2,1)}, bf16[1024,512]{1,0:T(8,128)(2,1)}, bf16[512,512]{1,0:T(8,128)(2,1)}) custom-call(bf16[1792,512]{1,0:T(8,128)(2,1)} %bitcast.4, bf16[1792,512]{1,0:T(8,128)(2,1)} %collective-permute-done.9.other), custom_call_target="tpu_custom_call" | custom-call | tf_op jit(solution)/shard_map/pallas_call | solution.py:341
  (38 shorter events, 6.2 us)
Async XLA Ops:
  0.6 0.8 copy-start.7
  1.5 0.7 copy-start.10
  2.3 9.3 %collective-permute-start = (bf16[16,512]{1,0:T(8,128)(2,1)S(1)}, bf16[16,512]{1,0:T(8,128)(2,1)S(1)}, u32[]{:S(2)}, u32[]{:S(2)}) collective-permute-start(bf16[16,512]{1,0:T(8,128)(2,1)S(1)} %get-tuple-element.24), channel_id=1, source_target_pairs={{0,16},{16,32},{32,48},{48,64},{64,80},{80,96},{96,112},{112,128},... | collective-permute-start | bytes 49160 | tf_op jit(solution)/shard_map/ppermute | solution.py:289
  5.0 6.6 %collective-permute-start.1 = (bf16[16,512]{1,0:T(8,128)(2,1)S(1)}, bf16[16,512]{1,0:T(8,128)(2,1)S(1)}, u32[]{:S(2)}, u32[]{:S(2)}) collective-permute-start(bf16[16,512]{1,0:T(8,128)(2,1)S(1)} %get-tuple-element.25), channel_id=1, source_target_pairs={{0,240},{16,0},{32,16},{48,32},{64,48},{80,64},{96,80},{112,96},{1... | collective-permute-start | bytes 49160 | tf_op jit(solution)/shard_map/ppermute | solution.py:290
  5.8 7.0 %collective-permute-start.2 = (bf16[16,512]{1,0:T(8,128)(2,1)S(1)}, bf16[16,512]{1,0:T(8,128)(2,1)S(1)}, u32[]{:S(2)}, u32[]{:S(2)}) collective-permute-start(bf16[16,512]{1,0:T(8,128)(2,1)S(1)} %get-tuple-element.26), channel_id=1, source_target_pairs={{0,1},{1,2},{2,3},{3,4},{4,5},{5,6},{6,7},{7,8},{8,9},{9,10},{10,1... | collective-permute-start | bytes 49160 | tf_op jit(solution)/shard_map/ppermute | solution.py:291
  6.7 6.1 %collective-permute-start.3 = (bf16[16,512]{1,0:T(8,128)(2,1)S(1)}, bf16[16,512]{1,0:T(8,128)(2,1)S(1)}, u32[]{:S(2)}, u32[]{:S(2)}) collective-permute-start(bf16[16,512]{1,0:T(8,128)(2,1)S(1)} %get-tuple-element.27), channel_id=1, source_target_pairs={{0,15},{1,0},{2,1},{3,2},{4,3},{5,4},{6,5},{7,6},{8,7},{9,8},{10,9... | collective-permute-start | bytes 49160 | tf_op jit(solution)/shard_map/ppermute | solution.py:292
  12.7 1.4 copy-start.1
  14.2 1.2 copy-start.2
  15.4 1.0 copy-start.3
  16.4 1.0 copy-start.4
  17.5 1.0 copy-start.5
  18.5 1.0 copy-start.6
  19.5 0.8 copy-start.8
  20.3 0.8 copy-start.9
  21.8 0.7 copy-start.13
  31.2 8.7 %collective-permute-start.8 = (bf16[1792,512]{1,0:T(8,128)(2,1)}, bf16[1792,512]{1,0:T(8,128)(2,1)S(1)}, u32[]{:S(2)}, u32[]{:S(2)}) collective-permute-start(bf16[1792,512]{1,0:T(8,128)(2,1)} %get-tuple-element.36), channel_id=1, source_target_pairs={{0,16},{16,0},{1,17},{17,1},{2,18},{18,2},{3,19},{19,3},{4,20},{20... | collective-permute-start | bytes 5505032 | tf_op jit(solution)/shard_map/ppermute | solution.py:319
  40.0 1.5 copy-start
  95.1 35.1 %copy-start.11 = (s32[1,1,4,16]{3,2,1,0:T(4,128)S(1)}, s32[1,1,4,16]{3,2,1,0:T(4,128)}, u32[]{:S(2)}) copy-start(s32[1,1,4,16]{3,2,1,0:T(4,128)} %lists.3) | copy-start | bytes 772
  119.1 12.0 %copy-start.14 = (bf16[16,112,512]{2,1,0:T(8,128)(2,1)}, bf16[16,112,512]{2,1,0:T(8,128)(2,1)S(1)}, u32[]{:S(2)}) copy-start(bf16[16,112,512]{2,1,0:T(8,128)(2,1)S(1)} %all_to_all.27) | copy-start | bytes 5505028
  119.1 12.0 %collective-permute-start.9 = (bf16[1792,512]{1,0:T(8,128)(2,1)S(1)}, bf16[1792,512]{1,0:T(8,128)(2,1)}, u32[]{:S(2)}, u32[]{:S(2)}) collective-permute-start(bf16[1792,512]{1,0:T(8,128)(2,1)S(1)} %bitcast.3), channel_id=1, source_target_pairs={{0,16},{16,0},{1,17},{17,1},{2,18},{18,2},{3,19},{19,3},{4,20},{20... | collective-permute-start | bytes 5505032 | tf_op jit(solution)/shard_map/ppermute | solution.py:340
  124.7 4.1 %collective-permute-start.4 = (bf16[16,512]{1,0:T(8,128)(2,1)S(1)}, bf16[16,512]{1,0:T(8,128)(2,1)S(1)}, u32[]{:S(2)}, u32[]{:S(2)}) collective-permute-start(bf16[16,512]{1,0:T(8,128)(2,1)S(1)} %get-tuple-element.30), channel_id=1, source_target_pairs={{0,16},{16,32},{32,48},{48,64},{64,80},{80,96},{96,112},{112,128},... | collective-permute-start | bytes 49160 | tf_op jit(solution)/shard_map/ppermute | solution.py:321
  124.7 4.1 %collective-permute-start.5 = (bf16[16,512]{1,0:T(8,128)(2,1)S(1)}, bf16[16,512]{1,0:T(8,128)(2,1)S(1)}, u32[]{:S(2)}, u32[]{:S(2)}) collective-permute-start(bf16[16,512]{1,0:T(8,128)(2,1)S(1)} %get-tuple-element.31), channel_id=1, source_target_pairs={{0,240},{16,0},{32,16},{48,32},{64,48},{80,64},{96,80},{112,96},{1... | collective-permute-start | bytes 49160 | tf_op jit(solution)/shard_map/ppermute | solution.py:322
  125.2 5.0 %collective-permute-start.6 = (bf16[16,512]{1,0:T(8,128)(2,1)S(1)}, bf16[16,512]{1,0:T(8,128)(2,1)S(1)}, u32[]{:S(2)}, u32[]{:S(2)}) collective-permute-start(bf16[16,512]{1,0:T(8,128)(2,1)S(1)} %get-tuple-element.32), channel_id=1, source_target_pairs={{0,1},{1,2},{2,3},{3,4},{4,5},{5,6},{6,7},{7,8},{8,9},{9,10},{10,1... | collective-permute-start | bytes 49160 | tf_op jit(solution)/shard_map/ppermute | solution.py:323
  125.4 4.8 %collective-permute-start.7 = (bf16[16,512]{1,0:T(8,128)(2,1)S(1)}, bf16[16,512]{1,0:T(8,128)(2,1)S(1)}, u32[]{:S(2)}, u32[]{:S(2)}) collective-permute-start(bf16[16,512]{1,0:T(8,128)(2,1)S(1)} %get-tuple-element.33), channel_id=1, source_target_pairs={{0,15},{1,0},{2,1},{3,2},{4,3},{5,4},{6,5},{7,6},{8,7},{9,8},{10,9... | collective-permute-start | bytes 49160 | tf_op jit(solution)/shard_map/ppermute | solution.py:324
  (1 other events, 0.7 us)

commit v2 on v1

v2 whole, which is shorter than its diff:
```python
import functools

import jax
import jax.numpy as jnp
from jax import lax
from jax.experimental import pallas as pl
from jax.experimental.pallas import tpu as pltpu
from jax.sharding import Mesh
from jax.sharding import PartitionSpec as P

BF = jnp.bfloat16
F32 = jnp.float32
GX = ("yh", "x", "c")
GY = ("yl", "z")
PLANE = ("yh", "x", "yl")
VMEM = pl.BlockSpec(memory_space=pltpu.VMEM)
ANY = pl.BlockSpec(memory_space=pl.ANY)


def dot(left, right):
    return jnp.dot(left, right, preferred_element_type=F32)


def dot_rows(left, right):
    return lax.dot_general(left, right, (((0,), (0,)), ((), ())), preferred_element_type=F32)


def dot_cols(left, right):
    return lax.dot_general(left, right, (((1,), (1,)), ((), ())), preferred_element_type=F32)


def hi_lo(values):
    high = values.astype(BF)
    low = (values - high.astype(F32)).astype(BF)
    return jnp.concatenate([high, low], axis=0)


def fold(values):
    half = values.shape[0] // 2
    return values[:half] + values[half:]


def layer_norm(values):
    mean = jnp.mean(values, axis=-1, keepdims=True)
    centred = values - mean
    scale = lax.rsqrt(jnp.mean(centred * centred, axis=-1, keepdims=True) + 1e-05)
    return centred * scale, scale


def norm_back(grad, normed, scale):
    first = jnp.mean(grad, axis=-1, keepdims=True)
    second = jnp.mean(grad * normed, axis=-1, keepdims=True)
    return scale * (grad - first - normed * second)


def silu_and_slope(values):
    sig = 1.0 / (1.0 + jnp.exp(-values))
    return values * sig, sig * (1.0 + values * (1.0 - sig))


def pick(row, count):
    rows = lax.broadcasted_iota(jnp.int32, (count, row.shape[-1]), 0)
    return jnp.where(rows == row, 1.0, 0.0)


def fetch(sources, targets, sems):
    copies = [
        pltpu.make_async_copy(source, target, sems.at[i])
        for i, (source, target) in enumerate(zip(sources, targets, strict=True))
    ]
    for copy in copies:
        copy.start()

    def ready(i):
        copies[i].wait()
        return targets[i]

    return ready


def parities():
    return lax.axis_index("c"), lax.rem(lax.axis_index("z"), 2)


def side_of(step, row_odd, col_odd):
    return (1 - row_odd, row_odd, 3 - col_odd, 2 + col_odd)[step]


def pack_kernel(nodes_hbm, lists_hbm, *refs):
    packs, (nodes, lists, sems) = refs[:4], refs[4:]
    ready = fetch((nodes_hbm.at[0, 0], lists_hbm.at[0, 0]), (nodes, lists), sems)
    odd = parities()
    ready(1)
    lat = ready(0)[...]
    for step in range(4):
        row = lists[pl.ds(side_of(step, *odd), 1), :]
        packs[step][...] = dot_rows(pick(row, lat.shape[0]).astype(BF), lat).astype(BF)


def layer_kernel(
    nodes_hbm,
    edges_hbm,
    halo0,
    halo1,
    halo2,
    halo3,
    senders_hbm,
    segments_hbm,
    cot_nodes_hbm,
    cot_edges_hbm,
    w_edge1_hbm,
    w_edge2_hbm,
    w_node1_hbm,
    w_node2_hbm,
    node_next,
    grad_edges,
    d_node,
    back0,
    back1,
    back2,
    back3,
    keep,
    send,
    nodes,
    edges,
    senders,
    segments,
    cot_nodes,
    cot_edges,
    w_edge1,
    w_edge2,
    w_node1,
    w_node2,
    ext_twice,
    node_twice,
    a_one,
    agg,
    a_three,
    d_ext,
    sems,
):
    ready = fetch(
        (
            senders_hbm.at[0],
            segments_hbm.at[0],
            nodes_hbm.at[0, 0],
            edges_hbm.at[0, 0],
            w_edge1_hbm,
            w_edge2_hbm,
            w_node1_hbm,
            w_node2_hbm,
            cot_nodes_hbm.at[0, 0],
            cot_edges_hbm.at[0, 0],
        ),
        (
            senders,
            segments,
            nodes,
            edges,
            w_edge1,
            w_edge2,
            w_node1,
            w_node2,
            cot_nodes,
            cot_edges,
        ),
        sems,
    )
    odd = parities()
    width = nodes.shape[1]
    count = nodes.shape[0]
    rows = halo0.shape[0]
    part = width // 2

    def put(block, left, right):
        for target, side in ((send, 1 - odd[0]), (keep, odd[0])):
            columns = pl.ds(pl.multiple_of(side * part, part), part)
            target[block * part : (block + 1) * part, :] = dot_rows(
                left[:, columns], right
            ).astype(BF)

    reach = ext_twice.shape[0] // 2
    by_send = pick(ready(0)[...], reach)
    by_recv = pick(ready(1)[...], count)
    from_ext = by_send.T.astype(BF)
    from_node = by_recv.T.astype(BF)
    to_ext = by_send.astype(BF)
    to_node = by_recv.astype(BF)
    wide = jnp.concatenate([from_ext, from_ext, from_node, from_node], axis=1)

    node = ready(2)[...]
    for start in (0, reach):
        ext_twice[start : start + count, :] = node
        for step, halo in enumerate((halo0, halo1, halo2, halo3)):
            place = start + count + side_of(step, *odd) * rows
            ext_twice[pl.ds(pl.multiple_of(place, rows), rows), :] = halo[...]
    for start in (0, count):
        node_twice[start : start + count, :] = node
    ext = ext_twice[:reach, :]
    edge = ready(3)[...]
    ready(4)

    terms = jnp.concatenate(
        [
            hi_lo(dot(ext, w_edge1[width : 2 * width, :])),
            hi_lo(dot(node, w_edge1[2 * width :, :])),
        ],
        axis=0,
    )
    z_one = dot(edge, w_edge1[:width, :]) + dot(wide, terms)
    act, slope_one = silu_and_slope(z_one)
    a_one[...] = act.astype(BF)
    ready(5)
    n_two, s_two = layer_norm(dot(a_one[...], w_edge2[...]))
    e_new = (edge.astype(F32) + n_two).astype(BF)
    agg[...] = dot(to_node, e_new).astype(BF)
    ready(6)
    z_three = dot(node, w_node1[:width, :]) + dot(agg[...], w_node1[width:, :])
    act, slope_three = silu_and_slope(z_three)
    a_three[...] = act.astype(BF)
    ready(7)
    n_four, s_four = layer_norm(dot(a_three[...], w_node2[...]))
    node_next[0, 0] = (node.astype(F32) + n_four).astype(BF)

    g_node = ready(8)[...].astype(F32)
    dz_four = norm_back(g_node, n_four, s_four).astype(BF)
    dz_three = (dot_cols(dz_four, w_node2[...]) * slope_three).astype(BF)
    dy_node = dot_cols(dz_three, w_node1[:width, :])
    dy_agg = dot_cols(dz_three, w_node1[width:, :])

    twice = jnp.concatenate([from_node, from_node], axis=1)
    de_new = ready(9)[...].astype(F32) + dot(twice, hi_lo(dy_agg))
    dz_two = norm_back(de_new, n_two, s_two).astype(BF)
    dz_one = (dot_cols(dz_two, w_edge2[...]) * slope_one).astype(BF)
    sum_send = hi_lo(dot(to_ext, dz_one))
    sum_recv = hi_lo(dot(to_node, dz_one))
    put(0, edges, dz_one)
    put(1, ext_twice, sum_send)
    put(2, node_twice, sum_recv)
    put(3, a_one, dz_two)
    put(4, nodes, dz_three)
    put(5, agg, dz_three)
    put(6, a_three, dz_four)
    grad_edges[0, 0] = (de_new + dot_cols(dz_one, w_edge1[:width, :])).astype(BF)
    d_ext[...] = fold(dot_cols(sum_send, w_edge1[width : 2 * width, :]))
    d_recv = fold(dot_cols(sum_recv, w_edge1[2 * width :, :]))
    d_node[...] = g_node + dy_node + d_recv + d_ext[:count, :]
    for step, back in enumerate((back0, back1, back2, back3)):
        place = count + side_of(step, *odd) * rows
        back[...] = d_ext[pl.ds(pl.multiple_of(place, rows), rows), :].astype(BF)


def pair_sum_kernel(mine, other, out):
    out[...] = (mine[...].astype(F32) + other[...].astype(F32)).astype(BF)


def plane_sum_kernel(parts, d_node, lists, ret0, ret1, ret2, ret3, out, grad_nodes):
    rows, lanes = out.shape[1], out.shape[2]
    for block in range(out.shape[0]):
        r, c = block % 2 * rows, block // 2 * lanes
        total = parts[0, r : r + rows, c : c + lanes].astype(F32)
        for part in range(1, parts.shape[0]):
            total = total + parts[part, r : r + rows, c : c + lanes].astype(F32)
        out[block] = total
    odd = parities()
    total = d_node[...]
    for step, ret in enumerate((ret0, ret1, ret2, ret3)):
        row = lists[0, 0, pl.ds(side_of(step, *odd), 1), :]
        total = total + dot(pick(row, total.shape[0]).astype(BF), ret[...])
    grad_nodes[0, 0] = total.astype(BF)


def line_sum_kernel(factor, parts, out):
    total = parts[0]
    for part in range(1, parts.shape[0]):
        total = total + parts[part]
    total = (total * factor).astype(BF)
    for part in range(out.shape[0]):
        out[part] = total


def spread_kernel(blocks, out):
    tops = jnp.concatenate([blocks[2 * i] for i in range(4)], axis=1)
    ends = jnp.concatenate([blocks[2 * i + 1] for i in range(4)], axis=1)
    whole = jnp.concatenate([tops, ends], axis=0)
    for part in range(out.shape[0]):
        out[part] = whole


def place_kernel(other_core, half, *refs):
    outs, sems = refs[-5:-1], refs[-1]
    part = outs[0].shape[1] // 2
    side = lax.axis_index("c")
    side = 1 - side if other_core else side
    copies = []
    for out in outs:
        for block in range(out.shape[0] // (2 * part)):
            place = pl.multiple_of((2 * block + side) * part, part)
            start = len(copies) * part
            copies.append(
                pltpu.make_async_copy(
                    half.at[start : start + part], out.at[pl.ds(place, part)], sems.at[len(copies)]
                )
            )
    for copy in copies:
        copy.start()
    for copy in copies:
        copy.wait()


def call(kernel, outs, ins, limit=24, scratch=(), **kwargs):
    return pl.pallas_call(
        kernel,
        out_shape=outs,
        in_specs=ins,
        out_specs=jax.tree.map(lambda _: VMEM, outs),
        scratch_shapes=list(scratch),
        compiler_params=pltpu.CompilerParams(vmem_limit_bytes=limit << 20),
        **kwargs,
    )


def shape(dims, kind=BF):
    return jax.ShapeDtypeStruct(dims, kind)


def in_hbm(*arrays):
    return [pltpu.with_memory_space_constraint(array, pltpu.HBM) for array in arrays]


def pairs(count, first):
    made = []
    for i in range(first, count + first, 2):
        made += [(i, (i + 1) % count), ((i + 1) % count, i)]
    return made


def exchange(blocks):
    nx, ny = lax.axis_size(GX), lax.axis_size(GY)
    return [
        lax.ppermute(blocks[0], GX, pairs(nx, 0)),
        lax.ppermute(blocks[1], GX, pairs(nx, 1)),
        lax.ppermute(blocks[2], GY, pairs(ny, 0)),
        lax.ppermute(blocks[3], GY, pairs(ny, 1)),
    ]


def local(
    nodes,
    edges,
    senders,
    segments,
    send_lists,
    cot_nodes,
    cot_edges,
    w_edge1,
    w_edge2,
    w_node1,
    w_node2,
):
    count, width = nodes.shape[2:]
    lines = edges.shape[2]
    rows = send_lists.shape[3]
    weights = (w_edge1, w_edge2, w_node1, w_node2)
    total = sum(w.shape[0] for w in weights)
    block = [shape((rows, width))] * 4
    packs = call(
        pack_kernel,
        block,
        [ANY] * 2,
        scratch=[
            pltpu.VMEM((count, width), BF),
            pltpu.VMEM((4, rows), jnp.int32),
            pltpu.SemaphoreType.DMA((2,)),
        ],
    )(*in_hbm(nodes, send_lists))
    halos = exchange(packs)
    half = shape((total // 2, width))
    reach = count + 4 * rows
    node_next, grad_edges, d_node, *backs, keep, send = call(
        layer_kernel,
        [shape(nodes.shape), shape(edges.shape), shape((count, width), F32)] + block + [half] * 2,
        [ANY] * 2 + [VMEM] * 4 + [ANY] * 8,
        limit=28,
        scratch=[
            pltpu.VMEM((count, width), BF),
            pltpu.VMEM((lines, width), BF),
            pltpu.VMEM((1, lines), jnp.int32),
            pltpu.VMEM((1, lines), jnp.int32),
            pltpu.VMEM((count, width), BF),
            pltpu.VMEM((lines, width), BF),
            *[pltpu.VMEM(w.shape, BF) for w in weights],
            pltpu.VMEM((2 * reach, width), BF),
            pltpu.VMEM((2 * count, width), BF),
            pltpu.VMEM((lines, width), BF),
            pltpu.VMEM((count, width), BF),
            pltpu.VMEM((count, width), BF),
            pltpu.VMEM((reach, width), F32),
            pltpu.SemaphoreType.DMA((10,)),
        ],
    )(
        *in_hbm(nodes, edges),
        *halos,
        *in_hbm(senders, segments, cot_nodes, cot_edges, *weights),
    )

    returned = exchange(backs)
    got = lax.ppermute(send, "c", pairs(2, 0))
    pair = call(pair_sum_kernel, half, [VMEM] * 2)(keep, got)

    plane, line = lax.axis_size(PLANE), lax.axis_size("z")
    strip = total // 2 // plane
    cut = (line, strip // 2, width * 2 // line)
    pieces = lax.all_to_all(pair, PLANE, 0, 0, tiled=True).reshape(plane, strip, width)
    pieces, grad_nodes = call(
        plane_sum_kernel, [shape(cut, F32), shape(nodes.shape)], [VMEM] * 7
    )(pieces, d_node, send_lists, *returned)
    pieces = lax.all_to_all(pieces, "z", 0, 0, tiled=True)
    factor = float(lines * plane * line * 2) ** -0.5
    pieces = call(functools.partial(line_sum_kernel, factor), shape(cut), [VMEM])(pieces)
    pieces = lax.all_to_all(pieces, "z", 0, 0, tiled=True)
    pieces = call(spread_kernel, shape((plane, strip, width)), [VMEM])(pieces)
    mine = lax.all_to_all(pieces, PLANE, 0, 0, tiled=True).reshape(total // 2, width)
    other = lax.ppermute(mine, "c", pairs(2, 0))
    outs = [shape(w.shape) for w in weights]
    sems = [pltpu.SemaphoreType.DMA((total // width,))]
    grads = pl.pallas_call(
        functools.partial(place_kernel, False),
        out_shape=outs,
        in_specs=[VMEM],
        out_specs=[ANY] * 4,
        scratch_shapes=sems,
    )(mine)
    grads = pl.pallas_call(
        functools.partial(place_kernel, True),
        out_shape=outs,
        in_specs=[VMEM] + [ANY] * 4,
        out_specs=[ANY] * 4,
        scratch_shapes=sems,
        input_output_aliases={1: 0, 2: 1, 3: 2, 4: 3},
    )(other, *grads)
    return (node_next, grad_nodes, grad_edges, *grads)


def solution(mesh):
    fine = Mesh(mesh.devices.reshape(2, 4, 2, 2, 8), ("yh", "x", "c", "yl", "z"))
    tile = P(GX, GY)
    return jax.shard_map(
        local,
        mesh=fine,
        in_specs=(tile,) * 7 + (P(),) * 4,
        out_specs=(tile,) * 3 + (P(),) * 4,
        check_vma=False,
    )
```

time: 247 us -> 128 us (0.52); the launches traced: 243 us -> 128 us
  Pallas kernels: 123 us -> 16.3 us
  blocking collectives: 76.7 us -> 53.5 us
  waiting for transfers between devices: 6.17 us -> 26.6 us
  local copies, waits for them, and re-layouts: 12.8 us -> 2.5 us
  starting transfers between devices: 24.1 us -> 28.3 us
    pallas_call x8, Pallas kernels: 123 us -> 16.3 us  [the longest x1 8.05 us: local(): call(layer_kernel, [shape(nodes.shape), shape(edges.shape), shape((count,...]
    all_to_all x1 -> x0, blocking collectives: 28.3 us -> none  [local(): lax.all_to_all(pair, PLANE, 0, 0, tiled=True).reshape(plane, strip, width)]
    ppermute x10, waiting for transfers between devices: 6.17 us -> 24.2 us  [the longest x2 18.8 us: exchange(): lax.ppermute(blocks[1], GX, pairs(nx, 1))]
    unnamed x30 -> x6, local copies, waits for them, and re-layouts: 12.8 us -> 2.5 us
    all_to_all x1, blocking collectives: 24 us -> 29.3 us  [local(): lax.all_to_all(pieces, PLANE, 0, 0, tiled=True).reshape(total // 2, width)]
    all_to_all x0 -> x1, starting transfers between devices: none -> 3.84 us  [local(): lax.all_to_all(pair, PLANE, 0, 0, tiled=True).reshape(plane, strip, width)]
  transfers between devices with their start and end apart: 10 -> 11, of which waited for: 3 -> 5; matrix products, arithmetic and copies ran while one was open for 0% -> 0% of each run, Pallas kernels for 0% -> 2%
where the time goes in v2:
time: 128 us
  blocking collectives  53.5 us (42%)
  starting transfers between devices  28.3 us (22%)
  waiting for transfers between devices  26.6 us (21%)
  Pallas kernels  16.3 us (13%)
  local copies, waits for them, and re-layouts  2.5 us (2%)
    all_to_all x1, blocking collectives, local(): lax.all_to_all(pieces, PLANE, 0, 0, tiled=True).reshape(total // 2, width)  29.3 us
    all_to_all x2, blocking collectives, local(): pieces = lax.all_to_all(pieces, 'z', 0, 0, tiled=True)  24.2 us
    ppermute x2, waiting for transfers between devices, exchange(): lax.ppermute(blocks[1], GX, pairs(nx, 1))  18.8 us
    ppermute x2, starting transfers between devices, exchange(): lax.ppermute(blocks[3], GY, pairs(ny, 1))  10.3 us
    pallas_call x1, Pallas kernels, local(): call(layer_kernel, [shape(nodes.shape), shape(edges.shape), shape((count,...  8.05 us
    ppermute x1, starting transfers between devices, local(): got = lax.ppermute(send, 'c', pairs(2, 0))  4.65 us
    all_to_all x1, starting transfers between devices, local(): lax.all_to_all(pair, PLANE, 0, 0, tiled=True).reshape(plane, strip, width)  3.84 us
    ppermute x2, starting transfers between devices, exchange(): lax.ppermute(blocks[0], GX, pairs(nx, 0))  3.79 us
  transfers between devices with their start and end apart: 11, of which 5 were waited for; matrix products, arithmetic and copies ran while one was open for 0% of the time, Pallas kernels for 2%

profile of v2, /device:TPU:1, one launch (start us, length us, event | category | flops | bytes accessed | tf_op | source)
XLA Modules:
  0.0 127.9 jit_solution(10675064359829172892)
XLA Ops:
  0.6 1.1 shard_map.162
  1.7 3.3 %collective-permute-start = (bf16[16,512]{1,0:T(8,128)(2,1)S(1)}, bf16[16,512]{1,0:T(8,128)(2,1)S(1)}, u32[]{:S(2)}, u32[]{:S(2)}) collective-permute-start(bf16[16,512]{1,0:T(8,128)(2,1)S(1)} %get-tuple-element.30), channel_id=1, source_target_pairs={{0,16},{16,0},{32,48},{48,32},{64,80},{80,64},{96,112},{112,96},{1... | collective-permute-start | bytes 49160 | tf_op jit(solution)/shard_map/ppermute | solution.py:341
  5.0 1.1 collective-permute-start.2
  6.1 5.7 %collective-permute-start.3 = (bf16[16,512]{1,0:T(8,128)(2,1)S(1)}, bf16[16,512]{1,0:T(8,128)(2,1)S(1)}, u32[]{:S(2)}, u32[]{:S(2)}) collective-permute-start(bf16[16,512]{1,0:T(8,128)(2,1)S(1)} %get-tuple-element.33), channel_id=1, source_target_pairs={{1,2},{2,1},{3,4},{4,3},{5,6},{6,5},{7,8},{8,7},{9,10},{10,9},{11,... | collective-permute-start | bytes 49160 | tf_op jit(solution)/shard_map/ppermute | solution.py:344
  11.8 1.1 collective-permute-done.3.halo3
  12.9 8.1 %shard_map.163 = (bf16[1,1,64,512]{3,2,1,0:T(8,128)(2,1)}, bf16[1,1,384,512]{3,2,1,0:T(8,128)(2,1)}, f32[64,512]{1,0:T(8,128)S(1)}, bf16[16,512]{1,0:T(8,128)(2,...) custom-call(bf16[1,1,64,512]{3,2,1,0:T(8,128)(2,1)} %nodes_hbm.3, ...), custom_call_target="tpu_custom_call" | custom-call | tf_op jit(solution)/shard_map/pallas_call | solution.py:380
  21.0 4.6 %collective-permute-start.4 = (bf16[1792,512]{1,0:T(8,128)(2,1)S(1)}, bf16[1792,512]{1,0:T(8,128)(2,1)S(1)}, u32[]{:S(2)}, u32[]{:S(2)}) collective-permute-start(bf16[1792,512]{1,0:T(8,128)(2,1)S(1)} %get-tuple-element.36), channel_id=1, source_target_pairs={{0,16},{16,0},{1,17},{17,1},{2,18},{18,2},{3,19},{19,3},{4,20},{20... | collective-permute-start | bytes 5505032 | tf_op jit(solution)/shard_map/ppermute | solution.py:408
  25.6 3.4 %collective-permute-done.4.other = bf16[1792,512]{1,0:T(8,128)(2,1)S(1)} collective-permute-done((bf16[1792,512]{1,0:T(8,128)(2,1)S(1)}, bf16[1792,512]{1,0:T(8,128)(2,1)S(1)}, u32[]{:S(2)}, u32[]{:S(2)}) %collective-permute-start.4) | collective-permute-done | bytes 1835040 | tf_op jit(solution)/shard_map/ppermute | solution.py:408
  29.5 1.2 copy-done
  30.7 3.8 %all-to-all-start = ((bf16[16,112,512]{2,1,0:T(8,128)(2,1)}), bf16[16,112,512]{2,1,0:T(8,128)(2,1)S(1)}, u32[]{:S(2)}, u32[]{:S(2)}) async-start(bf16[16,112,512]{2,1,0:T(8,128)(2,1)} %bitcast.2), calls=%async_computation | async-start | bytes 3670016 | tf_op jit(solution)/shard_map/all_to_all | solution.py:414
  34.6 0.5 collective-permute-start.5
  35.0 1.4 %collective-permute-start.6 = (bf16[16,512]{1,0:T(8,128)(2,1)S(1)}, bf16[16,512]{1,0:T(8,128)(2,1)S(1)}, u32[]{:S(2)}, u32[]{:S(2)}) collective-permute-start(bf16[16,512]{1,0:T(8,128)(2,1)S(1)} %get-tuple-element.39), channel_id=1, source_target_pairs={{16,32},{32,16},{48,64},{64,48},{80,96},{96,80},{112,128},{128,112... | collective-permute-start | bytes 49160 | tf_op jit(solution)/shard_map/ppermute | solution.py:342
  36.5 4.6 %collective-permute-start.8 = (bf16[16,512]{1,0:T(8,128)(2,1)S(1)}, bf16[16,512]{1,0:T(8,128)(2,1)S(1)}, u32[]{:S(2)}, u32[]{:S(2)}) collective-permute-start(bf16[16,512]{1,0:T(8,128)(2,1)S(1)} %get-tuple-element.41), channel_id=1, source_target_pairs={{1,2},{2,1},{3,4},{4,3},{5,6},{6,5},{7,8},{8,7},{9,10},{10,9},{11,... | collective-permute-start | bytes 49160 | tf_op jit(solution)/shard_map/ppermute | solution.py:344
  41.1 18.8 %collective-permute-done.6.ret1 = bf16[16,512]{1,0:T(8,128)(2,1)S(1)} collective-permute-done((bf16[16,512]{1,0:T(8,128)(2,1)S(1)}, bf16[16,512]{1,0:T(8,128)(2,1)S(1)}, u32[]{:S(2)}, u32[]{:S(2)}) %collective-permute-start.6) | collective-permute-done | bytes 16416 | tf_op jit(solution)/shard_map/ppermute | solution.py:342
  60.0 2.3 %all-to-all-done.parts = bf16[16,112,512]{2,1,0:T(8,128)(2,1)S(1)} async-done(((bf16[16,112,512]{2,1,0:T(8,128)(2,1)}), bf16[16,112,512]{2,1,0:T(8,128)(2,1)S(1)}, u32[]{:S(2)}, u32[]{:S(2)}) %all-to-all-start) | async-done | bytes 1835040 | tf_op jit(solution)/shard_map/all_to_all | solution.py:414
  62.3 1.1 shard_map.165
  63.4 13.9 %all_to_all.24.parts = f32[8,56,128]{2,1,0:T(8,128)S(1)} all-to-all(f32[8,56,128]{2,1,0:T(8,128)S(1)} %get-tuple-element.44), channel_id=1, replica_groups=mesh['yh'=2,'x'=4,'c'=2,'yl'=2,'z'=8] {'z'}, dimensions={0} | all-to-all | bytes 458752 | tf_op jit(solution)/shard_map/all_to_all | solution.py:418
  77.3 10.2 %all_to_all.25.blocks = bf16[8,56,128]{2,1,0:T(8,128)(2,1)S(1)} all-to-all(bf16[8,56,128]{2,1,0:T(8,128)(2,1)S(1)} %shard_map.166), channel_id=1, replica_groups=mesh['yh'=2,'x'=4,'c'=2,'yl'=2,'z'=8] {'z'}, dimensions={0} | all-to-all | bytes 229376 | tf_op jit(solution)/shard_map/all_to_all | solution.py:421
  87.7 29.3 %all_to_all.26 = bf16[16,112,512]{2,1,0:T(8,128)(2,1)} all-to-all(bf16[16,112,512]{2,1,0:T(8,128)(2,1)S(1)} %shard_map.167), channel_id=1, replica_groups=mesh['yh'=2,'x'=4,'c'=2,'yl'=2,'z'=8] {'yh','x','yl'}, dimensions={0} | all-to-all | bytes 3670016 | tf_op jit(solution)/shard_map/all_to_all | solution.py:423
  117.0 3.2 %collective-permute-start.9 = (bf16[1792,512]{1,0:T(8,128)(2,1)}, bf16[1792,512]{1,0:T(8,128)(2,1)S(1)}, u32[]{:S(2)}, u32[]{:S(2)}) collective-permute-start(bf16[1792,512]{1,0:T(8,128)(2,1)} %bitcast.1.half), channel_id=1, source_target_pairs={{0,16},{16,0},{1,17},{17,1},{2,18},{18,2},{3,19},{19,3},{4,20},{20... | collective-permute-start | bytes 5505032 | tf_op jit(solution)/shard_map/ppermute | solution.py:424
  120.3 2.8 %shard_map.168 = (bf16[1536,512]{1,0:T(8,128)(2,1)}, bf16[512,512]{1,0:T(8,128)(2,1)}, bf16[1024,512]{1,0:T(8,128)(2,1)}, bf16[512,512]{1,0:T(8,128)(2,1)}) custom-call(bf16[1792,512]{1,0:T(8,128)(2,1)} %bitcast.1.half), custom_call_target="tpu_custom_call" | custom-call | tf_op jit(solution)/shard_map/pallas_call | solution.py:427
  123.0 0.8 collective-permute-done.9.half
  123.9 1.3 copy-done.2
  125.1 2.8 %shard_map.169 = (bf16[1536,512]{1,0:T(8,128)(2,1)}, bf16[512,512]{1,0:T(8,128)(2,1)}, bf16[1024,512]{1,0:T(8,128)(2,1)}, bf16[512,512]{1,0:T(8,128)(2,1)}) custom-call(bf16[1792,512]{1,0:T(8,128)(2,1)} %copy-done.2, bf16[1536,512]{1,0:T(8,128)(2,1)} %get-tuple-element.45.refs_0_, ...), custom_call_target="tpu_custom_call", output_to_operand_aliasing={{0}: (1, {}), {1}: (2, {}), {2}: (3, {}), {3}: (4, {})} | custom-call | tf_op jit(solution)/shard_map/pallas_call | solution.py:434
  (15 shorter events, 0.6 us)
Async XLA Ops:
  1.7 10.1 %collective-permute-start = (bf16[16,512]{1,0:T(8,128)(2,1)S(1)}, bf16[16,512]{1,0:T(8,128)(2,1)S(1)}, u32[]{:S(2)}, u32[]{:S(2)}) collective-permute-start(bf16[16,512]{1,0:T(8,128)(2,1)S(1)} %get-tuple-element.30), channel_id=1, source_target_pairs={{0,16},{16,0},{32,48},{48,32},{64,80},{80,64},{96,112},{112,96},{1... | collective-permute-start | bytes 49160 | tf_op jit(solution)/shard_map/ppermute | solution.py:341
  5.0 6.8 %collective-permute-start.1 = (bf16[16,512]{1,0:T(8,128)(2,1)S(1)}, bf16[16,512]{1,0:T(8,128)(2,1)S(1)}, u32[]{:S(2)}, u32[]{:S(2)}) collective-permute-start(bf16[16,512]{1,0:T(8,128)(2,1)S(1)} %get-tuple-element.31), channel_id=1, source_target_pairs={{16,32},{32,16},{48,64},{64,48},{80,96},{96,80},{112,128},{128,112... | collective-permute-start | bytes 49160 | tf_op jit(solution)/shard_map/ppermute | solution.py:342
  5.0 6.8 %collective-permute-start.2 = (bf16[16,512]{1,0:T(8,128)(2,1)S(1)}, bf16[16,512]{1,0:T(8,128)(2,1)S(1)}, u32[]{:S(2)}, u32[]{:S(2)}) collective-permute-start(bf16[16,512]{1,0:T(8,128)(2,1)S(1)} %get-tuple-element.32), channel_id=1, source_target_pairs={{0,1},{1,0},{2,3},{3,2},{4,5},{5,4},{6,7},{7,6},{8,9},{9,8},{10,11... | collective-permute-start | bytes 49160 | tf_op jit(solution)/shard_map/ppermute | solution.py:343
  6.1 6.8 %collective-permute-start.3 = (bf16[16,512]{1,0:T(8,128)(2,1)S(1)}, bf16[16,512]{1,0:T(8,128)(2,1)S(1)}, u32[]{:S(2)}, u32[]{:S(2)}) collective-permute-start(bf16[16,512]{1,0:T(8,128)(2,1)S(1)} %get-tuple-element.33), channel_id=1, source_target_pairs={{1,2},{2,1},{3,4},{4,3},{5,6},{6,5},{7,8},{8,7},{9,10},{10,9},{11,... | collective-permute-start | bytes 49160 | tf_op jit(solution)/shard_map/ppermute | solution.py:344
  21.0 8.1 %collective-permute-start.4 = (bf16[1792,512]{1,0:T(8,128)(2,1)S(1)}, bf16[1792,512]{1,0:T(8,128)(2,1)S(1)}, u32[]{:S(2)}, u32[]{:S(2)}) collective-permute-start(bf16[1792,512]{1,0:T(8,128)(2,1)S(1)} %get-tuple-element.36), channel_id=1, source_target_pairs={{0,16},{16,0},{1,17},{17,1},{2,18},{18,2},{3,19},{19,3},{4,20},{20... | collective-permute-start | bytes 5505032 | tf_op jit(solution)/shard_map/ppermute | solution.py:408
  29.5 1.3 copy-start
  30.7 31.6 %copy-start.1 = (s32[1,1,4,16]{3,2,1,0:T(4,128)S(1)}, s32[1,1,4,16]{3,2,1,0:T(4,128)}, u32[]{:S(2)}) copy-start(s32[1,1,4,16]{3,2,1,0:T(4,128)} %lists.1) | copy-start | bytes 772
  30.7 31.6 %all-to-all-start = ((bf16[16,112,512]{2,1,0:T(8,128)(2,1)}), bf16[16,112,512]{2,1,0:T(8,128)(2,1)S(1)}, u32[]{:S(2)}, u32[]{:S(2)}) async-start(bf16[16,112,512]{2,1,0:T(8,128)(2,1)} %bitcast.2), calls=%async_computation | async-start | bytes 3670016 | tf_op jit(solution)/shard_map/all_to_all | solution.py:414
  34.6 6.5 %collective-permute-start.5 = (bf16[16,512]{1,0:T(8,128)(2,1)S(1)}, bf16[16,512]{1,0:T(8,128)(2,1)S(1)}, u32[]{:S(2)}, u32[]{:S(2)}) collective-permute-start(bf16[16,512]{1,0:T(8,128)(2,1)S(1)} %get-tuple-element.38), channel_id=1, source_target_pairs={{0,16},{16,0},{32,48},{48,32},{64,80},{80,64},{96,112},{112,96},{1... | collective-permute-start | bytes 49160 | tf_op jit(solution)/shard_map/ppermute | solution.py:341
  35.0 24.9 %collective-permute-start.6 = (bf16[16,512]{1,0:T(8,128)(2,1)S(1)}, bf16[16,512]{1,0:T(8,128)(2,1)S(1)}, u32[]{:S(2)}, u32[]{:S(2)}) collective-permute-start(bf16[16,512]{1,0:T(8,128)(2,1)S(1)} %get-tuple-element.39), channel_id=1, source_target_pairs={{16,32},{32,16},{48,64},{64,48},{80,96},{96,80},{112,128},{128,112... | collective-permute-start | bytes 49160 | tf_op jit(solution)/shard_map/ppermute | solution.py:342
  36.5 23.5 %collective-permute-start.7 = (bf16[16,512]{1,0:T(8,128)(2,1)S(1)}, bf16[16,512]{1,0:T(8,128)(2,1)S(1)}, u32[]{:S(2)}, u32[]{:S(2)}) collective-permute-start(bf16[16,512]{1,0:T(8,128)(2,1)S(1)} %get-tuple-element.40), channel_id=1, source_target_pairs={{0,1},{1,0},{2,3},{3,2},{4,5},{5,4},{6,7},{7,6},{8,9},{9,8},{10,11... | collective-permute-start | bytes 49160 | tf_op jit(solution)/shard_map/ppermute | solution.py:343
  36.5 23.5 %collective-permute-start.8 = (bf16[16,512]{1,0:T(8,128)(2,1)S(1)}, bf16[16,512]{1,0:T(8,128)(2,1)S(1)}, u32[]{:S(2)}, u32[]{:S(2)}) collective-permute-start(bf16[16,512]{1,0:T(8,128)(2,1)S(1)} %get-tuple-element.41), channel_id=1, source_target_pairs={{1,2},{2,1},{3,4},{4,3},{5,6},{6,5},{7,8},{8,7},{9,10},{10,9},{11,... | collective-permute-start | bytes 49160 | tf_op jit(solution)/shard_map/ppermute | solution.py:344
  117.0 6.8 %collective-permute-start.9 = (bf16[1792,512]{1,0:T(8,128)(2,1)}, bf16[1792,512]{1,0:T(8,128)(2,1)S(1)}, u32[]{:S(2)}, u32[]{:S(2)}) collective-permute-start(bf16[1792,512]{1,0:T(8,128)(2,1)} %bitcast.1.half), channel_id=1, source_target_pairs={{0,16},{16,0},{1,17},{17,1},{2,18},{18,2},{3,19},{19,3},{4,20},{20... | collective-permute-start | bytes 5505032 | tf_op jit(solution)/shard_map/ppermute | solution.py:424
  123.9 1.3 copy-start.2

commit v3 on v2

--- a/solution.py
+++ b/solution.py
@@ -83,7 +83,7 @@
 
 
 def side_of(step, row_odd, col_odd):
-    return (1 - row_odd, row_odd, 3 - col_odd, 2 + col_odd)[step]
+    return (2 + col_odd, row_odd, 1 - row_odd, 3 - col_odd)[step]
 
 
 def pack_kernel(nodes_hbm, lists_hbm, *refs):
@@ -254,37 +254,40 @@
     out[...] = (mine[...].astype(F32) + other[...].astype(F32)).astype(BF)
 
 
-def plane_sum_kernel(parts, d_node, lists, ret0, ret1, ret2, ret3, out, grad_nodes):
+def plane_sum_kernel(parts, *refs):
+    backs, out, onward = refs[:4], refs[4], refs[5:]
+    for back, ref in zip(backs, onward, strict=True):
+        ref[...] = back[...]
     rows, lanes = out.shape[1], out.shape[2]
     for block in range(out.shape[0]):
         r, c = block % 2 * rows, block // 2 * lanes
         total = parts[0, r : r + rows, c : c + lanes].astype(F32)
         for part in range(1, parts.shape[0]):
             total = total + parts[part, r : r + rows, c : c + lanes].astype(F32)
-        out[block] = total
+        out[block] = total.astype(BF)
+
+
+def line_sum_kernel(factor, parts, out):
+    total = parts[0].astype(F32)
+    for part in range(1, parts.shape[0]):
+        total = total + parts[part].astype(F32)
+    total = (total * factor).astype(BF)
+    for part in range(out.shape[0]):
+        out[part] = total
+
+
+def spread_kernel(blocks, d_node, lists, ret0, ret1, ret2, ret3, out, grad_nodes):
+    tops = jnp.concatenate([blocks[2 * i] for i in range(4)], axis=1)
+    ends = jnp.concatenate([blocks[2 * i + 1] for i in range(4)], axis=1)
+    whole = jnp.concatenate([tops, ends], axis=0)
+    for part in range(out.shape[0]):
+        out[part] = whole
     odd = parities()
     total = d_node[...]
     for step, ret in enumerate((ret0, ret1, ret2, ret3)):
         row = lists[0, 0, pl.ds(side_of(step, *odd), 1), :]
         total = total + dot(pick(row, total.shape[0]).astype(BF), ret[...])
     grad_nodes[0, 0] = total.astype(BF)
-
-
-def line_sum_kernel(factor, parts, out):
-    total = parts[0]
-    for part in range(1, parts.shape[0]):
-        total = total + parts[part]
-    total = (total * factor).astype(BF)
-    for part in range(out.shape[0]):
-        out[part] = total
-
-
-def spread_kernel(blocks, out):
-    tops = jnp.concatenate([blocks[2 * i] for i in range(4)], axis=1)
-    ends = jnp.concatenate([blocks[2 * i + 1] for i in range(4)], axis=1)
-    whole = jnp.concatenate([tops, ends], axis=0)
-    for part in range(out.shape[0]):
-        out[part] = whole
 
 
 def place_kernel(other_core, half, *refs):
@@ -338,10 +341,10 @@
 def exchange(blocks):
     nx, ny = lax.axis_size(GX), lax.axis_size(GY)
     return [
-        lax.ppermute(blocks[0], GX, pairs(nx, 0)),
+        lax.ppermute(blocks[0], GY, pairs(ny, 1)),
         lax.ppermute(blocks[1], GX, pairs(nx, 1)),
-        lax.ppermute(blocks[2], GY, pairs(ny, 0)),
-        lax.ppermute(blocks[3], GY, pairs(ny, 1)),
+        lax.ppermute(blocks[2], GX, pairs(nx, 0)),
+        lax.ppermute(blocks[3], GY, pairs(ny, 0)),
     ]
 
 
@@ -404,22 +407,24 @@
         *in_hbm(senders, segments, cot_nodes, cot_edges, *weights),
     )
 
-    returned = exchange(backs)
     got = lax.ppermute(send, "c", pairs(2, 0))
-    pair = call(pair_sum_kernel, half, [VMEM] * 2)(keep, got)
+    pair = call(pair_sum_kernel, half, [VMEM] * 2, limit=8)(keep, got)
 
     plane, line = lax.axis_size(PLANE), lax.axis_size("z")
     strip = total // 2 // plane
     cut = (line, strip // 2, width * 2 // line)
     pieces = lax.all_to_all(pair, PLANE, 0, 0, tiled=True).reshape(plane, strip, width)
-    pieces, grad_nodes = call(
-        plane_sum_kernel, [shape(cut, F32), shape(nodes.shape)], [VMEM] * 7
-    )(pieces, d_node, send_lists, *returned)
+    pieces, *backs = call(plane_sum_kernel, [shape(cut)] + block, [VMEM] * 5, limit=8)(
+        pieces, *backs
+    )
+    returned = exchange(backs)
     pieces = lax.all_to_all(pieces, "z", 0, 0, tiled=True)
     factor = float(lines * plane * line * 2) ** -0.5
-    pieces = call(functools.partial(line_sum_kernel, factor), shape(cut), [VMEM])(pieces)
+    pieces = call(functools.partial(line_sum_kernel, factor), shape(cut), [VMEM], limit=8)(pieces)
     pieces = lax.all_to_all(pieces, "z", 0, 0, tiled=True)
-    pieces = call(spread_kernel, shape((plane, strip, width)), [VMEM])(pieces)
+    pieces, grad_nodes = call(
+        spread_kernel, [shape((plane, strip, width)), shape(nodes.shape)], [VMEM] * 7, limit=8
+    )(pieces, d_node, send_lists, *returned)
     mine = lax.all_to_all(pieces, PLANE, 0, 0, tiled=True).reshape(total // 2, width)
     other = lax.ppermute(mine, "c", pairs(2, 0))
     outs = [shape(w.shape) for w in weights]
@@ -430,6 +435,7 @@
         in_specs=[VMEM],
         out_specs=[ANY] * 4,
         scratch_shapes=sems,
+        compiler_params=pltpu.CompilerParams(vmem_limit_bytes=4 << 20),
     )(mine)
     grads = pl.pallas_call(
         functools.partial(place_kernel, True),
@@ -437,6 +443,7 @@
         in_specs=[VMEM] + [ANY] * 4,
         out_specs=[ANY] * 4,
         scratch_shapes=sems,
+        compiler_params=pltpu.CompilerParams(vmem_limit_bytes=4 << 20),
         input_output_aliases={1: 0, 2: 1, 3: 2, 4: 3},
     )(other, *grads)
     return (node_next, grad_nodes, grad_edges, *grads)

time: 128 us -> 121 us (0.945)
  waiting for transfers between devices: 26.6 us -> 11 us
  blocking collectives: 53.5 us -> 68.7 us
  local copies, waits for them, and re-layouts: 2.5 us -> 0.01 us
  Pallas kernels: 16.3 us -> 13.9 us
  starting transfers between devices: 28.3 us -> 26.4 us
    all_to_all x0 -> x1, blocking collectives: none -> 29 us  [local(): lax.all_to_all(pair, PLANE, 0, 0, tiled=True).reshape(plane, strip, width)]
    ppermute x2, waiting for transfers between devices: 18.8 us -> 1.21 us  [exchange(): lax.ppermute(blocks[1], GX, pairs(nx, 1))]
    all_to_all x2 -> x1, blocking collectives: 24.2 us -> 10.1 us  [local(): pieces = lax.all_to_all(pieces, 'z', 0, 0, tiled=True)]
    ppermute x1, starting transfers between devices: 4.65 us -> 1.25 us  [local(): got = lax.ppermute(send, 'c', pairs(2, 0))]
    ppermute x2, starting transfers between devices: 1.43 us -> 4.77 us  [exchange(): lax.ppermute(blocks[1], GX, pairs(nx, 1))]
    ppermute x6, waiting for transfers between devices: 1.13 us -> 4.25 us  [the longest x2 3.41 us: exchange(): lax.ppermute(blocks[3], GY, pairs(ny, 0))]
    unnamed x6 -> x2, local copies, waits for them, and re-layouts: 2.5 us -> 0.01 us
    all_to_all x1, waiting for transfers between devices: 2.33 us -> 0.01 us  [local(): pieces = lax.all_to_all(pieces, 'z', 0, 0, tiled=True)]
  transfers between devices with their start and end apart: 11 -> 11, of which waited for: 5 -> 6; matrix products, arithmetic and copies ran while one was open for 0% -> 0% of each run, Pallas kernels for 2% -> 1%
where the time goes in v3:
time: 121 us
  blocking collectives  68.7 us (57%)
  starting transfers between devices  26.4 us (22%)
  Pallas kernels  13.9 us (11%)
  waiting for transfers between devices  11 us (9%)
    all_to_all x1, blocking collectives, local(): lax.all_to_all(pieces, PLANE, 0, 0, tiled=True).reshape(total // 2, width)  29.5 us
    all_to_all x1, blocking collectives, local(): lax.all_to_all(pair, PLANE, 0, 0, tiled=True).reshape(plane, strip, width)  29 us
    all_to_all x1, blocking collectives, local(): pieces = lax.all_to_all(pieces, 'z', 0, 0, tiled=True)  10.1 us
    ppermute x2, starting transfers between devices, exchange(): lax.ppermute(blocks[0], GY, pairs(ny, 1))  10.1 us
    pallas_call x1, Pallas kernels, local(): call(layer_kernel, [shape(nodes.shape), shape(edges.shape), shape((count,...  8.04 us
    ppermute x2, starting transfers between devices, exchange(): lax.ppermute(blocks[1], GX, pairs(nx, 1))  4.77 us
    ppermute x2, starting transfers between devices, exchange(): lax.ppermute(blocks[2], GX, pairs(nx, 0))  3.66 us
    ppermute x2, waiting for transfers between devices, exchange(): lax.ppermute(blocks[3], GY, pairs(ny, 0))  3.41 us
  transfers between devices with their start and end apart: 11, of which 6 were waited for; matrix products, arithmetic and copies ran while one was open for 0% of the time, Pallas kernels for 1%

profile of v3, /device:TPU:1, one launch (start us, length us, event | category | flops | bytes accessed | tf_op | source)
XLA Modules:
  0.0 120.7 jit_solution(12241536160056163138)
XLA Ops:
  0.6 1.1 shard_map.162
  1.7 7.5 %collective-permute-start = (bf16[16,512]{1,0:T(8,128)(2,1)S(1)}, bf16[16,512]{1,0:T(8,128)(2,1)S(1)}, u32[]{:S(2)}, u32[]{:S(2)}) collective-permute-start(bf16[16,512]{1,0:T(8,128)(2,1)S(1)} %get-tuple-element.35), channel_id=1, source_target_pairs={{1,2},{2,1},{3,4},{4,3},{5,6},{6,5},{7,8},{8,7},{9,10},{10,9},{11,... | collective-permute-start | bytes 49160 | tf_op jit(solution)/shard_map/ppermute | solution.py:344
  9.2 2.1 %collective-permute-start.1 = (bf16[16,512]{1,0:T(8,128)(2,1)S(1)}, bf16[16,512]{1,0:T(8,128)(2,1)S(1)}, u32[]{:S(2)}, u32[]{:S(2)}) collective-permute-start(bf16[16,512]{1,0:T(8,128)(2,1)S(1)} %get-tuple-element.36), channel_id=1, source_target_pairs={{16,32},{32,16},{48,64},{64,48},{80,96},{96,80},{112,128},{128,112... | collective-permute-start | bytes 49160 | tf_op jit(solution)/shard_map/ppermute | solution.py:345
  11.3 3.2 %collective-permute-start.2 = (bf16[16,512]{1,0:T(8,128)(2,1)S(1)}, bf16[16,512]{1,0:T(8,128)(2,1)S(1)}, u32[]{:S(2)}, u32[]{:S(2)}) collective-permute-start(bf16[16,512]{1,0:T(8,128)(2,1)S(1)} %get-tuple-element.37), channel_id=1, source_target_pairs={{0,16},{16,0},{32,48},{48,32},{64,80},{80,64},{96,112},{112,96},{1... | collective-permute-start | bytes 49160 | tf_op jit(solution)/shard_map/ppermute | solution.py:346
  14.4 0.8 collective-permute-done.2.halo2
  15.3 1.8 %collective-permute-done.3.halo3 = bf16[16,512]{1,0:T(8,128)(2,1)S(1)} collective-permute-done((bf16[16,512]{1,0:T(8,128)(2,1)S(1)}, bf16[16,512]{1,0:T(8,128)(2,1)S(1)}, u32[]{:S(2)}, u32[]{:S(2)}) %collective-permute-start.3) | collective-permute-done | bytes 16416 | tf_op jit(solution)/shard_map/ppermute | solution.py:347
  17.0 8.0 %shard_map.163 = (bf16[1,1,64,512]{3,2,1,0:T(8,128)(2,1)}, bf16[1,1,384,512]{3,2,1,0:T(8,128)(2,1)}, f32[64,512]{1,0:T(8,128)S(1)}, bf16[16,512]{1,0:T(8,128)(2,...) custom-call(bf16[1,1,64,512]{3,2,1,0:T(8,128)(2,1)} %nodes_hbm.3, ...), custom_call_target="tpu_custom_call" | custom-call | tf_op jit(solution)/shard_map/pallas_call | solution.py:383
  25.1 1.3 %collective-permute-start.4 = (bf16[1792,512]{1,0:T(8,128)(2,1)S(1)}, bf16[1792,512]{1,0:T(8,128)(2,1)S(1)}, u32[]{:S(2)}, u32[]{:S(2)}) collective-permute-start(bf16[1792,512]{1,0:T(8,128)(2,1)S(1)} %get-tuple-element.41), channel_id=1, source_target_pairs={{0,16},{16,0},{1,17},{17,1},{2,18},{18,2},{3,19},{19,3},{4,20},{20... | collective-permute-start | bytes 5505032 | tf_op jit(solution)/shard_map/ppermute | solution.py:410
  26.3 3.4 %collective-permute-done.4.other = bf16[1792,512]{1,0:T(8,128)(2,1)S(1)} collective-permute-done((bf16[1792,512]{1,0:T(8,128)(2,1)S(1)}, bf16[1792,512]{1,0:T(8,128)(2,1)S(1)}, u32[]{:S(2)}, u32[]{:S(2)}) %collective-permute-start.4) | collective-permute-done | bytes 1835040 | tf_op jit(solution)/shard_map/ppermute | solution.py:410
  30.1 29.0 %all_to_all.24.parts = bf16[16,112,512]{2,1,0:T(8,128)(2,1)S(1)} all-to-all(bf16[16,112,512]{2,1,0:T(8,128)(2,1)S(1)} %bitcast.4), channel_id=1, replica_groups=mesh['yh'=2,'x'=4,'c'=2,'yl'=2,'z'=8] {'yh','x','yl'}, dimensions={0} | all-to-all | bytes 3670016 | tf_op jit(solution)/shard_map/all_to_all | solution.py:416
  59.4 10.1 %all_to_all.25.parts = bf16[8,56,128]{2,1,0:T(8,128)(2,1)S(1)} all-to-all(bf16[8,56,128]{2,1,0:T(8,128)(2,1)S(1)} %get-tuple-element.46), channel_id=1, replica_groups=mesh['yh'=2,'x'=4,'c'=2,'yl'=2,'z'=8] {'z'}, dimensions={0} | all-to-all | bytes 229376 | tf_op jit(solution)/shard_map/all_to_all | solution.py:421
  69.5 0.7 shard_map.166
  70.2 3.4 %all-to-all-start.2 = ((bf16[8,56,128]{2,1,0:T(8,128)(2,1)}), bf16[8,56,128]{2,1,0:T(8,128)(2,1)S(1)}, u32[]{:S(2)}, u32[]{:S(2)}) async-start(bf16[8,56,128]{2,1,0:T(8,128)(2,1)} %shard_map.166), calls=%async_computation.2 | async-start | bytes 229376 | tf_op jit(solution)/shard_map/all_to_all | solution.py:424
  73.6 2.6 %collective-permute-start.5 = (bf16[16,512]{1,0:T(8,128)(2,1)S(1)}, bf16[16,512]{1,0:T(8,128)(2,1)S(1)}, u32[]{:S(2)}, u32[]{:S(2)}) collective-permute-start(bf16[16,512]{1,0:T(8,128)(2,1)S(1)} %get-tuple-element.48), channel_id=1, source_target_pairs={{1,2},{2,1},{3,4},{4,3},{5,6},{6,5},{7,8},{8,7},{9,10},{10,9},{11,... | collective-permute-start | bytes 49160 | tf_op jit(solution)/shard_map/ppermute | solution.py:344
  76.2 2.7 %collective-permute-start.6 = (bf16[16,512]{1,0:T(8,128)(2,1)S(1)}, bf16[16,512]{1,0:T(8,128)(2,1)S(1)}, u32[]{:S(2)}, u32[]{:S(2)}) collective-permute-start(bf16[16,512]{1,0:T(8,128)(2,1)S(1)} %get-tuple-element.49), channel_id=1, source_target_pairs={{16,32},{32,16},{48,64},{64,48},{80,96},{96,80},{112,128},{128,112... | collective-permute-start | bytes 49160 | tf_op jit(solution)/shard_map/ppermute | solution.py:345
  78.9 0.5 collective-permute-start.7
  79.4 1.2 %collective-permute-done.6.ret1 = bf16[16,512]{1,0:T(8,128)(2,1)S(1)} collective-permute-done((bf16[16,512]{1,0:T(8,128)(2,1)S(1)}, bf16[16,512]{1,0:T(8,128)(2,1)S(1)}, u32[]{:S(2)}, u32[]{:S(2)}) %collective-permute-start.6) | collective-permute-done | bytes 16416 | tf_op jit(solution)/shard_map/ppermute | solution.py:345
  80.6 1.7 %collective-permute-done.8.ret3 = bf16[16,512]{1,0:T(8,128)(2,1)S(1)} collective-permute-done((bf16[16,512]{1,0:T(8,128)(2,1)S(1)}, bf16[16,512]{1,0:T(8,128)(2,1)S(1)}, u32[]{:S(2)}, u32[]{:S(2)}) %collective-permute-start.8) | collective-permute-done | bytes 16416 | tf_op jit(solution)/shard_map/ppermute | solution.py:347
  82.3 1.0 shard_map.167
  83.3 29.5 %all_to_all.26 = bf16[16,112,512]{2,1,0:T(8,128)(2,1)S(1)} all-to-all(bf16[16,112,512]{2,1,0:T(8,128)(2,1)S(1)} %get-tuple-element.54), channel_id=1, replica_groups=mesh['yh'=2,'x'=4,'c'=2,'yl'=2,'z'=8] {'yh','x','yl'}, dimensions={0} | all-to-all | bytes 3670016 | tf_op jit(solution)/shard_map/all_to_all | solution.py:428
  112.8 3.2 %collective-permute-start.9 = (bf16[1792,512]{1,0:T(8,128)(2,1)S(1)}, bf16[1792,512]{1,0:T(8,128)(2,1)S(1)}, u32[]{:S(2)}, u32[]{:S(2)}) collective-permute-start(bf16[1792,512]{1,0:T(8,128)(2,1)S(1)} %bitcast.2), channel_id=1, source_target_pairs={{0,16},{16,0},{1,17},{17,1},{2,18},{18,2},{3,19},{19,3},{4,20},{20... | collective-permute-start | bytes 5505032 | tf_op jit(solution)/shard_map/ppermute | solution.py:429
  116.0 1.3 %shard_map.168 = (bf16[1536,512]{1,0:T(8,128)(2,1)}, bf16[512,512]{1,0:T(8,128)(2,1)}, bf16[1024,512]{1,0:T(8,128)(2,1)}, bf16[512,512]{1,0:T(8,128)(2,1)}) custom-call(bf16[1792,512]{1,0:T(8,128)(2,1)S(1)} %bitcast.3), custom_call_target="tpu_custom_call" | custom-call | tf_op jit(solution)/shard_map/pallas_call | solution.py:432
  117.3 2.1 %collective-permute-done.9.half = bf16[1792,512]{1,0:T(8,128)(2,1)S(1)} collective-permute-done((bf16[1792,512]{1,0:T(8,128)(2,1)S(1)}, bf16[1792,512]{1,0:T(8,128)(2,1)S(1)}, u32[]{:S(2)}, u32[]{:S(2)}) %collective-permute-start.9) | collective-permute-done | bytes 1835040 | tf_op jit(solution)/shard_map/ppermute | solution.py:429
  119.4 1.3 %shard_map.169 = (bf16[1536,512]{1,0:T(8,128)(2,1)}, bf16[512,512]{1,0:T(8,128)(2,1)}, bf16[1024,512]{1,0:T(8,128)(2,1)}, bf16[512,512]{1,0:T(8,128)(2,1)}) custom-call(bf16[1792,512]{1,0:T(8,128)(2,1)S(1)} %collective-permute-done.9.half, ...), custom_call_target="tpu_custom_call", output_to_operand_aliasing={{0}: (1, {}), {1}: (2, {}), {2}: (3, {}), {3}: (4, {})} | custom-call | tf_op jit(solution)/shard_map/pallas_call | solution.py:440
  (11 shorter events, 0.7 us)
Async XLA Ops:
  1.7 12.7 %collective-permute-start = (bf16[16,512]{1,0:T(8,128)(2,1)S(1)}, bf16[16,512]{1,0:T(8,128)(2,1)S(1)}, u32[]{:S(2)}, u32[]{:S(2)}) collective-permute-start(bf16[16,512]{1,0:T(8,128)(2,1)S(1)} %get-tuple-element.35), channel_id=1, source_target_pairs={{1,2},{2,1},{3,4},{4,3},{5,6},{6,5},{7,8},{8,7},{9,10},{10,9},{11,... | collective-permute-start | bytes 49160 | tf_op jit(solution)/shard_map/ppermute | solution.py:344
  9.2 5.2 %collective-permute-start.1 = (bf16[16,512]{1,0:T(8,128)(2,1)S(1)}, bf16[16,512]{1,0:T(8,128)(2,1)S(1)}, u32[]{:S(2)}, u32[]{:S(2)}) collective-permute-start(bf16[16,512]{1,0:T(8,128)(2,1)S(1)} %get-tuple-element.36), channel_id=1, source_target_pairs={{16,32},{32,16},{48,64},{64,48},{80,96},{96,80},{112,128},{128,112... | collective-permute-start | bytes 49160 | tf_op jit(solution)/shard_map/ppermute | solution.py:345
  11.3 4.0 %collective-permute-start.2 = (bf16[16,512]{1,0:T(8,128)(2,1)S(1)}, bf16[16,512]{1,0:T(8,128)(2,1)S(1)}, u32[]{:S(2)}, u32[]{:S(2)}) collective-permute-start(bf16[16,512]{1,0:T(8,128)(2,1)S(1)} %get-tuple-element.37), channel_id=1, source_target_pairs={{0,16},{16,0},{32,48},{48,32},{64,80},{80,64},{96,112},{112,96},{1... | collective-permute-start | bytes 49160 | tf_op jit(solution)/shard_map/ppermute | solution.py:346
  14.4 2.6 %collective-permute-start.3 = (bf16[16,512]{1,0:T(8,128)(2,1)S(1)}, bf16[16,512]{1,0:T(8,128)(2,1)S(1)}, u32[]{:S(2)}, u32[]{:S(2)}) collective-permute-start(bf16[16,512]{1,0:T(8,128)(2,1)S(1)} %get-tuple-element.38), channel_id=1, source_target_pairs={{0,1},{1,0},{2,3},{3,2},{4,5},{5,4},{6,7},{7,6},{8,9},{9,8},{10,11... | collective-permute-start | bytes 49160 | tf_op jit(solution)/shard_map/ppermute | solution.py:347
  25.1 4.7 %collective-permute-start.4 = (bf16[1792,512]{1,0:T(8,128)(2,1)S(1)}, bf16[1792,512]{1,0:T(8,128)(2,1)S(1)}, u32[]{:S(2)}, u32[]{:S(2)}) collective-permute-start(bf16[1792,512]{1,0:T(8,128)(2,1)S(1)} %get-tuple-element.41), channel_id=1, source_target_pairs={{0,16},{16,0},{1,17},{17,1},{2,18},{18,2},{3,19},{19,3},{4,20},{20... | collective-permute-start | bytes 5505032 | tf_op jit(solution)/shard_map/ppermute | solution.py:410
  59.1 23.2 %copy-start = (s32[1,1,4,16]{3,2,1,0:T(4,128)S(1)}, s32[1,1,4,16]{3,2,1,0:T(4,128)}, u32[]{:S(2)}) copy-start(s32[1,1,4,16]{3,2,1,0:T(4,128)} %lists.1) | copy-start | bytes 772
  70.2 12.1 %all-to-all-start.2 = ((bf16[8,56,128]{2,1,0:T(8,128)(2,1)}), bf16[8,56,128]{2,1,0:T(8,128)(2,1)S(1)}, u32[]{:S(2)}, u32[]{:S(2)}) async-start(bf16[8,56,128]{2,1,0:T(8,128)(2,1)} %shard_map.166), calls=%async_computation.2 | async-start | bytes 229376 | tf_op jit(solution)/shard_map/all_to_all | solution.py:424
  73.6 5.8 %collective-permute-start.5 = (bf16[16,512]{1,0:T(8,128)(2,1)S(1)}, bf16[16,512]{1,0:T(8,128)(2,1)S(1)}, u32[]{:S(2)}, u32[]{:S(2)}) collective-permute-start(bf16[16,512]{1,0:T(8,128)(2,1)S(1)} %get-tuple-element.48), channel_id=1, source_target_pairs={{1,2},{2,1},{3,4},{4,3},{5,6},{6,5},{7,8},{8,7},{9,10},{10,9},{11,... | collective-permute-start | bytes 49160 | tf_op jit(solution)/shard_map/ppermute | solution.py:344
  76.2 4.4 %collective-permute-start.6 = (bf16[16,512]{1,0:T(8,128)(2,1)S(1)}, bf16[16,512]{1,0:T(8,128)(2,1)S(1)}, u32[]{:S(2)}, u32[]{:S(2)}) collective-permute-start(bf16[16,512]{1,0:T(8,128)(2,1)S(1)} %get-tuple-element.49), channel_id=1, source_target_pairs={{16,32},{32,16},{48,64},{64,48},{80,96},{96,80},{112,128},{128,112... | collective-permute-start | bytes 49160 | tf_op jit(solution)/shard_map/ppermute | solution.py:345
  78.9 1.7 %collective-permute-start.7 = (bf16[16,512]{1,0:T(8,128)(2,1)S(1)}, bf16[16,512]{1,0:T(8,128)(2,1)S(1)}, u32[]{:S(2)}, u32[]{:S(2)}) collective-permute-start(bf16[16,512]{1,0:T(8,128)(2,1)S(1)} %get-tuple-element.50), channel_id=1, source_target_pairs={{0,16},{16,0},{32,48},{48,32},{64,80},{80,64},{96,112},{112,96},{1... | collective-permute-start | bytes 49160 | tf_op jit(solution)/shard_map/ppermute | solution.py:346
  79.4 2.9 %collective-permute-start.8 = (bf16[16,512]{1,0:T(8,128)(2,1)S(1)}, bf16[16,512]{1,0:T(8,128)(2,1)S(1)}, u32[]{:S(2)}, u32[]{:S(2)}) collective-permute-start(bf16[16,512]{1,0:T(8,128)(2,1)S(1)} %get-tuple-element.51), channel_id=1, source_target_pairs={{0,1},{1,0},{2,3},{3,2},{4,5},{5,4},{6,7},{7,6},{8,9},{9,8},{10,11... | collective-permute-start | bytes 49160 | tf_op jit(solution)/shard_map/ppermute | solution.py:347
  112.8 6.6 %collective-permute-start.9 = (bf16[1792,512]{1,0:T(8,128)(2,1)S(1)}, bf16[1792,512]{1,0:T(8,128)(2,1)S(1)}, u32[]{:S(2)}, u32[]{:S(2)}) collective-permute-start(bf16[1792,512]{1,0:T(8,128)(2,1)S(1)} %bitcast.2), channel_id=1, source_target_pairs={{0,16},{16,0},{1,17},{17,1},{2,18},{18,2},{3,19},{19,3},{4,20},{20... | collective-permute-start | bytes 5505032 | tf_op jit(solution)/shard_map/ppermute | solution.py:429

commit v4 on v3

v4 whole, which is shorter than its diff:
```python
import functools

import jax
import jax.numpy as jnp
from jax import lax
from jax.experimental import pallas as pl
from jax.experimental.pallas import tpu as pltpu
from jax.sharding import Mesh
from jax.sharding import PartitionSpec as P

BF = jnp.bfloat16
F32 = jnp.float32
GX = ("yh", "x", "c")
GY = ("yl", "z")
PLANE = ("yh", "x", "yl")
VMEM = pl.BlockSpec(memory_space=pltpu.VMEM)
ANY = pl.BlockSpec(memory_space=pl.ANY)


def dot(left, right):
    return jnp.dot(left, right, preferred_element_type=F32)


def dot_rows(left, right):
    return lax.dot_general(left, right, (((0,), (0,)), ((), ())), preferred_element_type=F32)


def dot_cols(left, right):
    return lax.dot_general(left, right, (((1,), (1,)), ((), ())), preferred_element_type=F32)


def hi_lo(values):
    high = values.astype(BF)
    low = (values - high.astype(F32)).astype(BF)
    return jnp.concatenate([high, low], axis=0)


def fold(values):
    half = values.shape[0] // 2
    return values[:half] + values[half:]


def layer_norm(values):
    mean = jnp.mean(values, axis=-1, keepdims=True)
    centred = values - mean
    scale = lax.rsqrt(jnp.mean(centred * centred, axis=-1, keepdims=True) + 1e-05)
    return centred * scale, scale


def norm_back(grad, normed, scale):
    first = jnp.mean(grad, axis=-1, keepdims=True)
    second = jnp.mean(grad * normed, axis=-1, keepdims=True)
    return scale * (grad - first - normed * second)


def silu_and_slope(values):
    sig = 1.0 / (1.0 + jnp.exp(-values))
    return values * sig, sig * (1.0 + values * (1.0 - sig))


def pick(row, count):
    rows = lax.broadcasted_iota(jnp.int32, (count, row.shape[-1]), 0)
    return jnp.where(rows == row, 1.0, 0.0)


def fetch(sources, targets, sems):
    copies = [
        pltpu.make_async_copy(source, target, sems.at[i])
        for i, (source, target) in enumerate(zip(sources, targets, strict=True))
    ]
    for copy in copies:
        copy.start()

    def ready(i):
        copies[i].wait()
        return targets[i]

    return ready


def parities():
    return lax.axis_index("c"), lax.rem(lax.axis_index("z"), 2)


def side_of(step, row_odd, col_odd):
    return (2 + col_odd, row_odd, 1 - row_odd, 3 - col_odd)[step]


def pack_kernel(nodes_hbm, lists_hbm, *refs):
    packs, (nodes, lists, sems) = refs[:4], refs[4:]
    ready = fetch((nodes_hbm.at[0, 0], lists_hbm.at[0, 0]), (nodes, lists), sems)
    odd = parities()
    ready(1)
    lat = ready(0)[...]
    for step in range(4):
        row = lists[pl.ds(side_of(step, *odd), 1), :]
        packs[step][...] = dot_rows(pick(row, lat.shape[0]).astype(BF), lat).astype(BF)


def load_kernel(
    packs,
    nodes_hbm,
    edges_hbm,
    senders_hbm,
    segments_hbm,
    cot_nodes_hbm,
    cot_edges_hbm,
    w_edge1_hbm,
    w_edge2_hbm,
    w_node1_hbm,
    w_node2_hbm,
    node,
    edge,
    cot_node,
    cot_edge,
    w_edge1,
    w_edge2,
    w_node1,
    w_node2,
    to_ext,
    to_node,
    from_node,
    from_halo,
    z_part,
    senders,
    segments,
    sems,
):
    del packs
    ready = fetch(
        (
            senders_hbm.at[0],
            segments_hbm.at[0],
            nodes_hbm.at[0, 0],
            w_edge1_hbm,
            edges_hbm.at[0, 0],
            w_edge2_hbm,
            w_node1_hbm,
            w_node2_hbm,
            cot_nodes_hbm.at[0, 0],
            cot_edges_hbm.at[0, 0],
        ),
        (
            senders,
            segments,
            node,
            w_edge1,
            edge,
            w_edge2,
            w_node1,
            w_node2,
            cot_node,
            cot_edge,
        ),
        sems,
    )
    count, width = node.shape
    by_send = pick(ready(0)[...], to_ext.shape[0])
    by_recv = pick(ready(1)[...], count)
    to_ext[...] = by_send.astype(BF)
    to_node[...] = by_recv.astype(BF)
    own = by_send[:count].T.astype(BF)
    halo = by_send[count:].T.astype(BF)
    recv = by_recv.T.astype(BF)
    from_halo[...] = jnp.concatenate([halo, halo], axis=1)
    from_node[...] = jnp.concatenate([recv, recv], axis=1)
    wide = jnp.concatenate([own, own, recv, recv], axis=1)
    lat = ready(2)[...]
    ready(3)
    terms = jnp.concatenate(
        [
            hi_lo(dot(lat, w_edge1[width : 2 * width, :])),
            hi_lo(dot(lat, w_edge1[2 * width :, :])),
        ],
        axis=0,
    )
    z_part[...] = dot(ready(4)[...], w_edge1[:width, :]) + dot(wide, terms)
    for i in range(5, 10):
        ready(i)


def put_half(target, side, pairs_of_block):
    for block, (left, right) in enumerate(pairs_of_block):
        part = left.shape[1] // 2
        columns = pl.ds(pl.multiple_of(side * part, part), part)
        target[block * part : (block + 1) * part, :] = dot_rows(
            left[:, columns], right[...]
        ).astype(BF)


def layer_kernel(
    halo0,
    halo1,
    halo2,
    halo3,
    node,
    edge,
    cot_node,
    cot_edge,
    w_edge1,
    w_edge2,
    w_node1,
    w_node2,
    to_ext,
    to_node,
    from_node,
    from_halo,
    z_part,
    node_next,
    send,
    ext_twice,
    node_twice,
    a_one,
    agg,
    a_three,
    dz_one,
    dz_two,
    dz_three,
    dz_four,
    sum_send,
    sum_recv,
    de_new,
    dn_part,
):
    odd = parities()
    count, width = node.shape
    rows = halo0.shape[0]
    reach = ext_twice.shape[0] // 2
    lat = node[...]
    for start in (0, reach):
        ext_twice[start : start + count, :] = lat
        for step, halo in enumerate((halo0, halo1, halo2, halo3)):
            place = start + count + side_of(step, *odd) * rows
            ext_twice[pl.ds(pl.multiple_of(place, rows), rows), :] = halo[...]
    for start in (0, count):
        node_twice[start : start + count, :] = lat

    terms = hi_lo(dot(ext_twice[count:reach, :], w_edge1[width : 2 * width, :]))
    z_one = z_part[...] + dot(from_halo[...], terms)
    act, slope_one = silu_and_slope(z_one)
    a_one[...] = act.astype(BF)
    n_two, s_two = layer_norm(dot(a_one[...], w_edge2[...]))
    e_new = (edge[...].astype(F32) + n_two).astype(BF)
    agg[...] = dot(to_node[...], e_new).astype(BF)
    z_three = dot(lat, w_node1[:width, :]) + dot(agg[...], w_node1[width:, :])
    act, slope_three = silu_and_slope(z_three)
    a_three[...] = act.astype(BF)
    n_four, s_four = layer_norm(dot(a_three[...], w_node2[...]))
    node_next[0, 0] = (lat.astype(F32) + n_four).astype(BF)

    g_node = cot_node[...].astype(F32)
    dz_four[...] = norm_back(g_node, n_four, s_four).astype(BF)
    dz_three[...] = (dot_cols(dz_four[...], w_node2[...]) * slope_three).astype(BF)
    dn_part[...] = g_node + dot_cols(dz_three[...], w_node1[:width, :])
    dy_agg = dot_cols(dz_three[...], w_node1[width:, :])

    de = cot_edge[...].astype(F32) + dot(from_node[...], hi_lo(dy_agg))
    de_new[...] = de
    dz_two[...] = norm_back(de, n_two, s_two).astype(BF)
    dz_one[...] = (dot_cols(dz_two[...], w_edge2[...]) * slope_one).astype(BF)
    sum_send[...] = hi_lo(dot(to_ext[...], dz_one[...]))
    sum_recv[...] = hi_lo(dot(to_node[...], dz_one[...]))
    put_half(
        send,
        1 - odd[0],
        (
            (edge, dz_one),
            (ext_twice, sum_send),
            (node_twice, sum_recv),
            (a_one, dz_two),
            (node, dz_three),
            (agg, dz_three),
            (a_three, dz_four),
        ),
    )


def rest_kernel(
    node,
    edge,
    w_edge1,
    ext_twice,
    node_twice,
    a_one,
    agg,
    a_three,
    dz_one,
    dz_two,
    dz_three,
    dz_four,
    sum_send,
    sum_recv,
    de_new,
    dn_part,
    keep,
    grad_edges,
    d_node,
    back0,
    back1,
    back2,
    back3,
    d_ext,
):
    odd = parities()
    count, width = node.shape
    rows = back0.shape[0]
    put_half(
        keep,
        odd[0],
        (
            (edge, dz_one),
            (ext_twice, sum_send),
            (node_twice, sum_recv),
            (a_one, dz_two),
            (node, dz_three),
            (agg, dz_three),
            (a_three, dz_four),
        ),
    )
    grad_edges[0, 0] = (de_new[...] + dot_cols(dz_one[...], w_edge1[:width, :])).astype(BF)
    d_ext[...] = fold(dot_cols(sum_send[...], w_edge1[width : 2 * width, :]))
    d_recv = fold(dot_cols(sum_recv[...], w_edge1[2 * width :, :]))
    d_node[...] = dn_part[...] + d_recv + d_ext[:count, :]
    for step, back in enumerate((back0, back1, back2, back3)):
        place = count + side_of(step, *odd) * rows
        back[...] = d_ext[pl.ds(pl.multiple_of(place, rows), rows), :].astype(BF)


def pair_sum_kernel(mine, other, out):
    out[...] = (mine[...].astype(F32) + other[...].astype(F32)).astype(BF)


def plane_sum_kernel(parts, *refs):
    backs, out, onward = refs[:4], refs[4], refs[5:]
    for back, ref in zip(backs, onward, strict=True):
        ref[...] = back[...]
    total = parts[0].astype(F32)
    for part in range(1, parts.shape[0]):
        total = total + parts[part].astype(F32)
    total = total.astype(BF)
    for part in range(out.shape[0]):
        out[part] = total


def line_sum_kernel(factor, parts, d_node, lists, ret0, ret1, ret2, ret3, out, grad_nodes):
    total = parts[0].astype(F32)
    for part in range(1, parts.shape[0]):
        total = total + parts[part].astype(F32)
    total = (total * factor).astype(BF)
    for part in range(out.shape[0]):
        out[part] = total
    odd = parities()
    grad = d_node[...]
    for step, ret in enumerate((ret0, ret1, ret2, ret3)):
        row = lists[0, 0, pl.ds(side_of(step, *odd), 1), :]
        grad = grad + dot(pick(row, grad.shape[0]).astype(BF), ret[...])
    grad_nodes[0, 0] = grad.astype(BF)


def place_kernel(other_core, half, *refs):
    outs, sems = refs[-5:-1], refs[-1]
    part = outs[0].shape[1] // 2
    side = lax.axis_index("c")
    side = 1 - side if other_core else side
    copies = []
    for out in outs:
        for block in range(out.shape[0] // (2 * part)):
            place = pl.multiple_of((2 * block + side) * part, part)
            start = len(copies) * part
            copies.append(
                pltpu.make_async_copy(
                    half.at[start : start + part], out.at[pl.ds(place, part)], sems.at[len(copies)]
                )
            )
    for copy in copies:
        copy.start()
    for copy in copies:
        copy.wait()


def call(kernel, outs, ins, limit=24, scratch=(), **kwargs):
    return pl.pallas_call(
        kernel,
        out_shape=outs,
        in_specs=ins,
        out_specs=jax.tree.map(lambda _: VMEM, outs),
        scratch_shapes=list(scratch),
        compiler_params=pltpu.CompilerParams(vmem_limit_bytes=limit << 20),
        **kwargs,
    )


def shape(dims, kind=BF):
    return jax.ShapeDtypeStruct(dims, kind)


def in_hbm(*arrays):
    return [pltpu.with_memory_space_constraint(array, pltpu.HBM) for array in arrays]


def pairs(count, first):
    made = []
    for i in range(first, count + first, 2):
        made += [(i, (i + 1) % count), ((i + 1) % count, i)]
    return made


def exchange(blocks):
    nx, ny = lax.axis_size(GX), lax.axis_size(GY)
    return [
        lax.ppermute(blocks[0], GY, pairs(ny, 1)),
        lax.ppermute(blocks[1], GX, pairs(nx, 1)),
        lax.ppermute(blocks[2], GX, pairs(nx, 0)),
        lax.ppermute(blocks[3], GY, pairs(ny, 0)),
    ]


def load(packs, nodes, edges, senders, segments, cot_nodes, cot_edges, weights):
    count, width = nodes.shape[2:]
    lines = edges.shape[2]
    reach = count + 4 * packs.shape[0]
    return call(
        load_kernel,
        [shape((count, width)), shape((lines, width))] * 2
        + [shape(w.shape) for w in weights]
        + [shape((reach, lines)), shape((count, lines))]
        + [shape((lines, 2 * count)), shape((lines, 2 * (reach - count)))]
        + [shape((lines, width), F32)],
        [VMEM] + [ANY] * 10,
        limit=12,
        scratch=[
            pltpu.VMEM((1, lines), jnp.int32),
            pltpu.VMEM((1, lines), jnp.int32),
            pltpu.SemaphoreType.DMA((10,)),
        ],
    )(packs, *in_hbm(nodes, edges, senders, segments, cot_nodes, cot_edges, *weights))


def layer(halos, loaded):
    node, edge, w_edge1 = loaded[0], loaded[1], loaded[4]
    (count, width), lines, rows = node.shape, edge.shape[0], halos[0].shape[0]
    reach = count + 4 * rows
    half = shape((sum(w.shape[0] for w in loaded[4:8]) // 2, width))
    on_edges, on_nodes = shape((lines, width)), shape((count, width))
    node_next, send, *state = call(
        layer_kernel,
        [shape((1, 1, count, width)), half]
        + [shape((2 * reach, width)), shape((2 * count, width)), on_edges, on_nodes, on_nodes]
        + [on_edges, on_edges, on_nodes, on_nodes]
        + [shape((2 * reach, width)), shape((2 * count, width))]
        + [shape((lines, width), F32), shape((count, width), F32)],
        [VMEM] * (4 + len(loaded)),
        limit=16,
    )(*halos, *loaded)
    keep, grad_edges, d_node, *backs = call(
        rest_kernel,
        [half, shape((1, 1, lines, width)), shape((count, width), F32)] + [shape((rows, width))] * 4,
        [VMEM] * (3 + len(state)),
        limit=12,
        scratch=[pltpu.VMEM((reach, width), F32)],
        cost_estimate=pl.CostEstimate(
            flops=2 * width * width * (4 * lines + 8 * reach),
            bytes_accessed=12 << 20,
            transcendentals=0,
        ),
    )(node, edge, w_edge1, *state)
    return node_next, send, keep, grad_edges, d_node, backs


def local(
    nodes,
    edges,
    senders,
    segments,
    send_lists,
    cot_nodes,
    cot_edges,
    w_edge1,
    w_edge2,
    w_node1,
    w_node2,
):
    count, width = nodes.shape[2:]
    lines = edges.shape[2]
    rows = send_lists.shape[3]
    weights = (w_edge1, w_edge2, w_node1, w_node2)
    total = sum(w.shape[0] for w in weights)
    block = [shape((rows, width))] * 4
    packs = call(
        pack_kernel,
        block,
        [ANY] * 2,
        scratch=[
            pltpu.VMEM((count, width), BF),
            pltpu.VMEM((4, rows), jnp.int32),
            pltpu.SemaphoreType.DMA((2,)),
        ],
    )(*in_hbm(nodes, send_lists))
    halos = exchange(packs)
    loaded = load(packs[0], nodes, edges, senders, segments, cot_nodes, cot_edges, weights)
    node_next, send, keep, grad_edges, d_node, backs = layer(halos, loaded)

    got = lax.ppermute(send, "c", pairs(2, 0))
    pair = call(pair_sum_kernel, shape(keep.shape), [VMEM] * 2, limit=8)(keep, got)

    plane, line = lax.axis_size(PLANE), lax.axis_size("z")
    strip = total // 2 // plane
    pieces = lax.all_to_all(pair, PLANE, 0, 0, tiled=True).reshape(plane, strip, width)
    pieces, *backs = call(
        plane_sum_kernel, [shape((line, strip, width))] + block, [VMEM] * 5, limit=8
    )(pieces, *backs)
    returned = exchange(backs)
    pieces = lax.all_to_all(pieces, "z", 0, 0, tiled=True)
    factor = float(lines * plane * line * 2) ** -0.5
    pieces, grad_nodes = call(
        functools.partial(line_sum_kernel, factor),
        [shape((plane, strip, width)), shape(nodes.shape)],
        [VMEM] * 7,
        limit=8,
    )(pieces, d_node, send_lists, *returned)
    mine = lax.all_to_all(pieces, PLANE, 0, 0, tiled=True).reshape(total // 2, width)
    other = lax.ppermute(mine, "c", pairs(2, 0))
    outs = [shape(w.shape) for w in weights]
    sems = [pltpu.SemaphoreType.DMA((total // width,))]
    grads = pl.pallas_call(
        functools.partial(place_kernel, False),
        out_shape=outs,
        in_specs=[VMEM],
        out_specs=[ANY] * 4,
        scratch_shapes=sems,
        compiler_params=pltpu.CompilerParams(vmem_limit_bytes=4 << 20),
    )(mine)
    grads = pl.pallas_call(
        functools.partial(place_kernel, True),
        out_shape=outs,
        in_specs=[VMEM] + [ANY] * 4,
        out_specs=[ANY] * 4,
        scratch_shapes=sems,
        compiler_params=pltpu.CompilerParams(vmem_limit_bytes=4 << 20),
        input_output_aliases={1: 0, 2: 1, 3: 2, 4: 3},
    )(other, *grads)
    return (node_next, grad_nodes, grad_edges, *grads)


def solution(mesh):
    fine = Mesh(mesh.devices.reshape(2, 4, 2, 2, 8), ("yh", "x", "c", "yl", "z"))
    tile = P(GX, GY)
    return jax.shard_map(
        local,
        mesh=fine,
        in_specs=(tile,) * 7 + (P(),) * 4,
        out_specs=(tile,) * 3 + (P(),) * 4,
        check_vma=False,
    )
```

time: 121 us -> 120 us (level)
  blocking collectives: 68.7 us -> 55.9 us
  waiting for transfers between devices: 11 us -> 23.2 us
    ppermute x2, waiting for transfers between devices: 0.01 us -> 13.1 us  [exchange(): lax.ppermute(blocks[0], GY, pairs(ny, 1))]
    all_to_all x1 -> x0, blocking collectives: 10.1 us -> none  [local(): pieces = lax.all_to_all(pieces, 'z', 0, 0, tiled=True)]
    all_to_all x1, waiting for transfers between devices: 0.01 us -> 5.33 us  [local(): pieces = lax.all_to_all(pieces, 'z', 0, 0, tiled=True)]
    ppermute x2, starting transfers between devices: 10.1 us -> 7.55 us  [exchange(): lax.ppermute(blocks[0], GY, pairs(ny, 1))]
    ppermute x2, waiting for transfers between devices: 3.41 us -> 1.06 us  [exchange(): lax.ppermute(blocks[3], GY, pairs(ny, 0))]
    ppermute x1, waiting for transfers between devices: 3.41 us -> 1.57 us  [local(): got = lax.ppermute(send, 'c', pairs(2, 0))]
    all_to_all x1, blocking collectives: 29.5 us -> 27.8 us  [local(): lax.all_to_all(pieces, PLANE, 0, 0, tiled=True).reshape(total // 2, width)]
    ppermute x2, starting transfers between devices: 0.01 us -> 1.64 us  [exchange(): lax.ppermute(blocks[3], GY, pairs(ny, 0))]
  transfers between devices with their start and end apart: 11 -> 11, of which waited for: 6 -> 5; matrix products, arithmetic and copies ran while one was open for 0% -> 0% of each run, Pallas kernels for 1% -> 5%
where the time goes in v4:
time: 120 us
  blocking collectives  55.9 us (47%)
  starting transfers between devices  25.6 us (21%)
  waiting for transfers between devices  23.2 us (19%)
  Pallas kernels  14.6 us (12%)
    all_to_all x1, blocking collectives, local(): lax.all_to_all(pair, PLANE, 0, 0, tiled=True).reshape(plane, strip, width)  28.1 us
    all_to_all x1, blocking collectives, local(): lax.all_to_all(pieces, PLANE, 0, 0, tiled=True).reshape(total // 2, width)  27.8 us
    ppermute x2, waiting for transfers between devices, exchange(): lax.ppermute(blocks[0], GY, pairs(ny, 1))  13.1 us
    ppermute x2, starting transfers between devices, exchange(): lax.ppermute(blocks[0], GY, pairs(ny, 1))  7.55 us
    all_to_all x1, waiting for transfers between devices, local(): pieces = lax.all_to_all(pieces, 'z', 0, 0, tiled=True)  5.33 us
    ppermute x2, starting transfers between devices, exchange(): lax.ppermute(blocks[1], GX, pairs(nx, 1))  4.79 us
    ppermute x2, starting transfers between devices, exchange(): lax.ppermute(blocks[2], GX, pairs(nx, 0))  4.23 us
    all_to_all x1, starting transfers between devices, local(): pieces = lax.all_to_all(pieces, 'z', 0, 0, tiled=True)  4.08 us
  transfers between devices with their start and end apart: 11, of which 5 were waited for; matrix products, arithmetic and copies ran while one was open for 0% of the time, Pallas kernels for 5%

profile of v4, /device:TPU:1, one launch (start us, length us, event | category | flops | bytes accessed | tf_op | source)
XLA Modules:
  0.0 119.9 jit_solution(13278305102535086386)
XLA Ops:
  0.6 1.1 shard_map.162
  1.7 2.7 %collective-permute-start.1 = (bf16[16,512]{1,0:T(8,128)(2,1)S(1)}, bf16[16,512]{1,0:T(8,128)(2,1)S(1)}, u32[]{:S(2)}, u32[]{:S(2)}) collective-permute-start(bf16[16,512]{1,0:T(8,128)(2,1)S(1)} %get-tuple-element.62), channel_id=1, source_target_pairs={{16,32},{32,16},{48,64},{64,48},{80,96},{96,80},{112,128},{128,112... | collective-permute-start | bytes 49160 | tf_op jit(solution)/shard_map/ppermute | solution.py:412
  4.4 3.7 %collective-permute-start.2 = (bf16[16,512]{1,0:T(8,128)(2,1)S(1)}, bf16[16,512]{1,0:T(8,128)(2,1)S(1)}, u32[]{:S(2)}, u32[]{:S(2)}) collective-permute-start(bf16[16,512]{1,0:T(8,128)(2,1)S(1)} %get-tuple-element.63), channel_id=1, source_target_pairs={{0,16},{16,0},{32,48},{48,32},{64,80},{80,64},{96,112},{112,96},{1... | collective-permute-start | bytes 49160 | tf_op jit(solution)/shard_map/ppermute | solution.py:413
  8.1 1.6 %collective-permute-start.3 = (bf16[16,512]{1,0:T(8,128)(2,1)S(1)}, bf16[16,512]{1,0:T(8,128)(2,1)S(1)}, u32[]{:S(2)}, u32[]{:S(2)}) collective-permute-start(bf16[16,512]{1,0:T(8,128)(2,1)S(1)} %get-tuple-element.64), channel_id=1, source_target_pairs={{0,1},{1,0},{2,3},{3,2},{4,5},{5,4},{6,7},{7,6},{8,9},{9,8},{10,11... | collective-permute-start | bytes 49160 | tf_op jit(solution)/shard_map/ppermute | solution.py:414
  9.8 4.8 %collective-permute-start = (bf16[16,512]{1,0:T(8,128)(2,1)S(1)}, bf16[16,512]{1,0:T(8,128)(2,1)S(1)}, u32[]{:S(2)}, u32[]{:S(2)}) collective-permute-start(bf16[16,512]{1,0:T(8,128)(2,1)S(1)} %get-tuple-element.61.packs), channel_id=1, source_target_pairs={{1,2},{2,1},{3,4},{4,3},{5,6},{6,5},{7,8},{8,7},{9,10},{10,9},{11,... | collective-permute-start | bytes 49160 | tf_op jit(solution)/shard_map/ppermute | solution.py:411
  14.5 2.4 %shard_map.163 = (bf16[64,512]{1,0:T(8,128)(2,1)S(1)}, bf16[384,512]{1,0:T(8,128)(2,1)S(1)}, bf16[64,512]{1,0:T(8,128)(2,1)S(1)}, bf16[384,512]{1,0:T(8,128)(2,1...) custom-call(bf16[16,512]{1,0:T(8,128)(2,1)S(1)} %get-tuple-element.6, ...), custom_call_target="tpu_custom_call" | custom-call | tf_op jit(solution)/shard_map/pallas_call | solution.py:422
  17.0 4.0 %shard_map.164 = (bf16[1,1,64,512]{3,2,1,0:T(8,128)(2,1)}, bf16[1792,512]{1,0:T(8,128)(2,1)S(1)}, bf16[256,512]{1,0:T(8,128)(2,1)S(1)}, bf16[128,512]{1,0:T(8,12...) custom-call(bf16[16,512]{1,0:T(8,128)(2,1)S(1)} %collective-permute-, ...), custom_call_target="tpu_custom_call" | custom-call | tf_op jit(solution)/shard_map/pallas_call | solution.py:445
  21.0 0.7 collective-permute-start.4
  21.7 1.8 %shard_map.165 = (bf16[1792,512]{1,0:T(8,128)(2,1)S(1)}, bf16[1,1,384,512]{3,2,1,0:T(8,128)(2,1)}, f32[64,512]{1,0:T(8,128)S(1)}, bf16[16,512]{1,0:T(8,128)(2,1)...) custom-call(bf16[64,512]{1,0:T(8,128)(2,1)S(1)} %get-tuple-element.65.node, ...), custom_call_target="tpu_custom_call" | custom-call | flops 1342177280 | bytes 12582912 | tf_op jit(solution)/shard_map/pallas_call | solution.py:455
  23.5 1.6 %collective-permute-done.4.other = bf16[1792,512]{1,0:T(8,128)(2,1)S(1)} collective-permute-done((bf16[1792,512]{1,0:T(8,128)(2,1)S(1)}, bf16[1792,512]{1,0:T(8,128)(2,1)S(1)}, u32[]{:S(2)}, u32[]{:S(2)}) %collective-permute-start.4) | collective-permute-done | bytes 1835040 | tf_op jit(solution)/shard_map/ppermute | solution.py:503
  25.5 28.1 %all_to_all.19.parts = bf16[16,112,512]{2,1,0:T(8,128)(2,1)S(1)} all-to-all(bf16[16,112,512]{2,1,0:T(8,128)(2,1)S(1)} %bitcast.4), channel_id=1, replica_groups=mesh['yh'=2,'x'=4,'c'=2,'yl'=2,'z'=8] {'yh','x','yl'}, dimensions={0} | all-to-all | bytes 3670016 | tf_op jit(solution)/shard_map/all_to_all | solution.py:508
  53.6 1.2 shard_map.167
  54.8 4.1 %all-to-all-start.1 = ((bf16[8,112,512]{2,1,0:T(8,128)(2,1)}), bf16[8,112,512]{2,1,0:T(8,128)(2,1)S(1)}, u32[]{:S(2)}, u32[]{:S(2)}) async-start(bf16[8,112,512]{2,1,0:T(8,128)(2,1)} %get-tuple-element.98), calls=%async_computation.1 | async-start | bytes 1835008 | tf_op jit(solution)/shard_map/all_to_all | solution.py:513
  58.9 2.8 %collective-permute-start.5 = (bf16[16,512]{1,0:T(8,128)(2,1)S(1)}, bf16[16,512]{1,0:T(8,128)(2,1)S(1)}, u32[]{:S(2)}, u32[]{:S(2)}) collective-permute-start(bf16[16,512]{1,0:T(8,128)(2,1)S(1)} %get-tuple-element.100), channel_id=1, source_target_pairs={{1,2},{2,1},{3,4},{4,3},{5,6},{6,5},{7,8},{8,7},{9,10},{10,9},{11,... | collective-permute-start | bytes 49160 | tf_op jit(solution)/shard_map/ppermute | solution.py:411
  61.7 2.1 %collective-permute-start.6 = (bf16[16,512]{1,0:T(8,128)(2,1)S(1)}, bf16[16,512]{1,0:T(8,128)(2,1)S(1)}, u32[]{:S(2)}, u32[]{:S(2)}) collective-permute-start(bf16[16,512]{1,0:T(8,128)(2,1)S(1)} %get-tuple-element.101), channel_id=1, source_target_pairs={{16,32},{32,16},{48,64},{64,48},{80,96},{96,80},{112,128},{128,112... | collective-permute-start | bytes 49160 | tf_op jit(solution)/shard_map/ppermute | solution.py:412
  64.3 13.1 %collective-permute-done.5.ret0 = bf16[16,512]{1,0:T(8,128)(2,1)S(1)} collective-permute-done((bf16[16,512]{1,0:T(8,128)(2,1)S(1)}, bf16[16,512]{1,0:T(8,128)(2,1)S(1)}, u32[]{:S(2)}, u32[]{:S(2)}) %collective-permute-start.5) | collective-permute-done | bytes 16416 | tf_op jit(solution)/shard_map/ppermute | solution.py:411
  77.3 1.1 collective-permute-done.8.ret3
  78.4 5.3 %all-to-all-done.1.parts = bf16[8,112,512]{2,1,0:T(8,128)(2,1)S(1)} async-done(((bf16[8,112,512]{2,1,0:T(8,128)(2,1)}), bf16[8,112,512]{2,1,0:T(8,128)(2,1)S(1)}, u32[]{:S(2)}, u32[]{:S(2)}) %all-to-all-start.1) | async-done | bytes 917536 | tf_op jit(solution)/shard_map/all_to_all | solution.py:513
  83.7 1.1 shard_map.168
  84.8 27.8 %all_to_all.20 = bf16[16,112,512]{2,1,0:T(8,128)(2,1)S(1)} all-to-all(bf16[16,112,512]{2,1,0:T(8,128)(2,1)S(1)} %get-tuple-element.106), channel_id=1, replica_groups=mesh['yh'=2,'x'=4,'c'=2,'yl'=2,'z'=8] {'yh','x','yl'}, dimensions={0} | all-to-all | bytes 3670016 | tf_op jit(solution)/shard_map/all_to_all | solution.py:521
  112.6 2.6 %collective-permute-start.9 = (bf16[1792,512]{1,0:T(8,128)(2,1)S(1)}, bf16[1792,512]{1,0:T(8,128)(2,1)S(1)}, u32[]{:S(2)}, u32[]{:S(2)}) collective-permute-start(bf16[1792,512]{1,0:T(8,128)(2,1)S(1)} %bitcast.2), channel_id=1, source_target_pairs={{0,16},{16,0},{1,17},{17,1},{2,18},{18,2},{3,19},{19,3},{4,20},{20... | collective-permute-start | bytes 5505032 | tf_op jit(solution)/shard_map/ppermute | solution.py:522
  115.3 1.3 %shard_map.169 = (bf16[1536,512]{1,0:T(8,128)(2,1)}, bf16[512,512]{1,0:T(8,128)(2,1)}, bf16[1024,512]{1,0:T(8,128)(2,1)}, bf16[512,512]{1,0:T(8,128)(2,1)}) custom-call(bf16[1792,512]{1,0:T(8,128)(2,1)S(1)} %bitcast.3), custom_call_target="tpu_custom_call" | custom-call | tf_op jit(solution)/shard_map/pallas_call | solution.py:525
  116.5 2.1 %collective-permute-done.9.half = bf16[1792,512]{1,0:T(8,128)(2,1)S(1)} collective-permute-done((bf16[1792,512]{1,0:T(8,128)(2,1)S(1)}, bf16[1792,512]{1,0:T(8,128)(2,1)S(1)}, u32[]{:S(2)}, u32[]{:S(2)}) %collective-permute-start.9) | collective-permute-done | bytes 1835040 | tf_op jit(solution)/shard_map/ppermute | solution.py:522
  118.7 1.3 %shard_map.170 = (bf16[1536,512]{1,0:T(8,128)(2,1)}, bf16[512,512]{1,0:T(8,128)(2,1)}, bf16[1024,512]{1,0:T(8,128)(2,1)}, bf16[512,512]{1,0:T(8,128)(2,1)}) custom-call(bf16[1792,512]{1,0:T(8,128)(2,1)S(1)} %collective-permute-done.9.half, ...), custom_call_target="tpu_custom_call", output_to_operand_aliasing={{0}: (1, {}), {1}: (2, {}), {2}: (3, {}), {3}: (4, {})} | custom-call | tf_op jit(solution)/shard_map/pallas_call | solution.py:533
  (11 shorter events, 0.9 us)
Async XLA Ops:
  1.7 15.2 %collective-permute-start.1 = (bf16[16,512]{1,0:T(8,128)(2,1)S(1)}, bf16[16,512]{1,0:T(8,128)(2,1)S(1)}, u32[]{:S(2)}, u32[]{:S(2)}) collective-permute-start(bf16[16,512]{1,0:T(8,128)(2,1)S(1)} %get-tuple-element.62), channel_id=1, source_target_pairs={{16,32},{32,16},{48,64},{64,48},{80,96},{96,80},{112,128},{128,112... | collective-permute-start | bytes 49160 | tf_op jit(solution)/shard_map/ppermute | solution.py:412
  4.4 12.6 %collective-permute-start.2 = (bf16[16,512]{1,0:T(8,128)(2,1)S(1)}, bf16[16,512]{1,0:T(8,128)(2,1)S(1)}, u32[]{:S(2)}, u32[]{:S(2)}) collective-permute-start(bf16[16,512]{1,0:T(8,128)(2,1)S(1)} %get-tuple-element.63), channel_id=1, source_target_pairs={{0,16},{16,0},{32,48},{48,32},{64,80},{80,64},{96,112},{112,96},{1... | collective-permute-start | bytes 49160 | tf_op jit(solution)/shard_map/ppermute | solution.py:413
  8.1 8.8 %collective-permute-start.3 = (bf16[16,512]{1,0:T(8,128)(2,1)S(1)}, bf16[16,512]{1,0:T(8,128)(2,1)S(1)}, u32[]{:S(2)}, u32[]{:S(2)}) collective-permute-start(bf16[16,512]{1,0:T(8,128)(2,1)S(1)} %get-tuple-element.64), channel_id=1, source_target_pairs={{0,1},{1,0},{2,3},{3,2},{4,5},{5,4},{6,7},{7,6},{8,9},{9,8},{10,11... | collective-permute-start | bytes 49160 | tf_op jit(solution)/shard_map/ppermute | solution.py:414
  9.8 7.2 %collective-permute-start = (bf16[16,512]{1,0:T(8,128)(2,1)S(1)}, bf16[16,512]{1,0:T(8,128)(2,1)S(1)}, u32[]{:S(2)}, u32[]{:S(2)}) collective-permute-start(bf16[16,512]{1,0:T(8,128)(2,1)S(1)} %get-tuple-element.61.packs), channel_id=1, source_target_pairs={{1,2},{2,1},{3,4},{4,3},{5,6},{6,5},{7,8},{8,7},{9,10},{10,9},{11,... | collective-permute-start | bytes 49160 | tf_op jit(solution)/shard_map/ppermute | solution.py:411
  21.0 4.1 %collective-permute-start.4 = (bf16[1792,512]{1,0:T(8,128)(2,1)S(1)}, bf16[1792,512]{1,0:T(8,128)(2,1)S(1)}, u32[]{:S(2)}, u32[]{:S(2)}) collective-permute-start(bf16[1792,512]{1,0:T(8,128)(2,1)S(1)} %get-tuple-element.93), channel_id=1, source_target_pairs={{0,16},{16,0},{1,17},{17,1},{2,18},{18,2},{3,19},{19,3},{4,20},{20... | collective-permute-start | bytes 5505032 | tf_op jit(solution)/shard_map/ppermute | solution.py:503
  53.6 30.1 %copy-start = (s32[1,1,4,16]{3,2,1,0:T(4,128)S(1)}, s32[1,1,4,16]{3,2,1,0:T(4,128)}, u32[]{:S(2)}) copy-start(s32[1,1,4,16]{3,2,1,0:T(4,128)} %lists.1) | copy-start | bytes 772
  54.8 28.9 %all-to-all-start.1 = ((bf16[8,112,512]{2,1,0:T(8,128)(2,1)}), bf16[8,112,512]{2,1,0:T(8,128)(2,1)S(1)}, u32[]{:S(2)}, u32[]{:S(2)}) async-start(bf16[8,112,512]{2,1,0:T(8,128)(2,1)} %get-tuple-element.98), calls=%async_computation.1 | async-start | bytes 1835008 | tf_op jit(solution)/shard_map/all_to_all | solution.py:513
  58.9 18.4 %collective-permute-start.5 = (bf16[16,512]{1,0:T(8,128)(2,1)S(1)}, bf16[16,512]{1,0:T(8,128)(2,1)S(1)}, u32[]{:S(2)}, u32[]{:S(2)}) collective-permute-start(bf16[16,512]{1,0:T(8,128)(2,1)S(1)} %get-tuple-element.100), channel_id=1, source_target_pairs={{1,2},{2,1},{3,4},{4,3},{5,6},{6,5},{7,8},{8,7},{9,10},{10,9},{11,... | collective-permute-start | bytes 49160 | tf_op jit(solution)/shard_map/ppermute | solution.py:411
  61.7 15.7 %collective-permute-start.6 = (bf16[16,512]{1,0:T(8,128)(2,1)S(1)}, bf16[16,512]{1,0:T(8,128)(2,1)S(1)}, u32[]{:S(2)}, u32[]{:S(2)}) collective-permute-start(bf16[16,512]{1,0:T(8,128)(2,1)S(1)} %get-tuple-element.101), channel_id=1, source_target_pairs={{16,32},{32,16},{48,64},{64,48},{80,96},{96,80},{112,128},{128,112... | collective-permute-start | bytes 49160 | tf_op jit(solution)/shard_map/ppermute | solution.py:412
  63.8 13.6 %collective-permute-start.7 = (bf16[16,512]{1,0:T(8,128)(2,1)S(1)}, bf16[16,512]{1,0:T(8,128)(2,1)S(1)}, u32[]{:S(2)}, u32[]{:S(2)}) collective-permute-start(bf16[16,512]{1,0:T(8,128)(2,1)S(1)} %get-tuple-element.102), channel_id=1, source_target_pairs={{0,16},{16,0},{32,48},{48,32},{64,80},{80,64},{96,112},{112,96},{1... | collective-permute-start | bytes 49160 | tf_op jit(solution)/shard_map/ppermute | solution.py:413
  64.3 14.1 %collective-permute-start.8 = (bf16[16,512]{1,0:T(8,128)(2,1)S(1)}, bf16[16,512]{1,0:T(8,128)(2,1)S(1)}, u32[]{:S(2)}, u32[]{:S(2)}) collective-permute-start(bf16[16,512]{1,0:T(8,128)(2,1)S(1)} %get-tuple-element.103), channel_id=1, source_target_pairs={{0,1},{1,0},{2,3},{3,2},{4,5},{5,4},{6,7},{7,6},{8,9},{9,8},{10,11... | collective-permute-start | bytes 49160 | tf_op jit(solution)/shard_map/ppermute | solution.py:414
  112.6 6.1 %collective-permute-start.9 = (bf16[1792,512]{1,0:T(8,128)(2,1)S(1)}, bf16[1792,512]{1,0:T(8,128)(2,1)S(1)}, u32[]{:S(2)}, u32[]{:S(2)}) collective-permute-start(bf16[1792,512]{1,0:T(8,128)(2,1)S(1)} %bitcast.2), channel_id=1, source_target_pairs={{0,16},{16,0},{1,17},{17,1},{2,18},{18,2},{3,19},{19,3},{4,20},{20... | collective-permute-start | bytes 5505032 | tf_op jit(solution)/shard_map/ppermute | solution.py:522

commit v5 on v4

--- a/solution.py
+++ b/solution.py
@@ -11,8 +11,9 @@
 BF = jnp.bfloat16
 F32 = jnp.float32
 GX = ("yh", "x", "c")
-GY = ("yl", "z")
-PLANE = ("yh", "x", "yl")
+GY = ("yl", "zh", "zl")
+NEAR = ("yh", "x", "yl", "zl")
+FAR = "zh"
 VMEM = pl.BlockSpec(memory_space=pltpu.VMEM)
 ANY = pl.BlockSpec(memory_space=pl.ANY)
 
@@ -79,7 +80,7 @@
 
 
 def parities():
-    return lax.axis_index("c"), lax.rem(lax.axis_index("z"), 2)
+    return lax.axis_index("c"), lax.axis_index("zl")
 
 
 def side_of(step, row_odd, col_odd):
@@ -330,7 +331,7 @@
     out[...] = (mine[...].astype(F32) + other[...].astype(F32)).astype(BF)
 
 
-def plane_sum_kernel(parts, *refs):
+def near_sum_kernel(parts, *refs):
     backs, out, onward = refs[:4], refs[4], refs[5:]
     for back, ref in zip(backs, onward, strict=True):
         ref[...] = back[...]
@@ -342,7 +343,7 @@
         out[part] = total
 
 
-def line_sum_kernel(factor, parts, d_node, lists, ret0, ret1, ret2, ret3, out, grad_nodes):
+def far_sum_kernel(factor, parts, d_node, lists, ret0, ret1, ret2, ret3, out, grad_nodes):
     total = parts[0].astype(F32)
     for part in range(1, parts.shape[0]):
         total = total + parts[part].astype(F32)
@@ -503,22 +504,22 @@
     got = lax.ppermute(send, "c", pairs(2, 0))
     pair = call(pair_sum_kernel, shape(keep.shape), [VMEM] * 2, limit=8)(keep, got)
 
-    plane, line = lax.axis_size(PLANE), lax.axis_size("z")
-    strip = total // 2 // plane
-    pieces = lax.all_to_all(pair, PLANE, 0, 0, tiled=True).reshape(plane, strip, width)
+    near, far = lax.axis_size(NEAR), lax.axis_size(FAR)
+    strip = total // 2 // near
+    pieces = lax.all_to_all(pair, NEAR, 0, 0, tiled=True).reshape(near, strip, width)
     pieces, *backs = call(
-        plane_sum_kernel, [shape((line, strip, width))] + block, [VMEM] * 5, limit=8
+        near_sum_kernel, [shape((far, strip, width))] + block, [VMEM] * 5, limit=8
     )(pieces, *backs)
     returned = exchange(backs)
-    pieces = lax.all_to_all(pieces, "z", 0, 0, tiled=True)
-    factor = float(lines * plane * line * 2) ** -0.5
+    pieces = lax.all_to_all(pieces, FAR, 0, 0, tiled=True)
+    factor = float(lines * near * far * 2) ** -0.5
     pieces, grad_nodes = call(
-        functools.partial(line_sum_kernel, factor),
-        [shape((plane, strip, width)), shape(nodes.shape)],
+        functools.partial(far_sum_kernel, factor),
+        [shape((near, strip, width)), shape(nodes.shape)],
         [VMEM] * 7,
         limit=8,
     )(pieces, d_node, send_lists, *returned)
-    mine = lax.all_to_all(pieces, PLANE, 0, 0, tiled=True).reshape(total // 2, width)
+    mine = lax.all_to_all(pieces, NEAR, 0, 0, tiled=True).reshape(total // 2, width)
     other = lax.ppermute(mine, "c", pairs(2, 0))
     outs = [shape(w.shape) for w in weights]
     sems = [pltpu.SemaphoreType.DMA((total // width,))]
@@ -543,7 +544,7 @@
 
 
 def solution(mesh):
-    fine = Mesh(mesh.devices.reshape(2, 4, 2, 2, 8), ("yh", "x", "c", "yl", "z"))
+    fine = Mesh(mesh.devices.reshape(2, 4, 2, 2, 4, 2), ("yh", "x", "c", "yl", "zh", "zl"))
     tile = P(GX, GY)
     return jax.shard_map(
         local,

time: 120 us -> 109 us (0.908)
  waiting for transfers between devices: 23.2 us -> 6.75 us
  blocking collectives: 55.9 us -> 60.3 us
    ppermute x2, waiting for transfers between devices: 13.1 us -> 0.01 us  [exchange(): lax.ppermute(blocks[0], GY, pairs(ny, 1))]
    all_to_all x1, waiting for transfers between devices: 5.33 us -> 0.01 us  [local(): pieces = lax.all_to_all(pieces, FAR, 0, 0, tiled=True)]
    all_to_all x2, blocking collectives: 55.9 us -> 60.3 us  [the longest x1 30.6 us: local(): lax.all_to_all(pieces, NEAR, 0, 0, tiled=True).reshape(total // 2, width)]
    ppermute x2, starting transfers between devices: 4.79 us -> 6.82 us  [exchange(): lax.ppermute(blocks[1], GX, pairs(nx, 1))]
    ppermute x2, waiting for transfers between devices: 0.01 us -> 1.71 us  [exchange(): lax.ppermute(blocks[1], GX, pairs(nx, 1))]
    ppermute x2, starting transfers between devices: 7.55 us -> 6.21 us  [exchange(): lax.ppermute(blocks[0], GY, pairs(ny, 1))]
  transfers between devices with their start and end apart: 11 -> 11, of which waited for: 5 -> 4; matrix products, arithmetic and copies ran while one was open for 0% -> 0% of each run, Pallas kernels for 5% -> 5%
where the time goes in v5:
time: 109 us; the launch traced here: 108 us
  blocking collectives  60.3 us (55%)
  starting transfers between devices  26.5 us (24%)
  Pallas kernels  14.2 us (13%)
  waiting for transfers between devices  6.75 us (6%)
    all_to_all x1, blocking collectives, local(): lax.all_to_all(pieces, NEAR, 0, 0, tiled=True).reshape(total // 2, width)  30.6 us
    all_to_all x1, blocking collectives, local(): lax.all_to_all(pair, NEAR, 0, 0, tiled=True).reshape(near, strip, width)  29.7 us
    ppermute x2, starting transfers between devices, exchange(): lax.ppermute(blocks[1], GX, pairs(nx, 1))  6.82 us
    ppermute x2, starting transfers between devices, exchange(): lax.ppermute(blocks[0], GY, pairs(ny, 1))  6.21 us
    all_to_all x1, starting transfers between devices, local(): pieces = lax.all_to_all(pieces, FAR, 0, 0, tiled=True)  4.53 us
    pallas_call x1, Pallas kernels, layer(): call(layer_kernel, [shape((1, 1, count, width)), half] + [shape((2 * reac...  4.01 us
    ppermute x2, starting transfers between devices, exchange(): lax.ppermute(blocks[2], GX, pairs(nx, 0))  3.74 us
    ppermute x1, starting transfers between devices, local(): other = lax.ppermute(mine, 'c', pairs(2, 0))  2.86 us
  transfers between devices with their start and end apart: 11, of which 4 were waited for; matrix products, arithmetic and copies ran while one was open for 0% of the time, Pallas kernels for 5%

profile of v5, /device:TPU:1, one launch (start us, length us, event | category | flops | bytes accessed | tf_op | source)
XLA Modules:
  0.0 108.4 jit_solution(12088741626172481003)
XLA Ops:
  0.6 1.1 shard_map.162
  1.7 2.7 %collective-permute-start.1 = (bf16[16,512]{1,0:T(8,128)(2,1)S(1)}, bf16[16,512]{1,0:T(8,128)(2,1)S(1)}, u32[]{:S(2)}, u32[]{:S(2)}) collective-permute-start(bf16[16,512]{1,0:T(8,128)(2,1)S(1)} %get-tuple-element.62), channel_id=1, source_target_pairs={{16,32},{32,16},{48,64},{64,48},{80,96},{96,80},{112,128},{128,112... | collective-permute-start | bytes 49160 | tf_op jit(solution)/shard_map/ppermute | solution.py:413
  4.4 3.7 %collective-permute-start.2 = (bf16[16,512]{1,0:T(8,128)(2,1)S(1)}, bf16[16,512]{1,0:T(8,128)(2,1)S(1)}, u32[]{:S(2)}, u32[]{:S(2)}) collective-permute-start(bf16[16,512]{1,0:T(8,128)(2,1)S(1)} %get-tuple-element.63), channel_id=1, source_target_pairs={{0,16},{16,0},{32,48},{48,32},{64,80},{80,64},{96,112},{112,96},{1... | collective-permute-start | bytes 49160 | tf_op jit(solution)/shard_map/ppermute | solution.py:414
  8.1 1.6 %collective-permute-start.3 = (bf16[16,512]{1,0:T(8,128)(2,1)S(1)}, bf16[16,512]{1,0:T(8,128)(2,1)S(1)}, u32[]{:S(2)}, u32[]{:S(2)}) collective-permute-start(bf16[16,512]{1,0:T(8,128)(2,1)S(1)} %get-tuple-element.64), channel_id=1, source_target_pairs={{0,1},{1,0},{2,3},{3,2},{4,5},{5,4},{6,7},{7,6},{8,9},{9,8},{10,11... | collective-permute-start | bytes 49160 | tf_op jit(solution)/shard_map/ppermute | solution.py:415
  9.8 4.8 %collective-permute-start = (bf16[16,512]{1,0:T(8,128)(2,1)S(1)}, bf16[16,512]{1,0:T(8,128)(2,1)S(1)}, u32[]{:S(2)}, u32[]{:S(2)}) collective-permute-start(bf16[16,512]{1,0:T(8,128)(2,1)S(1)} %get-tuple-element.61.packs), channel_id=1, source_target_pairs={{1,2},{2,1},{3,4},{4,3},{5,6},{6,5},{7,8},{8,7},{9,10},{10,9},{11,... | collective-permute-start | bytes 49160 | tf_op jit(solution)/shard_map/ppermute | solution.py:412
  14.5 2.4 %shard_map.163 = (bf16[64,512]{1,0:T(8,128)(2,1)S(1)}, bf16[384,512]{1,0:T(8,128)(2,1)S(1)}, bf16[64,512]{1,0:T(8,128)(2,1)S(1)}, bf16[384,512]{1,0:T(8,128)(2,1...) custom-call(bf16[16,512]{1,0:T(8,128)(2,1)S(1)} %get-tuple-element.6, ...), custom_call_target="tpu_custom_call" | custom-call | tf_op jit(solution)/shard_map/pallas_call | solution.py:423
  17.0 4.0 %shard_map.164 = (bf16[1,1,64,512]{3,2,1,0:T(8,128)(2,1)}, bf16[1792,512]{1,0:T(8,128)(2,1)S(1)}, bf16[256,512]{1,0:T(8,128)(2,1)S(1)}, bf16[128,512]{1,0:T(8,12...) custom-call(bf16[16,512]{1,0:T(8,128)(2,1)S(1)} %collective-permute-, ...), custom_call_target="tpu_custom_call" | custom-call | tf_op jit(solution)/shard_map/pallas_call | solution.py:446
  21.0 0.7 collective-permute-start.4
  21.7 1.8 %shard_map.165 = (bf16[1792,512]{1,0:T(8,128)(2,1)S(1)}, bf16[1,1,384,512]{3,2,1,0:T(8,128)(2,1)}, f32[64,512]{1,0:T(8,128)S(1)}, bf16[16,512]{1,0:T(8,128)(2,1)...) custom-call(bf16[64,512]{1,0:T(8,128)(2,1)S(1)} %get-tuple-element.65.node, ...), custom_call_target="tpu_custom_call" | custom-call | flops 1342177280 | bytes 12582912 | tf_op jit(solution)/shard_map/pallas_call | solution.py:456
  23.5 1.6 %collective-permute-done.4.other = bf16[1792,512]{1,0:T(8,128)(2,1)S(1)} collective-permute-done((bf16[1792,512]{1,0:T(8,128)(2,1)S(1)}, bf16[1792,512]{1,0:T(8,128)(2,1)S(1)}, u32[]{:S(2)}, u32[]{:S(2)}) %collective-permute-start.4) | collective-permute-done | bytes 1835040 | tf_op jit(solution)/shard_map/ppermute | solution.py:504
  25.1 0.4 shard_map.166
  25.5 29.7 %all_to_all.19.parts = bf16[32,56,512]{2,1,0:T(8,128)(2,1)S(1)} all-to-all(bf16[32,56,512]{2,1,0:T(8,128)(2,1)S(1)} %bitcast.4), channel_id=1, replica_groups=mesh['yh'=2,'x'=4,'c'=2,'yl'=2,'zh'=4,'zl'=2] {'yh','x','yl','zl'}, dimensions={0} | all-to-all | bytes 3670016 | tf_op jit(solution)/shard_map/all_to_all | solution.py:509
  55.2 0.9 shard_map.167
  56.1 4.5 %all-to-all-start.1 = ((bf16[4,56,512]{2,1,0:T(8,128)(2,1)}), bf16[4,56,512]{2,1,0:T(8,128)(2,1)S(1)}, u32[]{:S(2)}, u32[]{:S(2)}) async-start(bf16[4,56,512]{2,1,0:T(8,128)(2,1)} %get-tuple-element.98), calls=%async_computation.1 | async-start | bytes 458752 | tf_op jit(solution)/shard_map/all_to_all | solution.py:514
  60.7 1.4 %collective-permute-start.5 = (bf16[16,512]{1,0:T(8,128)(2,1)S(1)}, bf16[16,512]{1,0:T(8,128)(2,1)S(1)}, u32[]{:S(2)}, u32[]{:S(2)}) collective-permute-start(bf16[16,512]{1,0:T(8,128)(2,1)S(1)} %get-tuple-element.100), channel_id=1, source_target_pairs={{1,2},{2,1},{3,4},{4,3},{5,6},{6,5},{7,8},{8,7},{9,10},{10,9},{11,... | collective-permute-start | bytes 49160 | tf_op jit(solution)/shard_map/ppermute | solution.py:412
  62.1 4.1 %collective-permute-start.6 = (bf16[16,512]{1,0:T(8,128)(2,1)S(1)}, bf16[16,512]{1,0:T(8,128)(2,1)S(1)}, u32[]{:S(2)}, u32[]{:S(2)}) collective-permute-start(bf16[16,512]{1,0:T(8,128)(2,1)S(1)} %get-tuple-element.101), channel_id=1, source_target_pairs={{16,32},{32,16},{48,64},{64,48},{80,96},{96,80},{112,128},{128,112... | collective-permute-start | bytes 49160 | tf_op jit(solution)/shard_map/ppermute | solution.py:413
  66.2 1.7 %collective-permute-done.6.ret1 = bf16[16,512]{1,0:T(8,128)(2,1)S(1)} collective-permute-done((bf16[16,512]{1,0:T(8,128)(2,1)S(1)}, bf16[16,512]{1,0:T(8,128)(2,1)S(1)}, u32[]{:S(2)}, u32[]{:S(2)}) %collective-permute-start.6) | collective-permute-done | bytes 16416 | tf_op jit(solution)/shard_map/ppermute | solution.py:413
  67.9 1.3 %collective-permute-done.8.ret3 = bf16[16,512]{1,0:T(8,128)(2,1)S(1)} collective-permute-done((bf16[16,512]{1,0:T(8,128)(2,1)S(1)}, bf16[16,512]{1,0:T(8,128)(2,1)S(1)}, u32[]{:S(2)}, u32[]{:S(2)}) %collective-permute-start.8) | collective-permute-done | bytes 16416 | tf_op jit(solution)/shard_map/ppermute | solution.py:415
  69.3 1.0 shard_map.168
  70.3 30.6 %all_to_all.20 = bf16[32,56,512]{2,1,0:T(8,128)(2,1)S(1)} all-to-all(bf16[32,56,512]{2,1,0:T(8,128)(2,1)S(1)} %get-tuple-element.106), channel_id=1, replica_groups=mesh['yh'=2,'x'=4,'c'=2,'yl'=2,'zh'=4,'zl'=2] {'yh','x','yl','zl'}, dimensions={0} | all-to-all | bytes 3670016 | tf_op jit(solution)/shard_map/all_to_all | solution.py:522
  100.9 2.9 %collective-permute-start.9 = (bf16[1792,512]{1,0:T(8,128)(2,1)S(1)}, bf16[1792,512]{1,0:T(8,128)(2,1)S(1)}, u32[]{:S(2)}, u32[]{:S(2)}) collective-permute-start(bf16[1792,512]{1,0:T(8,128)(2,1)S(1)} %bitcast.2), channel_id=1, source_target_pairs={{0,16},{16,0},{1,17},{17,1},{2,18},{18,2},{3,19},{19,3},{4,20},{20... | collective-permute-start | bytes 5505032 | tf_op jit(solution)/shard_map/ppermute | solution.py:523
  103.7 1.3 %shard_map.169 = (bf16[1536,512]{1,0:T(8,128)(2,1)}, bf16[512,512]{1,0:T(8,128)(2,1)}, bf16[1024,512]{1,0:T(8,128)(2,1)}, bf16[512,512]{1,0:T(8,128)(2,1)}) custom-call(bf16[1792,512]{1,0:T(8,128)(2,1)S(1)} %bitcast.3), custom_call_target="tpu_custom_call" | custom-call | tf_op jit(solution)/shard_map/pallas_call | solution.py:526
  105.0 2.1 %collective-permute-done.9.half = bf16[1792,512]{1,0:T(8,128)(2,1)S(1)} collective-permute-done((bf16[1792,512]{1,0:T(8,128)(2,1)S(1)}, bf16[1792,512]{1,0:T(8,128)(2,1)S(1)}, u32[]{:S(2)}, u32[]{:S(2)}) %collective-permute-start.9) | collective-permute-done | bytes 1835040 | tf_op jit(solution)/shard_map/ppermute | solution.py:523
  107.1 1.3 %shard_map.170 = (bf16[1536,512]{1,0:T(8,128)(2,1)}, bf16[512,512]{1,0:T(8,128)(2,1)}, bf16[1024,512]{1,0:T(8,128)(2,1)}, bf16[512,512]{1,0:T(8,128)(2,1)}) custom-call(bf16[1792,512]{1,0:T(8,128)(2,1)S(1)} %collective-permute-done.9.half, ...), custom_call_target="tpu_custom_call", output_to_operand_aliasing={{0}: (1, {}), {1}: (2, {}), {2}: (3, {}), {3}: (4, {})} | custom-call | tf_op jit(solution)/shard_map/pallas_call | solution.py:534
  (11 shorter events, 0.0 us)
Async XLA Ops:
  1.7 15.2 %collective-permute-start.1 = (bf16[16,512]{1,0:T(8,128)(2,1)S(1)}, bf16[16,512]{1,0:T(8,128)(2,1)S(1)}, u32[]{:S(2)}, u32[]{:S(2)}) collective-permute-start(bf16[16,512]{1,0:T(8,128)(2,1)S(1)} %get-tuple-element.62), channel_id=1, source_target_pairs={{16,32},{32,16},{48,64},{64,48},{80,96},{96,80},{112,128},{128,112... | collective-permute-start | bytes 49160 | tf_op jit(solution)/shard_map/ppermute | solution.py:413
  4.4 12.6 %collective-permute-start.2 = (bf16[16,512]{1,0:T(8,128)(2,1)S(1)}, bf16[16,512]{1,0:T(8,128)(2,1)S(1)}, u32[]{:S(2)}, u32[]{:S(2)}) collective-permute-start(bf16[16,512]{1,0:T(8,128)(2,1)S(1)} %get-tuple-element.63), channel_id=1, source_target_pairs={{0,16},{16,0},{32,48},{48,32},{64,80},{80,64},{96,112},{112,96},{1... | collective-permute-start | bytes 49160 | tf_op jit(solution)/shard_map/ppermute | solution.py:414
  8.1 8.8 %collective-permute-start.3 = (bf16[16,512]{1,0:T(8,128)(2,1)S(1)}, bf16[16,512]{1,0:T(8,128)(2,1)S(1)}, u32[]{:S(2)}, u32[]{:S(2)}) collective-permute-start(bf16[16,512]{1,0:T(8,128)(2,1)S(1)} %get-tuple-element.64), channel_id=1, source_target_pairs={{0,1},{1,0},{2,3},{3,2},{4,5},{5,4},{6,7},{7,6},{8,9},{9,8},{10,11... | collective-permute-start | bytes 49160 | tf_op jit(solution)/shard_map/ppermute | solution.py:415
  9.8 7.2 %collective-permute-start = (bf16[16,512]{1,0:T(8,128)(2,1)S(1)}, bf16[16,512]{1,0:T(8,128)(2,1)S(1)}, u32[]{:S(2)}, u32[]{:S(2)}) collective-permute-start(bf16[16,512]{1,0:T(8,128)(2,1)S(1)} %get-tuple-element.61.packs), channel_id=1, source_target_pairs={{1,2},{2,1},{3,4},{4,3},{5,6},{6,5},{7,8},{8,7},{9,10},{10,9},{11,... | collective-permute-start | bytes 49160 | tf_op jit(solution)/shard_map/ppermute | solution.py:412
  21.0 4.1 %collective-permute-start.4 = (bf16[1792,512]{1,0:T(8,128)(2,1)S(1)}, bf16[1792,512]{1,0:T(8,128)(2,1)S(1)}, u32[]{:S(2)}, u32[]{:S(2)}) collective-permute-start(bf16[1792,512]{1,0:T(8,128)(2,1)S(1)} %get-tuple-element.93), channel_id=1, source_target_pairs={{0,16},{16,0},{1,17},{17,1},{2,18},{18,2},{3,19},{19,3},{4,20},{20... | collective-permute-start | bytes 5505032 | tf_op jit(solution)/shard_map/ppermute | solution.py:504
  55.2 14.1 %copy-start = (s32[1,1,4,16]{3,2,1,0:T(4,128)S(1)}, s32[1,1,4,16]{3,2,1,0:T(4,128)}, u32[]{:S(2)}) copy-start(s32[1,1,4,16]{3,2,1,0:T(4,128)} %lists.1) | copy-start | bytes 772
  56.1 13.2 %all-to-all-start.1 = ((bf16[4,56,512]{2,1,0:T(8,128)(2,1)}), bf16[4,56,512]{2,1,0:T(8,128)(2,1)S(1)}, u32[]{:S(2)}, u32[]{:S(2)}) async-start(bf16[4,56,512]{2,1,0:T(8,128)(2,1)} %get-tuple-element.98), calls=%async_computation.1 | async-start | bytes 458752 | tf_op jit(solution)/shard_map/all_to_all | solution.py:514
  60.7 5.6 %collective-permute-start.5 = (bf16[16,512]{1,0:T(8,128)(2,1)S(1)}, bf16[16,512]{1,0:T(8,128)(2,1)S(1)}, u32[]{:S(2)}, u32[]{:S(2)}) collective-permute-start(bf16[16,512]{1,0:T(8,128)(2,1)S(1)} %get-tuple-element.100), channel_id=1, source_target_pairs={{1,2},{2,1},{3,4},{4,3},{5,6},{6,5},{7,8},{8,7},{9,10},{10,9},{11,... | collective-permute-start | bytes 49160 | tf_op jit(solution)/shard_map/ppermute | solution.py:412
  62.1 5.8 %collective-permute-start.6 = (bf16[16,512]{1,0:T(8,128)(2,1)S(1)}, bf16[16,512]{1,0:T(8,128)(2,1)S(1)}, u32[]{:S(2)}, u32[]{:S(2)}) collective-permute-start(bf16[16,512]{1,0:T(8,128)(2,1)S(1)} %get-tuple-element.101), channel_id=1, source_target_pairs={{16,32},{32,16},{48,64},{64,48},{80,96},{96,80},{112,128},{128,112... | collective-permute-start | bytes 49160 | tf_op jit(solution)/shard_map/ppermute | solution.py:413
  66.2 1.7 %collective-permute-start.7 = (bf16[16,512]{1,0:T(8,128)(2,1)S(1)}, bf16[16,512]{1,0:T(8,128)(2,1)S(1)}, u32[]{:S(2)}, u32[]{:S(2)}) collective-permute-start(bf16[16,512]{1,0:T(8,128)(2,1)S(1)} %get-tuple-element.102), channel_id=1, source_target_pairs={{0,16},{16,0},{32,48},{48,32},{64,80},{80,64},{96,112},{112,96},{1... | collective-permute-start | bytes 49160 | tf_op jit(solution)/shard_map/ppermute | solution.py:414
  66.2 3.1 %collective-permute-start.8 = (bf16[16,512]{1,0:T(8,128)(2,1)S(1)}, bf16[16,512]{1,0:T(8,128)(2,1)S(1)}, u32[]{:S(2)}, u32[]{:S(2)}) collective-permute-start(bf16[16,512]{1,0:T(8,128)(2,1)S(1)} %get-tuple-element.103), channel_id=1, source_target_pairs={{0,1},{1,0},{2,3},{3,2},{4,5},{5,4},{6,7},{7,6},{8,9},{9,8},{10,11... | collective-permute-start | bytes 49160 | tf_op jit(solution)/shard_map/ppermute | solution.py:415
  100.9 6.3 %collective-permute-start.9 = (bf16[1792,512]{1,0:T(8,128)(2,1)S(1)}, bf16[1792,512]{1,0:T(8,128)(2,1)S(1)}, u32[]{:S(2)}, u32[]{:S(2)}) collective-permute-start(bf16[1792,512]{1,0:T(8,128)(2,1)S(1)} %bitcast.2), channel_id=1, source_target_pairs={{0,16},{16,0},{1,17},{17,1},{2,18},{18,2},{3,19},{19,3},{4,20},{20... | collective-permute-start | bytes 5505032 | tf_op jit(solution)/shard_map/ppermute | solution.py:523

commit v6 on v5

--- a/solution.py
+++ b/solution.py
@@ -12,8 +12,21 @@
 F32 = jnp.float32
 GX = ("yh", "x", "c")
 GY = ("yl", "zh", "zl")
-NEAR = ("yh", "x", "yl", "zl")
-FAR = "zh"
+ALL = ("yh", "x", "c", "yl", "zh", "zl")
+
+
+def place(x, y, core, z):
+    return ((y // 2 * 4 + x) * 2 + core) * 16 + y % 2 * 8 + z % 8
+
+
+def groups():
+    four, lines = range(4), [(o, k) for o in range(4) for k in range(4)]
+    near = [[place(k, o, 0, 2 * p + b) for k in four for b in (0, 1)] for o, p in lines]
+    near += [[place(o, k, 1, 2 * p + 1 + b) for k in four for b in (0, 1)] for o, p in lines]
+    ring = [[place(o, k, 0, z) for k in four] for o in four for z in range(8)]
+    ring += [[place(k, o, 1, z) for k in four] for o in four for z in range(8)]
+    far = [[place(x, y, c, 2 * p + b + c) for p in four] for x, y in lines for c in (0, 1) for b in (0, 1)]
+    return near, ring, far
 VMEM = pl.BlockSpec(memory_space=pltpu.VMEM)
 ANY = pl.BlockSpec(memory_space=pl.ANY)
 
@@ -81,6 +94,9 @@
 
 def parities():
     return lax.axis_index("c"), lax.axis_index("zl")
+
+
+ROW_STEPS, COLUMN_STEPS = (1, 2), (0, 3)
 
 
 def side_of(step, row_odd, col_odd):
@@ -331,31 +347,49 @@
     out[...] = (mine[...].astype(F32) + other[...].astype(F32)).astype(BF)
 
 
-def near_sum_kernel(parts, *refs):
-    backs, out, onward = refs[:4], refs[4], refs[5:]
-    for back, ref in zip(backs, onward, strict=True):
-        ref[...] = back[...]
+def sum_parts(parts):
     total = parts[0].astype(F32)
     for part in range(1, parts.shape[0]):
         total = total + parts[part].astype(F32)
-    total = total.astype(BF)
+    return total
+
+
+def near_sum_kernel(parts, out):
+    out[...] = sum_parts(parts).astype(BF)
+
+
+def ring_sum_kernel(parts, back0, back1, out, onward0, onward1):
+    onward0[...] = back0[...]
+    onward1[...] = back1[...]
+    total = sum_parts(parts).astype(BF)
     for part in range(out.shape[0]):
         out[part] = total
 
 
-def far_sum_kernel(factor, parts, d_node, lists, ret0, ret1, ret2, ret3, out, grad_nodes):
-    total = parts[0].astype(F32)
-    for part in range(1, parts.shape[0]):
-        total = total + parts[part].astype(F32)
-    total = (total * factor).astype(BF)
+def add_returned(grad, lists, steps, returned):
+    odd = parities()
+    for step, ret in zip(steps, returned, strict=True):
+        row = lists[0, 0, pl.ds(side_of(step, *odd), 1), :]
+        grad = grad + dot(pick(row, grad.shape[0]).astype(BF), ret[...])
+    return grad
+
+
+def far_sum_kernel(
+    factor, parts, d_node, lists, ret0, ret1, back0, back1, out, grad, onward0, onward1
+):
+    onward0[...] = back0[...]
+    onward1[...] = back1[...]
+    total = (sum_parts(parts) * factor).astype(BF)
     for part in range(out.shape[0]):
         out[part] = total
-    odd = parities()
-    grad = d_node[...]
-    for step, ret in enumerate((ret0, ret1, ret2, ret3)):
-        row = lists[0, 0, pl.ds(side_of(step, *odd), 1), :]
-        grad = grad + dot(pick(row, grad.shape[0]).astype(BF), ret[...])
-    grad_nodes[0, 0] = grad.astype(BF)
+    grad[...] = add_returned(d_node[...], lists, ROW_STEPS, (ret0, ret1))
+
+
+def spread_kernel(whole, grad, lists, ret0, ret1, out, grad_nodes):
+    rows = whole[...]
+    for part in range(out.shape[0]):
+        out[part] = rows
+    grad_nodes[0, 0] = add_returned(grad[...], lists, COLUMN_STEPS, (ret0, ret1)).astype(BF)
 
 
 def place_kernel(other_core, half, *refs):
@@ -401,19 +435,22 @@
 
 def pairs(count, first):
     made = []
-    for i in range(first, count + first, 2):
-        made += [(i, (i + 1) % count), ((i + 1) % count, i)]
+    for i in range(first, count - 1, 2):
+        made += [(i, i + 1), (i + 1, i)]
     return made
 
 
-def exchange(blocks):
-    nx, ny = lax.axis_size(GX), lax.axis_size(GY)
+def exchange(blocks, steps):
+    axes = (GY, GX, GX, GY)
+    first = (1, 1, 0, 0)
     return [
-        lax.ppermute(blocks[0], GY, pairs(ny, 1)),
-        lax.ppermute(blocks[1], GX, pairs(nx, 1)),
-        lax.ppermute(blocks[2], GX, pairs(nx, 0)),
-        lax.ppermute(blocks[3], GY, pairs(ny, 0)),
+        lax.ppermute(block, axes[step], pairs(lax.axis_size(axes[step]), first[step]))
+        for step, block in zip(steps, blocks, strict=True)
     ]
+
+
+def swap(rows, groups):
+    return lax.all_to_all(rows, ALL, 0, 0, axis_index_groups=groups, tiled=True)
 
 
 def load(packs, nodes, edges, senders, segments, cot_nodes, cot_edges, weights):
@@ -497,29 +534,39 @@
             pltpu.SemaphoreType.DMA((2,)),
         ],
     )(*in_hbm(nodes, send_lists))
-    halos = exchange(packs)
-    loaded = load(packs[0], nodes, edges, senders, segments, cot_nodes, cot_edges, weights)
+    halos = exchange(packs, range(4))
+    loaded = load(packs[3], nodes, edges, senders, segments, cot_nodes, cot_edges, weights)
     node_next, send, keep, grad_edges, d_node, backs = layer(halos, loaded)
 
     got = lax.ppermute(send, "c", pairs(2, 0))
     pair = call(pair_sum_kernel, shape(keep.shape), [VMEM] * 2, limit=8)(keep, got)
 
-    near, far = lax.axis_size(NEAR), lax.axis_size(FAR)
-    strip = total // 2 // near
-    pieces = lax.all_to_all(pair, NEAR, 0, 0, tiled=True).reshape(near, strip, width)
-    pieces, *backs = call(
-        near_sum_kernel, [shape((far, strip, width))] + block, [VMEM] * 5, limit=8
-    )(pieces, *backs)
-    returned = exchange(backs)
-    pieces = lax.all_to_all(pieces, FAR, 0, 0, tiled=True)
-    factor = float(lines * near * far * 2) ** -0.5
-    pieces, grad_nodes = call(
+    near, ring, far = groups()
+    n_near, n_ring, n_far = len(near[0]), len(ring[0]), len(far[0])
+    mid = total // 2 // n_near
+    strip = mid // n_ring
+    factor = float(lines * 2 * n_near * n_ring * n_far) ** -0.5
+    two = block[:2]
+    pieces = swap(pair, near).reshape(n_near, mid, width)
+    pieces = call(near_sum_kernel, shape((mid, width)), [VMEM], limit=8)(pieces)
+    pieces = swap(pieces, ring).reshape(n_ring, strip, width)
+    pieces, *by_row = call(
+        ring_sum_kernel, [shape((n_far, strip, width))] + two, [VMEM] * 3, limit=8
+    )(pieces, *[backs[step] for step in ROW_STEPS])
+    by_row = exchange(by_row, ROW_STEPS)
+    pieces = swap(pieces, far)
+    pieces, grad, *by_column = call(
         functools.partial(far_sum_kernel, factor),
-        [shape((near, strip, width)), shape(nodes.shape)],
+        [shape((n_ring, strip, width)), shape(d_node.shape, F32)] + two,
         [VMEM] * 7,
         limit=8,
-    )(pieces, d_node, send_lists, *returned)
-    mine = lax.all_to_all(pieces, NEAR, 0, 0, tiled=True).reshape(total // 2, width)
+    )(pieces, d_node, send_lists, *by_row, *[backs[step] for step in COLUMN_STEPS])
+    by_column = exchange(by_column, COLUMN_STEPS)
+    pieces = swap(pieces, ring).reshape(mid, width)
+    pieces, grad_nodes = call(
+        spread_kernel, [shape((n_near, mid, width)), shape(nodes.shape)], [VMEM] * 5, limit=8
+    )(pieces, grad, send_lists, *by_column)
+    mine = swap(pieces, near).reshape(total // 2, width)
     other = lax.ppermute(mine, "c", pairs(2, 0))
     outs = [shape(w.shape) for w in weights]
     sems = [pltpu.SemaphoreType.DMA((total // width,))]

time: 109 us -> 107 us (0.982)
  blocking collectives: 60.3 us -> 53.5 us
  starting transfers between devices: 26.5 us -> 29.8 us
    all_to_all x2 -> x3, blocking collectives: 60.3 us -> 53.5 us  [swap(): return lax.all_to_all(rows, ALL, 0, 0, axis_index_groups=groups, tiled=True)]
    all_to_all x1 -> x2, starting transfers between devices: 4.53 us -> 8.32 us  [swap(): return lax.all_to_all(rows, ALL, 0, 0, axis_index_groups=groups, tiled=True)]
    all_to_all x1 -> x2, waiting for transfers between devices: 0.01 us -> 1.29 us  [swap(): return lax.all_to_all(rows, ALL, 0, 0, axis_index_groups=groups, tiled=True)]
    pallas_call x2 -> x4, Pallas kernels: 1.9 us -> 2.64 us  [the longest x1 0.91 us: local(): call(spread_kernel, [shape((n_near, mid, width)), shape(nodes.shape)], [V...]
  transfers between devices with their start and end apart: 11 -> 12, of which waited for: 4 -> 5; matrix products, arithmetic and copies ran while one was open for 0% -> 0% of each run, Pallas kernels for 5% -> 5%
where the time goes in v6:
time: 107 us; the launch traced here: 106 us
  blocking collectives  53.5 us (50%)
  starting transfers between devices  29.8 us (28%)
  Pallas kernels  14.9 us (14%)
  waiting for transfers between devices  7.43 us (7%)
    all_to_all x3, blocking collectives, swap(): return lax.all_to_all(rows, ALL, 0, 0, axis_index_groups=groups, tiled=True)  53.5 us
    ppermute x8, starting transfers between devices, exchange(): lax.ppermute(block, axes[step], pairs(lax.axis_size(axes[step]), first[st...  18.2 us
    all_to_all x2, starting transfers between devices, swap(): return lax.all_to_all(rows, ALL, 0, 0, axis_index_groups=groups, tiled=True)  8.32 us
    pallas_call x1, Pallas kernels, layer(): call(layer_kernel, [shape((1, 1, count, width)), half] + [shape((2 * reac...  4 us
    ppermute x8, waiting for transfers between devices, exchange(): lax.ppermute(block, axes[step], pairs(lax.axis_size(axes[step]), first[st...  2.45 us
    ppermute x1, starting transfers between devices, local(): other = lax.ppermute(mine, 'c', pairs(2, 0))  2.43 us
    pallas_call x1, Pallas kernels, load(): call(load_kernel, [shape((count, width)), shape((lines, width))] * 2 + [s...  2.39 us
  transfers between devices with their start and end apart: 12, of which 5 were waited for; matrix products, arithmetic and copies ran while one was open for 0% of the time, Pallas kernels for 5%

profile of v6, /device:TPU:1, one launch (start us, length us, event | category | flops | bytes accessed | tf_op | source)
XLA Modules:
  0.0 106.4 jit_solution(4837636514793921318)
XLA Ops:
  0.6 1.1 %shard_map.162 = (bf16[16,512]{1,0:T(8,128)(2,1)S(1)}, bf16[16,512]{1,0:T(8,128)(2,1)S(1)}, bf16[16,512]{1,0:T(8,128)(2,1)S(1)}, bf16[16,512]{1,0:T(8,128)(2,1)S(1)}) custom-call(bf16[1,1,64,512]{3,2,1,0:T(8,128)(2,1)} %nodes_hbm.3, s32[1,1,4,16]{3,2,1,0:T(4,128)} %lists.3), custom_call_target="tpu_custom_call" | custom-call | tf_op jit(solution)/shard_map/pallas_call | solution.py:527
  2.4 4.5 %collective-permute-start.1 = (bf16[16,512]{1,0:T(8,128)(2,1)S(1)}, bf16[16,512]{1,0:T(8,128)(2,1)S(1)}, u32[]{:S(2)}, u32[]{:S(2)}) collective-permute-start(bf16[16,512]{1,0:T(8,128)(2,1)S(1)} %get-tuple-element.64), channel_id=1, source_target_pairs={{16,32},{32,16},{48,64},{64,48},{80,96},{96,80},{112,128},{128,112... | collective-permute-start | bytes 49160 | tf_op jit(solution)/shard_map/ppermute | solution.py:447
  7.0 4.9 %collective-permute-start.3 = (bf16[16,512]{1,0:T(8,128)(2,1)S(1)}, bf16[16,512]{1,0:T(8,128)(2,1)S(1)}, u32[]{:S(2)}, u32[]{:S(2)}) collective-permute-start(bf16[16,512]{1,0:T(8,128)(2,1)S(1)} %get-tuple-element.66.packs), channel_id=1, source_target_pairs={{0,1},{1,0},{2,3},{3,2},{4,5},{5,4},{6,7},{7,6},{8,9},{9,8},{10,11... | collective-permute-start | bytes 49160 | tf_op jit(solution)/shard_map/ppermute | solution.py:447
  11.9 2.4 %shard_map.163 = (bf16[64,512]{1,0:T(8,128)(2,1)S(1)}, bf16[384,512]{1,0:T(8,128)(2,1)S(1)}, bf16[64,512]{1,0:T(8,128)(2,1)S(1)}, bf16[384,512]{1,0:T(8,128)(2,1...) custom-call(bf16[16,512]{1,0:T(8,128)(2,1)S(1)} %get-tuple-element.6, ...), custom_call_target="tpu_custom_call" | custom-call | tf_op jit(solution)/shard_map/pallas_call | solution.py:460
  14.3 4.0 %shard_map.164 = (bf16[1,1,64,512]{3,2,1,0:T(8,128)(2,1)}, bf16[1792,512]{1,0:T(8,128)(2,1)S(1)}, bf16[256,512]{1,0:T(8,128)(2,1)S(1)}, bf16[128,512]{1,0:T(8,12...) custom-call(bf16[16,512]{1,0:T(8,128)(2,1)S(1)} %collective-permute-, ...), custom_call_target="tpu_custom_call" | custom-call | tf_op jit(solution)/shard_map/pallas_call | solution.py:483
  18.3 0.8 collective-permute-start.4
  19.2 1.8 %shard_map.165 = (bf16[1792,512]{1,0:T(8,128)(2,1)S(1)}, bf16[1,1,384,512]{3,2,1,0:T(8,128)(2,1)}, f32[64,512]{1,0:T(8,128)S(1)}, bf16[16,512]{1,0:T(8,128)(2,1)...) custom-call(bf16[64,512]{1,0:T(8,128)(2,1)S(1)} %get-tuple-element.67.node, ...), custom_call_target="tpu_custom_call" | custom-call | flops 1342177280 | bytes 12582912 | tf_op jit(solution)/shard_map/pallas_call | solution.py:493
  21.0 1.6 %collective-permute-done.4.other = bf16[1792,512]{1,0:T(8,128)(2,1)S(1)} collective-permute-done((bf16[1792,512]{1,0:T(8,128)(2,1)S(1)}, bf16[1792,512]{1,0:T(8,128)(2,1)S(1)}, u32[]{:S(2)}, u32[]{:S(2)}) %collective-permute-start.4) | collective-permute-done | bytes 1835040 | tf_op jit(solution)/shard_map/ppermute | solution.py:541
  23.0 24.7 %all_to_all.33.parts = bf16[8,224,512]{2,1,0:T(8,128)(2,1)S(1)} all-to-all(bf16[8,224,512]{2,1,0:T(8,128)(2,1)S(1)} %bitcast.6), channel_id=1, replica_groups={{0,1,32,33,64,65,96,97},{2,3,34,35,66,67,98,99},{4,5,36,37,68,69,100,10..., dimensions={0} | all-to-all | bytes 3670016 | tf_op jit(solution)/shard_map/all_to_all | solution.py:453
  47.9 7.7 %all_to_all.34.parts = bf16[4,56,512]{2,1,0:T(8,128)(2,1)S(1)} all-to-all(bf16[4,56,512]{2,1,0:T(8,128)(2,1)S(1)} %bitcast.8), channel_id=1, replica_groups={{0,8,128,136},{1,9,129,137},{2,10,130,138},{3,11,131,139},{4,12,132,140..., dimensions={0} | all-to-all | bytes 458752 | tf_op jit(solution)/shard_map/all_to_all | solution.py:453
  56.3 3.6 %all-to-all-start.2 = ((bf16[4,56,512]{2,1,0:T(8,128)(2,1)}), bf16[4,56,512]{2,1,0:T(8,128)(2,1)S(1)}, u32[]{:S(2)}, u32[]{:S(2)}) async-start(bf16[4,56,512]{2,1,0:T(8,128)(2,1)} %get-tuple-element.98), calls=%async_computation.2 | async-start | bytes 458752 | tf_op jit(solution)/shard_map/all_to_all | solution.py:453
  60.0 3.7 %collective-permute-start.5 = (bf16[16,512]{1,0:T(8,128)(2,1)S(1)}, bf16[16,512]{1,0:T(8,128)(2,1)S(1)}, u32[]{:S(2)}, u32[]{:S(2)}) collective-permute-start(bf16[16,512]{1,0:T(8,128)(2,1)S(1)} %get-tuple-element.100), channel_id=1, source_target_pairs={{16,32},{32,16},{48,64},{64,48},{80,96},{96,80},{112,128},{128,112... | collective-permute-start | bytes 49160 | tf_op jit(solution)/shard_map/ppermute | solution.py:447
  63.8 1.3 %collective-permute-done.5.ret0 = bf16[16,512]{1,0:T(8,128)(2,1)S(1)} collective-permute-done((bf16[16,512]{1,0:T(8,128)(2,1)S(1)}, bf16[16,512]{1,0:T(8,128)(2,1)S(1)}, u32[]{:S(2)}, u32[]{:S(2)}) %collective-permute-start.5) | collective-permute-done | bytes 16416 | tf_op jit(solution)/shard_map/ppermute | solution.py:447
  65.1 1.3 %all-to-all-done.2.parts = bf16[4,56,512]{2,1,0:T(8,128)(2,1)S(1)} async-done(((bf16[4,56,512]{2,1,0:T(8,128)(2,1)}), bf16[4,56,512]{2,1,0:T(8,128)(2,1)S(1)}, u32[]{:S(2)}, u32[]{:S(2)}) %all-to-all-start.2) | async-done | bytes 229408 | tf_op jit(solution)/shard_map/all_to_all | solution.py:453
  66.4 0.8 shard_map.169
  67.2 4.7 %all-to-all-start.3 = ((bf16[4,56,512]{2,1,0:T(8,128)(2,1)}), bf16[4,56,512]{2,1,0:T(8,128)(2,1)S(1)}, u32[]{:S(2)}, u32[]{:S(2)}) async-start(bf16[4,56,512]{2,1,0:T(8,128)(2,1)} %get-tuple-element.104), calls=%async_computation.3 | async-start | bytes 458752 | tf_op jit(solution)/shard_map/all_to_all | solution.py:453
  72.5 3.6 %collective-permute-start.8 = (bf16[16,512]{1,0:T(8,128)(2,1)S(1)}, bf16[16,512]{1,0:T(8,128)(2,1)S(1)}, u32[]{:S(2)}, u32[]{:S(2)}) collective-permute-start(bf16[16,512]{1,0:T(8,128)(2,1)S(1)} %get-tuple-element.107), channel_id=1, source_target_pairs={{0,1},{1,0},{2,3},{3,2},{4,5},{5,4},{6,7},{7,6},{8,9},{9,8},{10,11... | collective-permute-start | bytes 49160 | tf_op jit(solution)/shard_map/ppermute | solution.py:447
  76.1 1.1 %collective-permute-done.8.ret1 = bf16[16,512]{1,0:T(8,128)(2,1)S(1)} collective-permute-done((bf16[16,512]{1,0:T(8,128)(2,1)S(1)}, bf16[16,512]{1,0:T(8,128)(2,1)S(1)}, u32[]{:S(2)}, u32[]{:S(2)}) %collective-permute-start.8) | collective-permute-done | bytes 16416 | tf_op jit(solution)/shard_map/ppermute | solution.py:447
  77.2 0.9 shard_map.170
  78.2 21.1 %all_to_all.35 = bf16[8,224,512]{2,1,0:T(8,128)(2,1)S(1)} all-to-all(bf16[8,224,512]{2,1,0:T(8,128)(2,1)S(1)} %get-tuple-element.110), channel_id=1, replica_groups={{0,1,32,33,64,65,96,97},{2,3,34,35,66,67,98,99},{4,5,36,37,68,69,100,10..., dimensions={0} | all-to-all | bytes 3670016 | tf_op jit(solution)/shard_map/all_to_all | solution.py:453
  99.3 2.4 %collective-permute-start.9 = (bf16[1792,512]{1,0:T(8,128)(2,1)S(1)}, bf16[1792,512]{1,0:T(8,128)(2,1)S(1)}, u32[]{:S(2)}, u32[]{:S(2)}) collective-permute-start(bf16[1792,512]{1,0:T(8,128)(2,1)S(1)} %bitcast.4), channel_id=1, source_target_pairs={{0,16},{16,0},{1,17},{17,1},{2,18},{18,2},{3,19},{19,3},{4,20},{20... | collective-permute-start | bytes 5505032 | tf_op jit(solution)/shard_map/ppermute | solution.py:570
  101.7 1.3 %shard_map.171 = (bf16[1536,512]{1,0:T(8,128)(2,1)}, bf16[512,512]{1,0:T(8,128)(2,1)}, bf16[1024,512]{1,0:T(8,128)(2,1)}, bf16[512,512]{1,0:T(8,128)(2,1)}) custom-call(bf16[1792,512]{1,0:T(8,128)(2,1)S(1)} %bitcast.5), custom_call_target="tpu_custom_call" | custom-call | tf_op jit(solution)/shard_map/pallas_call | solution.py:573
  103.0 2.1 %collective-permute-done.9.half = bf16[1792,512]{1,0:T(8,128)(2,1)S(1)} collective-permute-done((bf16[1792,512]{1,0:T(8,128)(2,1)S(1)}, bf16[1792,512]{1,0:T(8,128)(2,1)S(1)}, u32[]{:S(2)}, u32[]{:S(2)}) %collective-permute-start.9) | collective-permute-done | bytes 1835040 | tf_op jit(solution)/shard_map/ppermute | solution.py:570
  105.1 1.3 %shard_map.172 = (bf16[1536,512]{1,0:T(8,128)(2,1)}, bf16[512,512]{1,0:T(8,128)(2,1)}, bf16[1024,512]{1,0:T(8,128)(2,1)}, bf16[512,512]{1,0:T(8,128)(2,1)}) custom-call(bf16[1792,512]{1,0:T(8,128)(2,1)S(1)} %collective-permute-done.9.half, ...), custom_call_target="tpu_custom_call", output_to_operand_aliasing={{0}: (1, {}), {1}: (2, {}), {2}: (3, {}), {3}: (4, {})} | custom-call | tf_op jit(solution)/shard_map/pallas_call | solution.py:581
  (16 shorter events, 2.9 us)
Async XLA Ops:
  1.7 12.6 %collective-permute-start = (bf16[16,512]{1,0:T(8,128)(2,1)S(1)}, bf16[16,512]{1,0:T(8,128)(2,1)S(1)}, u32[]{:S(2)}, u32[]{:S(2)}) collective-permute-start(bf16[16,512]{1,0:T(8,128)(2,1)S(1)} %get-tuple-element.63), channel_id=1, source_target_pairs={{1,2},{2,1},{3,4},{4,3},{5,6},{6,5},{7,8},{8,7},{9,10},{10,9},{11,... | collective-permute-start | bytes 49160 | tf_op jit(solution)/shard_map/ppermute | solution.py:447
  2.4 11.9 %collective-permute-start.1 = (bf16[16,512]{1,0:T(8,128)(2,1)S(1)}, bf16[16,512]{1,0:T(8,128)(2,1)S(1)}, u32[]{:S(2)}, u32[]{:S(2)}) collective-permute-start(bf16[16,512]{1,0:T(8,128)(2,1)S(1)} %get-tuple-element.64), channel_id=1, source_target_pairs={{16,32},{32,16},{48,64},{64,48},{80,96},{96,80},{112,128},{128,112... | collective-permute-start | bytes 49160 | tf_op jit(solution)/shard_map/ppermute | solution.py:447
  6.9 7.4 %collective-permute-start.2 = (bf16[16,512]{1,0:T(8,128)(2,1)S(1)}, bf16[16,512]{1,0:T(8,128)(2,1)S(1)}, u32[]{:S(2)}, u32[]{:S(2)}) collective-permute-start(bf16[16,512]{1,0:T(8,128)(2,1)S(1)} %get-tuple-element.65), channel_id=1, source_target_pairs={{0,16},{16,0},{32,48},{48,32},{64,80},{80,64},{96,112},{112,96},{1... | collective-permute-start | bytes 49160 | tf_op jit(solution)/shard_map/ppermute | solution.py:447
  7.0 7.3 %collective-permute-start.3 = (bf16[16,512]{1,0:T(8,128)(2,1)S(1)}, bf16[16,512]{1,0:T(8,128)(2,1)S(1)}, u32[]{:S(2)}, u32[]{:S(2)}) collective-permute-start(bf16[16,512]{1,0:T(8,128)(2,1)S(1)} %get-tuple-element.66.packs), channel_id=1, source_target_pairs={{0,1},{1,0},{2,3},{3,2},{4,5},{5,4},{6,7},{7,6},{8,9},{9,8},{10,11... | collective-permute-start | bytes 49160 | tf_op jit(solution)/shard_map/ppermute | solution.py:447
  18.3 4.2 %collective-permute-start.4 = (bf16[1792,512]{1,0:T(8,128)(2,1)S(1)}, bf16[1792,512]{1,0:T(8,128)(2,1)S(1)}, u32[]{:S(2)}, u32[]{:S(2)}) collective-permute-start(bf16[1792,512]{1,0:T(8,128)(2,1)S(1)} %get-tuple-element.95), channel_id=1, source_target_pairs={{0,16},{16,0},{1,17},{17,1},{2,18},{18,2},{3,19},{19,3},{4,20},{20... | collective-permute-start | bytes 5505032 | tf_op jit(solution)/shard_map/ppermute | solution.py:541
  47.6 18.8 %copy-start = (s32[1,1,4,16]{3,2,1,0:T(4,128)S(1)}, s32[1,1,4,16]{3,2,1,0:T(4,128)}, u32[]{:S(2)}) copy-start(s32[1,1,4,16]{3,2,1,0:T(4,128)} %lists.3) | copy-start | bytes 772
  56.3 10.1 %all-to-all-start.2 = ((bf16[4,56,512]{2,1,0:T(8,128)(2,1)}), bf16[4,56,512]{2,1,0:T(8,128)(2,1)S(1)}, u32[]{:S(2)}, u32[]{:S(2)}) async-start(bf16[4,56,512]{2,1,0:T(8,128)(2,1)} %get-tuple-element.98), calls=%async_computation.2 | async-start | bytes 458752 | tf_op jit(solution)/shard_map/all_to_all | solution.py:453
  60.0 5.1 %collective-permute-start.5 = (bf16[16,512]{1,0:T(8,128)(2,1)S(1)}, bf16[16,512]{1,0:T(8,128)(2,1)S(1)}, u32[]{:S(2)}, u32[]{:S(2)}) collective-permute-start(bf16[16,512]{1,0:T(8,128)(2,1)S(1)} %get-tuple-element.100), channel_id=1, source_target_pairs={{16,32},{32,16},{48,64},{64,48},{80,96},{96,80},{112,128},{128,112... | collective-permute-start | bytes 49160 | tf_op jit(solution)/shard_map/ppermute | solution.py:447
  63.7 1.4 %collective-permute-start.6 = (bf16[16,512]{1,0:T(8,128)(2,1)S(1)}, bf16[16,512]{1,0:T(8,128)(2,1)S(1)}, u32[]{:S(2)}, u32[]{:S(2)}) collective-permute-start(bf16[16,512]{1,0:T(8,128)(2,1)S(1)} %get-tuple-element.101), channel_id=1, source_target_pairs={{0,16},{16,0},{32,48},{48,32},{64,80},{80,64},{96,112},{112,96},{1... | collective-permute-start | bytes 49160 | tf_op jit(solution)/shard_map/ppermute | solution.py:447
  67.2 10.1 %all-to-all-start.3 = ((bf16[4,56,512]{2,1,0:T(8,128)(2,1)}), bf16[4,56,512]{2,1,0:T(8,128)(2,1)S(1)}, u32[]{:S(2)}, u32[]{:S(2)}) async-start(bf16[4,56,512]{2,1,0:T(8,128)(2,1)} %get-tuple-element.104), calls=%async_computation.3 | async-start | bytes 458752 | tf_op jit(solution)/shard_map/all_to_all | solution.py:453
  71.9 4.2 %collective-permute-start.7 = (bf16[16,512]{1,0:T(8,128)(2,1)S(1)}, bf16[16,512]{1,0:T(8,128)(2,1)S(1)}, u32[]{:S(2)}, u32[]{:S(2)}) collective-permute-start(bf16[16,512]{1,0:T(8,128)(2,1)S(1)} %get-tuple-element.106), channel_id=1, source_target_pairs={{1,2},{2,1},{3,4},{4,3},{5,6},{6,5},{7,8},{8,7},{9,10},{10,9},{11,... | collective-permute-start | bytes 49160 | tf_op jit(solution)/shard_map/ppermute | solution.py:447
  72.5 4.7 %collective-permute-start.8 = (bf16[16,512]{1,0:T(8,128)(2,1)S(1)}, bf16[16,512]{1,0:T(8,128)(2,1)S(1)}, u32[]{:S(2)}, u32[]{:S(2)}) collective-permute-start(bf16[16,512]{1,0:T(8,128)(2,1)S(1)} %get-tuple-element.107), channel_id=1, source_target_pairs={{0,1},{1,0},{2,3},{3,2},{4,5},{5,4},{6,7},{7,6},{8,9},{9,8},{10,11... | collective-permute-start | bytes 49160 | tf_op jit(solution)/shard_map/ppermute | solution.py:447
  99.3 5.8 %collective-permute-start.9 = (bf16[1792,512]{1,0:T(8,128)(2,1)S(1)}, bf16[1792,512]{1,0:T(8,128)(2,1)S(1)}, u32[]{:S(2)}, u32[]{:S(2)}) collective-permute-start(bf16[1792,512]{1,0:T(8,128)(2,1)S(1)} %bitcast.4), channel_id=1, source_target_pairs={{0,16},{16,0},{1,17},{17,1},{2,18},{18,2},{3,19},{19,3},{4,20},{20... | collective-permute-start | bytes 5505032 | tf_op jit(solution)/shard_map/ppermute | solution.py:570

commit v7 on v6

--- a/solution.py
+++ b/solution.py
@@ -96,7 +96,7 @@
     return lax.axis_index("c"), lax.axis_index("zl")
 
 
-ROW_STEPS, COLUMN_STEPS = (1, 2), (0, 3)
+CORE_STEP, CHIP_STEPS = 2, (0, 1, 3)
 
 
 def side_of(step, row_odd, col_odd):
@@ -277,6 +277,15 @@
     dz_one[...] = (dot_cols(dz_two[...], w_edge2[...]) * slope_one).astype(BF)
     sum_send[...] = hi_lo(dot(to_ext[...], dz_one[...]))
     sum_recv[...] = hi_lo(dot(to_node[...], dz_one[...]))
+    first = count + side_of(CORE_STEP, *odd) * rows
+    ride = jnp.concatenate(
+        [
+            sum_send[pl.ds(pl.multiple_of(first, rows), rows), :],
+            sum_send[pl.ds(pl.multiple_of(reach + first, rows), rows), :],
+        ],
+        axis=0,
+    )
+    send[send.shape[0] - rows :, :] = fold(dot_cols(ride, w_edge1[width : 2 * width, :])).astype(BF)
     put_half(
         send,
         1 - odd[0],
@@ -315,7 +324,6 @@
     back0,
     back1,
     back2,
-    back3,
     d_ext,
 ):
     odd = parities()
@@ -338,13 +346,15 @@
     d_ext[...] = fold(dot_cols(sum_send[...], w_edge1[width : 2 * width, :]))
     d_recv = fold(dot_cols(sum_recv[...], w_edge1[2 * width :, :]))
     d_node[...] = dn_part[...] + d_recv + d_ext[:count, :]
-    for step, back in enumerate((back0, back1, back2, back3)):
+    for step, back in zip(CHIP_STEPS, (back0, back1, back2), strict=True):
         place = count + side_of(step, *odd) * rows
         back[...] = d_ext[pl.ds(pl.multiple_of(place, rows), rows), :].astype(BF)
 
 
-def pair_sum_kernel(mine, other, out):
-    out[...] = (mine[...].astype(F32) + other[...].astype(F32)).astype(BF)
+def pair_sum_kernel(mine, other, out, ret):
+    rows = mine.shape[0]
+    out[...] = (mine[...].astype(F32) + other[:rows, :].astype(F32)).astype(BF)
+    ret[...] = other[rows:, :]
 
 
 def sum_parts(parts):
@@ -358,38 +368,31 @@
     out[...] = sum_parts(parts).astype(BF)
 
 
-def ring_sum_kernel(parts, back0, back1, out, onward0, onward1):
-    onward0[...] = back0[...]
-    onward1[...] = back1[...]
+def ring_sum_kernel(parts, *refs):
+    backs, out, onward = refs[:3], refs[3], refs[4:]
+    for back, ref in zip(backs, onward, strict=True):
+        ref[...] = back[...]
     total = sum_parts(parts).astype(BF)
     for part in range(out.shape[0]):
         out[part] = total
 
 
-def add_returned(grad, lists, steps, returned):
-    odd = parities()
-    for step, ret in zip(steps, returned, strict=True):
-        row = lists[0, 0, pl.ds(side_of(step, *odd), 1), :]
-        grad = grad + dot(pick(row, grad.shape[0]).astype(BF), ret[...])
-    return grad
-
-
-def far_sum_kernel(
-    factor, parts, d_node, lists, ret0, ret1, back0, back1, out, grad, onward0, onward1
-):
-    onward0[...] = back0[...]
-    onward1[...] = back1[...]
+def far_sum_kernel(factor, parts, d_node, lists, ret0, ret1, ret2, ret3, out, grad_nodes):
     total = (sum_parts(parts) * factor).astype(BF)
     for part in range(out.shape[0]):
         out[part] = total
-    grad[...] = add_returned(d_node[...], lists, ROW_STEPS, (ret0, ret1))
-
-
-def spread_kernel(whole, grad, lists, ret0, ret1, out, grad_nodes):
+    odd = parities()
+    grad = d_node[...]
+    for step, ret in zip((CORE_STEP, *CHIP_STEPS), (ret0, ret1, ret2, ret3), strict=True):
+        row = lists[0, 0, pl.ds(side_of(step, *odd), 1), :]
+        grad = grad + dot(pick(row, grad.shape[0]).astype(BF), ret[...])
+    grad_nodes[0, 0] = grad.astype(BF)
+
+
+def spread_kernel(whole, out):
     rows = whole[...]
     for part in range(out.shape[0]):
         out[part] = rows
-    grad_nodes[0, 0] = add_returned(grad[...], lists, COLUMN_STEPS, (ret0, ret1)).astype(BF)
 
 
 def place_kernel(other_core, half, *refs):
@@ -435,8 +438,8 @@
 
 def pairs(count, first):
     made = []
-    for i in range(first, count - 1, 2):
-        made += [(i, i + 1), (i + 1, i)]
+    for i in range(first, count + first, 2):
+        made += [(i, (i + 1) % count), ((i + 1) % count, i)]
     return made
 
 
@@ -478,11 +481,11 @@
     node, edge, w_edge1 = loaded[0], loaded[1], loaded[4]
     (count, width), lines, rows = node.shape, edge.shape[0], halos[0].shape[0]
     reach = count + 4 * rows
-    half = shape((sum(w.shape[0] for w in loaded[4:8]) // 2, width))
+    half = sum(w.shape[0] for w in loaded[4:8]) // 2
     on_edges, on_nodes = shape((lines, width)), shape((count, width))
     node_next, send, *state = call(
         layer_kernel,
-        [shape((1, 1, count, width)), half]
+        [shape((1, 1, count, width)), shape((half + rows, width))]
         + [shape((2 * reach, width)), shape((2 * count, width)), on_edges, on_nodes, on_nodes]
         + [on_edges, on_edges, on_nodes, on_nodes]
         + [shape((2 * reach, width)), shape((2 * count, width))]
@@ -492,7 +495,8 @@
     )(*halos, *loaded)
     keep, grad_edges, d_node, *backs = call(
         rest_kernel,
-        [half, shape((1, 1, lines, width)), shape((count, width), F32)] + [shape((rows, width))] * 4,
+        [shape((half, width)), shape((1, 1, lines, width)), shape((count, width), F32)]
+        + [shape((rows, width))] * 3,
         [VMEM] * (3 + len(state)),
         limit=12,
         scratch=[pltpu.VMEM((reach, width), F32)],
@@ -539,33 +543,31 @@
     node_next, send, keep, grad_edges, d_node, backs = layer(halos, loaded)
 
     got = lax.ppermute(send, "c", pairs(2, 0))
-    pair = call(pair_sum_kernel, shape(keep.shape), [VMEM] * 2, limit=8)(keep, got)
+    pair, core_back = call(
+        pair_sum_kernel, [shape(keep.shape), shape((rows, width))], [VMEM] * 2, limit=8
+    )(keep, got)
 
     near, ring, far = groups()
     n_near, n_ring, n_far = len(near[0]), len(ring[0]), len(far[0])
     mid = total // 2 // n_near
     strip = mid // n_ring
     factor = float(lines * 2 * n_near * n_ring * n_far) ** -0.5
-    two = block[:2]
     pieces = swap(pair, near).reshape(n_near, mid, width)
     pieces = call(near_sum_kernel, shape((mid, width)), [VMEM], limit=8)(pieces)
     pieces = swap(pieces, ring).reshape(n_ring, strip, width)
-    pieces, *by_row = call(
-        ring_sum_kernel, [shape((n_far, strip, width))] + two, [VMEM] * 3, limit=8
-    )(pieces, *[backs[step] for step in ROW_STEPS])
-    by_row = exchange(by_row, ROW_STEPS)
+    pieces, *backs = call(
+        ring_sum_kernel, [shape((n_far, strip, width))] + block[:3], [VMEM] * 4, limit=8
+    )(pieces, *backs)
+    returned = exchange(backs, CHIP_STEPS)
     pieces = swap(pieces, far)
-    pieces, grad, *by_column = call(
+    pieces, grad_nodes = call(
         functools.partial(far_sum_kernel, factor),
-        [shape((n_ring, strip, width)), shape(d_node.shape, F32)] + two,
+        [shape((n_ring, strip, width)), shape(nodes.shape)],
         [VMEM] * 7,
         limit=8,
-    )(pieces, d_node, send_lists, *by_row, *[backs[step] for step in COLUMN_STEPS])
-    by_column = exchange(by_column, COLUMN_STEPS)
+    )(pieces, d_node, send_lists, core_back, *returned)
     pieces = swap(pieces, ring).reshape(mid, width)
-    pieces, grad_nodes = call(
-        spread_kernel, [shape((n_near, mid, width)), shape(nodes.shape)], [VMEM] * 5, limit=8
-    )(pieces, grad, send_lists, *by_column)
+    pieces = call(spread_kernel, shape((n_near, mid, width)), [VMEM], limit=8)(pieces)
     mine = swap(pieces, near).reshape(total // 2, width)
     other = lax.ppermute(mine, "c", pairs(2, 0))
     outs = [shape(w.shape) for w in weights]

time: 107 us -> 103 us (0.963)
  starting transfers between devices: 29.8 us -> 24.5 us
  blocking collectives: 53.5 us -> 56 us
    all_to_all x2 -> x1, starting transfers between devices: 8.32 us -> 3.63 us  [swap(): return lax.all_to_all(rows, ALL, 0, 0, axis_index_groups=groups, tiled=True)]
    all_to_all x3 -> x4, blocking collectives: 53.5 us -> 56 us  [swap(): return lax.all_to_all(rows, ALL, 0, 0, axis_index_groups=groups, tiled=True)]
    all_to_all x2 -> x1, waiting for transfers between devices: 1.29 us -> 0.01 us  [swap(): return lax.all_to_all(rows, ALL, 0, 0, axis_index_groups=groups, tiled=True)]
    ppermute x8 -> x7, waiting for transfers between devices: 2.45 us -> 3.41 us  [exchange(): lax.ppermute(block, axes[step], pairs(lax.axis_size(axes[step]), first[st...]
    ppermute x8 -> x7, starting transfers between devices: 18.2 us -> 17.3 us  [exchange(): lax.ppermute(block, axes[step], pairs(lax.axis_size(axes[step]), first[st...]
  transfers between devices with their start and end apart: 12 -> 10, of which waited for: 5 -> 4; matrix products, arithmetic and copies ran while one was open for 0% -> 0% of each run, Pallas kernels for 5% -> 5%
where the time goes in v7:
time: 103 us
  blocking collectives  56 us (54%)
  starting transfers between devices  24.5 us (24%)
  Pallas kernels  14.3 us (14%)
  waiting for transfers between devices  7.19 us (7%)
    all_to_all x4, blocking collectives, swap(): return lax.all_to_all(rows, ALL, 0, 0, axis_index_groups=groups, tiled=True)  56 us
    ppermute x7, starting transfers between devices, exchange(): lax.ppermute(block, axes[step], pairs(lax.axis_size(axes[step]), first[st...  17.3 us
    pallas_call x1, Pallas kernels, layer(): call(layer_kernel, [shape((1, 1, count, width)), shape((half + rows, widt...  4.14 us
    all_to_all x1, starting transfers between devices, swap(): return lax.all_to_all(rows, ALL, 0, 0, axis_index_groups=groups, tiled=True)  3.63 us
    ppermute x7, waiting for transfers between devices, exchange(): lax.ppermute(block, axes[step], pairs(lax.axis_size(axes[step]), first[st...  3.41 us
    pallas_call x1, Pallas kernels, load(): call(load_kernel, [shape((count, width)), shape((lines, width))] * 2 + [s...  2.39 us
    ppermute x1, starting transfers between devices, local(): other = lax.ppermute(mine, 'c', pairs(2, 0))  2.27 us
    ppermute x1, waiting for transfers between devices, local(): other = lax.ppermute(mine, 'c', pairs(2, 0))  2.13 us
  transfers between devices with their start and end apart: 10, of which 4 were waited for; matrix products, arithmetic and copies ran while one was open for 0% of the time, Pallas kernels for 5%

profile of v7, /device:TPU:1, one launch (start us, length us, event | category | flops | bytes accessed | tf_op | source)
XLA Modules:
  0.0 102.7 jit_solution(15470850559739865197)
XLA Ops:
  0.6 1.1 %shard_map.162 = (bf16[16,512]{1,0:T(8,128)(2,1)S(1)}, bf16[16,512]{1,0:T(8,128)(2,1)S(1)}, bf16[16,512]{1,0:T(8,128)(2,1)S(1)}, bf16[16,512]{1,0:T(8,128)(2,1)S(1)}) custom-call(bf16[1,1,64,512]{3,2,1,0:T(8,128)(2,1)} %nodes_hbm.3, s32[1,1,4,16]{3,2,1,0:T(4,128)} %lists.1), custom_call_target="tpu_custom_call" | custom-call | tf_op jit(solution)/shard_map/pallas_call | solution.py:531
  1.7 7.5 %collective-permute-start = (bf16[16,512]{1,0:T(8,128)(2,1)S(1)}, bf16[16,512]{1,0:T(8,128)(2,1)S(1)}, u32[]{:S(2)}, u32[]{:S(2)}) collective-permute-start(bf16[16,512]{1,0:T(8,128)(2,1)S(1)} %get-tuple-element.61), channel_id=1, source_target_pairs={{1,2},{2,1},{3,4},{4,3},{5,6},{6,5},{7,8},{8,7},{9,10},{10,9},{11,... | collective-permute-start | bytes 49160 | tf_op jit(solution)/shard_map/ppermute | solution.py:450
  9.2 2.1 %collective-permute-start.1 = (bf16[16,512]{1,0:T(8,128)(2,1)S(1)}, bf16[16,512]{1,0:T(8,128)(2,1)S(1)}, u32[]{:S(2)}, u32[]{:S(2)}) collective-permute-start(bf16[16,512]{1,0:T(8,128)(2,1)S(1)} %get-tuple-element.62), channel_id=1, source_target_pairs={{16,32},{32,16},{48,64},{64,48},{80,96},{96,80},{112,128},{128,112... | collective-permute-start | bytes 49160 | tf_op jit(solution)/shard_map/ppermute | solution.py:450
  11.3 3.2 %collective-permute-start.2 = (bf16[16,512]{1,0:T(8,128)(2,1)S(1)}, bf16[16,512]{1,0:T(8,128)(2,1)S(1)}, u32[]{:S(2)}, u32[]{:S(2)}) collective-permute-start(bf16[16,512]{1,0:T(8,128)(2,1)S(1)} %get-tuple-element.63), channel_id=1, source_target_pairs={{0,16},{16,0},{32,48},{48,32},{64,80},{80,64},{96,112},{112,96},{1... | collective-permute-start | bytes 49160 | tf_op jit(solution)/shard_map/ppermute | solution.py:450
  14.4 2.4 %shard_map.163 = (bf16[64,512]{1,0:T(8,128)(2,1)S(1)}, bf16[384,512]{1,0:T(8,128)(2,1)S(1)}, bf16[64,512]{1,0:T(8,128)(2,1)S(1)}, bf16[384,512]{1,0:T(8,128)(2,1...) custom-call(bf16[16,512]{1,0:T(8,128)(2,1)S(1)} %get-tuple-element.6, ...), custom_call_target="tpu_custom_call" | custom-call | tf_op jit(solution)/shard_map/pallas_call | solution.py:463
  17.0 4.1 %shard_map.164 = (bf16[1,1,64,512]{3,2,1,0:T(8,128)(2,1)}, bf16[1808,512]{1,0:T(8,128)(2,1)S(1)}, bf16[256,512]{1,0:T(8,128)(2,1)S(1)}, bf16[128,512]{1,0:T(8,12...) custom-call(bf16[16,512]{1,0:T(8,128)(2,1)S(1)} %collective-permute-, ...), custom_call_target="tpu_custom_call" | custom-call | tf_op jit(solution)/shard_map/pallas_call | solution.py:486
  21.2 1.3 %collective-permute-start.4 = (bf16[1808,512]{1,0:T(8,128)(2,1)S(1)}, bf16[1808,512]{1,0:T(8,128)(2,1)S(1)}, u32[]{:S(2)}, u32[]{:S(2)}) collective-permute-start(bf16[1808,512]{1,0:T(8,128)(2,1)S(1)} %get-tuple-element.93), channel_id=1, source_target_pairs={{0,16},{16,0},{1,17},{17,1},{2,18},{18,2},{3,19},{19,3},{4,20},{20... | collective-permute-start | bytes 5554184 | tf_op jit(solution)/shard_map/ppermute | solution.py:545
  22.4 1.8 %shard_map.165 = (bf16[1792,512]{1,0:T(8,128)(2,1)S(1)}, bf16[1,1,384,512]{3,2,1,0:T(8,128)(2,1)}, f32[64,512]{1,0:T(8,128)S(1)}, bf16[16,512]{1,0:T(8,128)(2,1)...) custom-call(bf16[64,512]{1,0:T(8,128)(2,1)S(1)} %get-tuple-element.65.node, ...), custom_call_target="tpu_custom_call" | custom-call | flops 1342177280 | bytes 12582912 | tf_op jit(solution)/shard_map/pallas_call | solution.py:496
  24.2 1.7 %collective-permute-done.4.other = bf16[1808,512]{1,0:T(8,128)(2,1)S(1)} collective-permute-done((bf16[1808,512]{1,0:T(8,128)(2,1)S(1)}, bf16[1808,512]{1,0:T(8,128)(2,1)S(1)}, u32[]{:S(2)}, u32[]{:S(2)}) %collective-permute-start.4) | collective-permute-done | bytes 1851424 | tf_op jit(solution)/shard_map/ppermute | solution.py:545
  25.9 0.4 shard_map.166
  26.3 18.5 %all_to_all.33.parts = bf16[8,224,512]{2,1,0:T(8,128)(2,1)S(1)} all-to-all(bf16[8,224,512]{2,1,0:T(8,128)(2,1)S(1)} %bitcast.6), channel_id=1, replica_groups={{0,1,32,33,64,65,96,97},{2,3,34,35,66,67,98,99},{4,5,36,37,68,69,100,10..., dimensions={0} | all-to-all | bytes 3670016 | tf_op jit(solution)/shard_map/all_to_all | solution.py:456
  45.1 8.6 %all_to_all.34.parts = bf16[4,56,512]{2,1,0:T(8,128)(2,1)S(1)} all-to-all(bf16[4,56,512]{2,1,0:T(8,128)(2,1)S(1)} %bitcast.7), channel_id=1, replica_groups={{0,8,128,136},{1,9,129,137},{2,10,130,138},{3,11,131,139},{4,12,132,140..., dimensions={0} | all-to-all | bytes 458752 | tf_op jit(solution)/shard_map/all_to_all | solution.py:456
  53.6 0.7 shard_map.168
  54.4 3.6 %all-to-all-start.2 = ((bf16[4,56,512]{2,1,0:T(8,128)(2,1)}), bf16[4,56,512]{2,1,0:T(8,128)(2,1)S(1)}, u32[]{:S(2)}, u32[]{:S(2)}) async-start(bf16[4,56,512]{2,1,0:T(8,128)(2,1)} %get-tuple-element.98), calls=%async_computation.2 | async-start | bytes 458752 | tf_op jit(solution)/shard_map/all_to_all | solution.py:456
  58.0 2.7 %collective-permute-start.5 = (bf16[16,512]{1,0:T(8,128)(2,1)S(1)}, bf16[16,512]{1,0:T(8,128)(2,1)S(1)}, u32[]{:S(2)}, u32[]{:S(2)}) collective-permute-start(bf16[16,512]{1,0:T(8,128)(2,1)S(1)} %get-tuple-element.101), channel_id=1, source_target_pairs={{1,2},{2,1},{3,4},{4,3},{5,6},{6,5},{7,8},{8,7},{9,10},{10,9},{11,... | collective-permute-start | bytes 49160 | tf_op jit(solution)/shard_map/ppermute | solution.py:450
  60.7 1.9 %collective-permute-start.6 = (bf16[16,512]{1,0:T(8,128)(2,1)S(1)}, bf16[16,512]{1,0:T(8,128)(2,1)S(1)}, u32[]{:S(2)}, u32[]{:S(2)}) collective-permute-start(bf16[16,512]{1,0:T(8,128)(2,1)S(1)} %get-tuple-element.102), channel_id=1, source_target_pairs={{16,32},{32,16},{48,64},{64,48},{80,96},{96,80},{112,128},{128,112... | collective-permute-start | bytes 49160 | tf_op jit(solution)/shard_map/ppermute | solution.py:450
  62.6 3.2 %collective-permute-done.5.ret1 = bf16[16,512]{1,0:T(8,128)(2,1)S(1)} collective-permute-done((bf16[16,512]{1,0:T(8,128)(2,1)S(1)}, bf16[16,512]{1,0:T(8,128)(2,1)S(1)}, u32[]{:S(2)}, u32[]{:S(2)}) %collective-permute-start.5) | collective-permute-done | bytes 16416 | tf_op jit(solution)/shard_map/ppermute | solution.py:450
  65.9 0.9 shard_map.169
  66.8 9.6 %all_to_all.35 = bf16[4,56,512]{2,1,0:T(8,128)(2,1)S(1)} all-to-all(bf16[4,56,512]{2,1,0:T(8,128)(2,1)S(1)} %get-tuple-element.106), channel_id=1, replica_groups={{0,8,128,136},{1,9,129,137},{2,10,130,138},{3,11,131,139},{4,12,132,140..., dimensions={0} | all-to-all | bytes 458752 | tf_op jit(solution)/shard_map/all_to_all | solution.py:456
  76.5 19.2 %all_to_all.36 = bf16[8,224,512]{2,1,0:T(8,128)(2,1)S(1)} all-to-all(bf16[8,224,512]{2,1,0:T(8,128)(2,1)S(1)} %shard_map.170), channel_id=1, replica_groups={{0,1,32,33,64,65,96,97},{2,3,34,35,66,67,98,99},{4,5,36,37,68,69,100,10..., dimensions={0} | all-to-all | bytes 3670016 | tf_op jit(solution)/shard_map/all_to_all | solution.py:456
  95.7 2.3 %collective-permute-start.8 = (bf16[1792,512]{1,0:T(8,128)(2,1)S(1)}, bf16[1792,512]{1,0:T(8,128)(2,1)S(1)}, u32[]{:S(2)}, u32[]{:S(2)}) collective-permute-start(bf16[1792,512]{1,0:T(8,128)(2,1)S(1)} %bitcast.4), channel_id=1, source_target_pairs={{0,16},{16,0},{1,17},{17,1},{2,18},{18,2},{3,19},{19,3},{4,20},{20... | collective-permute-start | bytes 5505032 | tf_op jit(solution)/shard_map/ppermute | solution.py:572
  98.0 1.3 %shard_map.171 = (bf16[1536,512]{1,0:T(8,128)(2,1)}, bf16[512,512]{1,0:T(8,128)(2,1)}, bf16[1024,512]{1,0:T(8,128)(2,1)}, bf16[512,512]{1,0:T(8,128)(2,1)}) custom-call(bf16[1792,512]{1,0:T(8,128)(2,1)S(1)} %bitcast.5), custom_call_target="tpu_custom_call" | custom-call | tf_op jit(solution)/shard_map/pallas_call | solution.py:575
  99.3 2.1 %collective-permute-done.8.half = bf16[1792,512]{1,0:T(8,128)(2,1)S(1)} collective-permute-done((bf16[1792,512]{1,0:T(8,128)(2,1)S(1)}, bf16[1792,512]{1,0:T(8,128)(2,1)S(1)}, u32[]{:S(2)}, u32[]{:S(2)}) %collective-permute-start.8) | collective-permute-done | bytes 1835040 | tf_op jit(solution)/shard_map/ppermute | solution.py:572
  101.4 1.3 %shard_map.172 = (bf16[1536,512]{1,0:T(8,128)(2,1)}, bf16[512,512]{1,0:T(8,128)(2,1)}, bf16[1024,512]{1,0:T(8,128)(2,1)}, bf16[512,512]{1,0:T(8,128)(2,1)}) custom-call(bf16[1792,512]{1,0:T(8,128)(2,1)S(1)} %collective-permute-done.8.half, ...), custom_call_target="tpu_custom_call", output_to_operand_aliasing={{0}: (1, {}), {1}: (2, {}), {2}: (3, {}), {3}: (4, {})} | custom-call | tf_op jit(solution)/shard_map/pallas_call | solution.py:583
  (13 shorter events, 0.5 us)
Async XLA Ops:
  1.7 15.1 %collective-permute-start = (bf16[16,512]{1,0:T(8,128)(2,1)S(1)}, bf16[16,512]{1,0:T(8,128)(2,1)S(1)}, u32[]{:S(2)}, u32[]{:S(2)}) collective-permute-start(bf16[16,512]{1,0:T(8,128)(2,1)S(1)} %get-tuple-element.61), channel_id=1, source_target_pairs={{1,2},{2,1},{3,4},{4,3},{5,6},{6,5},{7,8},{8,7},{9,10},{10,9},{11,... | collective-permute-start | bytes 49160 | tf_op jit(solution)/shard_map/ppermute | solution.py:450
  9.2 7.6 %collective-permute-start.1 = (bf16[16,512]{1,0:T(8,128)(2,1)S(1)}, bf16[16,512]{1,0:T(8,128)(2,1)S(1)}, u32[]{:S(2)}, u32[]{:S(2)}) collective-permute-start(bf16[16,512]{1,0:T(8,128)(2,1)S(1)} %get-tuple-element.62), channel_id=1, source_target_pairs={{16,32},{32,16},{48,64},{64,48},{80,96},{96,80},{112,128},{128,112... | collective-permute-start | bytes 49160 | tf_op jit(solution)/shard_map/ppermute | solution.py:450
  11.3 5.6 %collective-permute-start.2 = (bf16[16,512]{1,0:T(8,128)(2,1)S(1)}, bf16[16,512]{1,0:T(8,128)(2,1)S(1)}, u32[]{:S(2)}, u32[]{:S(2)}) collective-permute-start(bf16[16,512]{1,0:T(8,128)(2,1)S(1)} %get-tuple-element.63), channel_id=1, source_target_pairs={{0,16},{16,0},{32,48},{48,32},{64,80},{80,64},{96,112},{112,96},{1... | collective-permute-start | bytes 49160 | tf_op jit(solution)/shard_map/ppermute | solution.py:450
  14.4 2.6 %collective-permute-start.3 = (bf16[16,512]{1,0:T(8,128)(2,1)S(1)}, bf16[16,512]{1,0:T(8,128)(2,1)S(1)}, u32[]{:S(2)}, u32[]{:S(2)}) collective-permute-start(bf16[16,512]{1,0:T(8,128)(2,1)S(1)} %get-tuple-element.64.packs), channel_id=1, source_target_pairs={{0,1},{1,0},{2,3},{3,2},{4,5},{5,4},{6,7},{7,6},{8,9},{9,8},{10,11... | collective-permute-start | bytes 49160 | tf_op jit(solution)/shard_map/ppermute | solution.py:450
  21.2 4.7 %collective-permute-start.4 = (bf16[1808,512]{1,0:T(8,128)(2,1)S(1)}, bf16[1808,512]{1,0:T(8,128)(2,1)S(1)}, u32[]{:S(2)}, u32[]{:S(2)}) collective-permute-start(bf16[1808,512]{1,0:T(8,128)(2,1)S(1)} %get-tuple-element.93), channel_id=1, source_target_pairs={{0,16},{16,0},{1,17},{17,1},{2,18},{18,2},{3,19},{19,3},{4,20},{20... | collective-permute-start | bytes 5554184 | tf_op jit(solution)/shard_map/ppermute | solution.py:545
  44.8 21.0 %copy-start = (s32[1,1,4,16]{3,2,1,0:T(4,128)S(1)}, s32[1,1,4,16]{3,2,1,0:T(4,128)}, u32[]{:S(2)}) copy-start(s32[1,1,4,16]{3,2,1,0:T(4,128)} %lists.1) | copy-start | bytes 772
  54.4 11.5 %all-to-all-start.2 = ((bf16[4,56,512]{2,1,0:T(8,128)(2,1)}), bf16[4,56,512]{2,1,0:T(8,128)(2,1)S(1)}, u32[]{:S(2)}, u32[]{:S(2)}) async-start(bf16[4,56,512]{2,1,0:T(8,128)(2,1)} %get-tuple-element.98), calls=%async_computation.2 | async-start | bytes 458752 | tf_op jit(solution)/shard_map/all_to_all | solution.py:456
  58.0 7.9 %collective-permute-start.5 = (bf16[16,512]{1,0:T(8,128)(2,1)S(1)}, bf16[16,512]{1,0:T(8,128)(2,1)S(1)}, u32[]{:S(2)}, u32[]{:S(2)}) collective-permute-start(bf16[16,512]{1,0:T(8,128)(2,1)S(1)} %get-tuple-element.101), channel_id=1, source_target_pairs={{1,2},{2,1},{3,4},{4,3},{5,6},{6,5},{7,8},{8,7},{9,10},{10,9},{11,... | collective-permute-start | bytes 49160 | tf_op jit(solution)/shard_map/ppermute | solution.py:450
  60.7 5.2 %collective-permute-start.6 = (bf16[16,512]{1,0:T(8,128)(2,1)S(1)}, bf16[16,512]{1,0:T(8,128)(2,1)S(1)}, u32[]{:S(2)}, u32[]{:S(2)}) collective-permute-start(bf16[16,512]{1,0:T(8,128)(2,1)S(1)} %get-tuple-element.102), channel_id=1, source_target_pairs={{16,32},{32,16},{48,64},{64,48},{80,96},{96,80},{112,128},{128,112... | collective-permute-start | bytes 49160 | tf_op jit(solution)/shard_map/ppermute | solution.py:450
  62.6 3.3 %collective-permute-start.7 = (bf16[16,512]{1,0:T(8,128)(2,1)S(1)}, bf16[16,512]{1,0:T(8,128)(2,1)S(1)}, u32[]{:S(2)}, u32[]{:S(2)}) collective-permute-start(bf16[16,512]{1,0:T(8,128)(2,1)S(1)} %get-tuple-element.103), channel_id=1, source_target_pairs={{0,1},{1,0},{2,3},{3,2},{4,5},{5,4},{6,7},{7,6},{8,9},{9,8},{10,11... | collective-permute-start | bytes 49160 | tf_op jit(solution)/shard_map/ppermute | solution.py:450
  95.7 5.7 %collective-permute-start.8 = (bf16[1792,512]{1,0:T(8,128)(2,1)S(1)}, bf16[1792,512]{1,0:T(8,128)(2,1)S(1)}, u32[]{:S(2)}, u32[]{:S(2)}) collective-permute-start(bf16[1792,512]{1,0:T(8,128)(2,1)S(1)} %bitcast.4), channel_id=1, source_target_pairs={{0,16},{16,0},{1,17},{17,1},{2,18},{18,2},{3,19},{19,3},{4,20},{20... | collective-permute-start | bytes 5505032 | tf_op jit(solution)/shard_map/ppermute | solution.py:572

commit v8 on v7

--- a/solution.py
+++ b/solution.py
@@ -223,8 +223,8 @@
     from_node,
     from_halo,
     z_part,
-    node_next,
     send,
+    next_node,
     ext_twice,
     node_twice,
     a_one,
@@ -263,7 +263,7 @@
     act, slope_three = silu_and_slope(z_three)
     a_three[...] = act.astype(BF)
     n_four, s_four = layer_norm(dot(a_three[...], w_node2[...]))
-    node_next[0, 0] = (lat.astype(F32) + n_four).astype(BF)
+    next_node[...] = (lat.astype(F32) + n_four).astype(BF)
 
     g_node = cot_node[...].astype(F32)
     dz_four[...] = norm_back(g_node, n_four, s_four).astype(BF)
@@ -305,6 +305,7 @@
     node,
     edge,
     w_edge1,
+    next_node,
     ext_twice,
     node_twice,
     a_one,
@@ -319,6 +320,7 @@
     de_new,
     dn_part,
     keep,
+    node_next,
     grad_edges,
     d_node,
     back0,
@@ -326,6 +328,7 @@
     back2,
     d_ext,
 ):
+    node_next[0, 0] = next_node[...]
     odd = parities()
     count, width = node.shape
     rows = back0.shape[0]
@@ -377,42 +380,54 @@
         out[part] = total
 
 
-def far_sum_kernel(factor, parts, d_node, lists, ret0, ret1, ret2, ret3, out, grad_nodes):
+def far_sum_kernel(factor, parts, *refs):
+    returned, out, onward = refs[:3], refs[3], refs[4:]
+    for ret, ref in zip(returned, onward, strict=True):
+        ref[...] = ret[...]
     total = (sum_parts(parts) * factor).astype(BF)
     for part in range(out.shape[0]):
         out[part] = total
+
+
+def spread_kernel(whole, out):
+    rows = whole[...]
+    for part in range(out.shape[0]):
+        out[part] = rows
+
+
+def place_half(side, half, outs, sems):
+    part = outs[0].shape[1] // 2
+    copies = []
+    for out in outs:
+        for block in range(out.shape[0] // (2 * part)):
+            target = pl.multiple_of((2 * block + side) * part, part)
+            start = len(copies) * part
+            copies.append(
+                pltpu.make_async_copy(
+                    half.at[start : start + part], out.at[pl.ds(target, part)], sems.at[len(copies)]
+                )
+            )
+    for copy in copies:
+        copy.start()
+    return copies
+
+
+def own_kernel(half, d_node, lists, ret0, ret1, ret2, ret3, *refs):
+    outs, grad_nodes, sems = refs[:4], refs[4], refs[5]
     odd = parities()
+    copies = place_half(odd[0], half, outs, sems)
     grad = d_node[...]
     for step, ret in zip((CORE_STEP, *CHIP_STEPS), (ret0, ret1, ret2, ret3), strict=True):
         row = lists[0, 0, pl.ds(side_of(step, *odd), 1), :]
         grad = grad + dot(pick(row, grad.shape[0]).astype(BF), ret[...])
     grad_nodes[0, 0] = grad.astype(BF)
-
-
-def spread_kernel(whole, out):
-    rows = whole[...]
-    for part in range(out.shape[0]):
-        out[part] = rows
-
-
-def place_kernel(other_core, half, *refs):
+    for copy in copies:
+        copy.wait()
+
+
+def other_kernel(half, *refs):
     outs, sems = refs[-5:-1], refs[-1]
-    part = outs[0].shape[1] // 2
-    side = lax.axis_index("c")
-    side = 1 - side if other_core else side
-    copies = []
-    for out in outs:
-        for block in range(out.shape[0] // (2 * part)):
-            place = pl.multiple_of((2 * block + side) * part, part)
-            start = len(copies) * part
-            copies.append(
-                pltpu.make_async_copy(
-                    half.at[start : start + part], out.at[pl.ds(place, part)], sems.at[len(copies)]
-                )
-            )
-    for copy in copies:
-        copy.start()
-    for copy in copies:
+    for copy in place_half(1 - parities()[0], half, outs, sems):
         copy.wait()
 
 
@@ -483,9 +498,9 @@
     reach = count + 4 * rows
     half = sum(w.shape[0] for w in loaded[4:8]) // 2
     on_edges, on_nodes = shape((lines, width)), shape((count, width))
-    node_next, send, *state = call(
+    send, *state = call(
         layer_kernel,
-        [shape((1, 1, count, width)), shape((half + rows, width))]
+        [shape((half + rows, width)), on_nodes]
         + [shape((2 * reach, width)), shape((2 * count, width)), on_edges, on_nodes, on_nodes]
         + [on_edges, on_edges, on_nodes, on_nodes]
         + [shape((2 * reach, width)), shape((2 * count, width))]
@@ -493,9 +508,10 @@
         [VMEM] * (4 + len(loaded)),
         limit=16,
     )(*halos, *loaded)
-    keep, grad_edges, d_node, *backs = call(
+    keep, node_next, grad_edges, d_node, *backs = call(
         rest_kernel,
-        [shape((half, width)), shape((1, 1, lines, width)), shape((count, width), F32)]
+        [shape((half, width)), shape((1, 1, count, width)), shape((1, 1, lines, width))]
+        + [shape((count, width), F32)]
         + [shape((rows, width))] * 3,
         [VMEM] * (3 + len(state)),
         limit=12,
@@ -560,33 +576,34 @@
     )(pieces, *backs)
     returned = exchange(backs, CHIP_STEPS)
     pieces = swap(pieces, far)
-    pieces, grad_nodes = call(
+    pieces, *returned = call(
         functools.partial(far_sum_kernel, factor),
-        [shape((n_ring, strip, width)), shape(nodes.shape)],
-        [VMEM] * 7,
+        [shape((n_ring, strip, width))] + block[:3],
+        [VMEM] * 4,
         limit=8,
-    )(pieces, d_node, send_lists, core_back, *returned)
+    )(pieces, *returned)
     pieces = swap(pieces, ring).reshape(mid, width)
     pieces = call(spread_kernel, shape((n_near, mid, width)), [VMEM], limit=8)(pieces)
     mine = swap(pieces, near).reshape(total // 2, width)
     other = lax.ppermute(mine, "c", pairs(2, 0))
     outs = [shape(w.shape) for w in weights]
+    small = pltpu.CompilerParams(vmem_limit_bytes=4 << 20)
     sems = [pltpu.SemaphoreType.DMA((total // width,))]
+    *grads, grad_nodes = pl.pallas_call(
+        own_kernel,
+        out_shape=outs + [shape(nodes.shape)],
+        in_specs=[VMEM] * 7,
+        out_specs=[ANY] * 4 + [VMEM],
+        scratch_shapes=sems,
+        compiler_params=small,
+    )(mine, d_node, send_lists, core_back, *returned)
     grads = pl.pallas_call(
-        functools.partial(place_kernel, False),
-        out_shape=outs,
-        in_specs=[VMEM],
-        out_specs=[ANY] * 4,
-        scratch_shapes=sems,
-        compiler_params=pltpu.CompilerParams(vmem_limit_bytes=4 << 20),
-    )(mine)
-    grads = pl.pallas_call(
-        functools.partial(place_kernel, True),
+        other_kernel,
         out_shape=outs,
         in_specs=[VMEM] + [ANY] * 4,
         out_specs=[ANY] * 4,
         scratch_shapes=sems,
-        compiler_params=pltpu.CompilerParams(vmem_limit_bytes=4 << 20),
+        compiler_params=small,
         input_output_aliases={1: 0, 2: 1, 3: 2, 4: 3},
     )(other, *grads)
     return (node_next, grad_nodes, grad_edges, *grads)

time: 103 us -> 102 us (level)
  transfers between devices with their start and end apart: 10 -> 10, of which waited for: 4 -> 4; matrix products, arithmetic and copies ran while one was open for 0% -> 0% of each run, Pallas kernels for 5% -> 6%
where the time goes in v8:
time: 102 us
  blocking collectives  56 us (55%)
  starting transfers between devices  24.6 us (24%)
  Pallas kernels  14.3 us (14%)
  waiting for transfers between devices  6.38 us (6%)
    all_to_all x4, blocking collectives, swap(): return lax.all_to_all(rows, ALL, 0, 0, axis_index_groups=groups, tiled=True)  56 us
    ppermute x7, starting transfers between devices, exchange(): lax.ppermute(block, axes[step], pairs(lax.axis_size(axes[step]), first[st...  17.4 us
    pallas_call x1, Pallas kernels, layer(): call(layer_kernel, [shape((half + rows, width)), on_nodes] + [shape((2 *...  4.12 us
    all_to_all x1, starting transfers between devices, swap(): return lax.all_to_all(rows, ALL, 0, 0, axis_index_groups=groups, tiled=True)  3.63 us
    ppermute x7, waiting for transfers between devices, exchange(): lax.ppermute(block, axes[step], pairs(lax.axis_size(axes[step]), first[st...  3.41 us
    pallas_call x1, Pallas kernels, load(): call(load_kernel, [shape((count, width)), shape((lines, width))] * 2 + [s...  2.39 us
    ppermute x1, starting transfers between devices, local(): other = lax.ppermute(mine, 'c', pairs(2, 0))  2.27 us
  transfers between devices with their start and end apart: 10, of which 4 were waited for; matrix products, arithmetic and copies ran while one was open for 0% of the time, Pallas kernels for 6%

profile of v8, /device:TPU:1, one launch (start us, length us, event | category | flops | bytes accessed | tf_op | source)
XLA Modules:
  0.0 101.9 jit_solution(12763854351781259942)
XLA Ops:
  0.6 1.1 %shard_map.162 = (bf16[16,512]{1,0:T(8,128)(2,1)S(1)}, bf16[16,512]{1,0:T(8,128)(2,1)S(1)}, bf16[16,512]{1,0:T(8,128)(2,1)S(1)}, bf16[16,512]{1,0:T(8,128)(2,1)S(1)}) custom-call(bf16[1,1,64,512]{3,2,1,0:T(8,128)(2,1)} %nodes_hbm.3, s32[1,1,4,16]{3,2,1,0:T(4,128)} %lists.1), custom_call_target="tpu_custom_call" | custom-call | tf_op jit(solution)/shard_map/pallas_call | solution.py:547
  1.7 7.5 %collective-permute-start = (bf16[16,512]{1,0:T(8,128)(2,1)S(1)}, bf16[16,512]{1,0:T(8,128)(2,1)S(1)}, u32[]{:S(2)}, u32[]{:S(2)}) collective-permute-start(bf16[16,512]{1,0:T(8,128)(2,1)S(1)} %get-tuple-element.69), channel_id=1, source_target_pairs={{1,2},{2,1},{3,4},{4,3},{5,6},{6,5},{7,8},{8,7},{9,10},{10,9},{11,... | collective-permute-start | bytes 49160 | tf_op jit(solution)/shard_map/ppermute | solution.py:465
  9.2 2.1 %collective-permute-start.1 = (bf16[16,512]{1,0:T(8,128)(2,1)S(1)}, bf16[16,512]{1,0:T(8,128)(2,1)S(1)}, u32[]{:S(2)}, u32[]{:S(2)}) collective-permute-start(bf16[16,512]{1,0:T(8,128)(2,1)S(1)} %get-tuple-element.70), channel_id=1, source_target_pairs={{16,32},{32,16},{48,64},{64,48},{80,96},{96,80},{112,128},{128,112... | collective-permute-start | bytes 49160 | tf_op jit(solution)/shard_map/ppermute | solution.py:465
  11.3 3.2 %collective-permute-start.2 = (bf16[16,512]{1,0:T(8,128)(2,1)S(1)}, bf16[16,512]{1,0:T(8,128)(2,1)S(1)}, u32[]{:S(2)}, u32[]{:S(2)}) collective-permute-start(bf16[16,512]{1,0:T(8,128)(2,1)S(1)} %get-tuple-element.71), channel_id=1, source_target_pairs={{0,16},{16,0},{32,48},{48,32},{64,80},{80,64},{96,112},{112,96},{1... | collective-permute-start | bytes 49160 | tf_op jit(solution)/shard_map/ppermute | solution.py:465
  14.4 2.4 %shard_map.163 = (bf16[64,512]{1,0:T(8,128)(2,1)S(1)}, bf16[384,512]{1,0:T(8,128)(2,1)S(1)}, bf16[64,512]{1,0:T(8,128)(2,1)S(1)}, bf16[384,512]{1,0:T(8,128)(2,1...) custom-call(bf16[16,512]{1,0:T(8,128)(2,1)S(1)} %get-tuple-element.6, ...), custom_call_target="tpu_custom_call" | custom-call | tf_op jit(solution)/shard_map/pallas_call | solution.py:478
  17.0 4.1 %shard_map.164 = (bf16[1808,512]{1,0:T(8,128)(2,1)S(1)}, bf16[64,512]{1,0:T(8,128)(2,1)S(1)}, bf16[256,512]{1,0:T(8,128)(2,1)S(1)}, bf16[128,512]{1,0:T(8,128)(2...) custom-call(bf16[16,512]{1,0:T(8,128)(2,1)S(1)} %collective-permute-, ...), custom_call_target="tpu_custom_call" | custom-call | tf_op jit(solution)/shard_map/pallas_call | solution.py:501
  21.1 1.3 %collective-permute-start.4 = (bf16[1808,512]{1,0:T(8,128)(2,1)S(1)}, bf16[1808,512]{1,0:T(8,128)(2,1)S(1)}, u32[]{:S(2)}, u32[]{:S(2)}) collective-permute-start(bf16[1808,512]{1,0:T(8,128)(2,1)S(1)} %get-tuple-element.98), channel_id=1, source_target_pairs={{0,16},{16,0},{1,17},{17,1},{2,18},{18,2},{3,19},{19,3},{4,20},{20... | collective-permute-start | bytes 5554184 | tf_op jit(solution)/shard_map/ppermute | solution.py:561
  22.4 1.9 %shard_map.165 = (bf16[1792,512]{1,0:T(8,128)(2,1)S(1)}, bf16[1,1,64,512]{3,2,1,0:T(8,128)(2,1)}, bf16[1,1,384,512]{3,2,1,0:T(8,128)(2,1)}, f32[64,512]{1,0:T(8,...) custom-call(bf16[64,512]{1,0:T(8,128)(2,1)S(1)} %get-tuple-element.66.node, ...), custom_call_target="tpu_custom_call" | custom-call | flops 1342177280 | bytes 12582912 | tf_op jit(solution)/shard_map/pallas_call | solution.py:511
  24.4 1.5 %collective-permute-done.4.other = bf16[1808,512]{1,0:T(8,128)(2,1)S(1)} collective-permute-done((bf16[1808,512]{1,0:T(8,128)(2,1)S(1)}, bf16[1808,512]{1,0:T(8,128)(2,1)S(1)}, u32[]{:S(2)}, u32[]{:S(2)}) %collective-permute-start.4) | collective-permute-done | bytes 1851424 | tf_op jit(solution)/shard_map/ppermute | solution.py:561
  25.9 0.4 shard_map.166
  26.3 18.5 %all_to_all.33.parts = bf16[8,224,512]{2,1,0:T(8,128)(2,1)S(1)} all-to-all(bf16[8,224,512]{2,1,0:T(8,128)(2,1)S(1)} %bitcast.6), channel_id=1, replica_groups={{0,1,32,33,64,65,96,97},{2,3,34,35,66,67,98,99},{4,5,36,37,68,69,100,10..., dimensions={0} | all-to-all | bytes 3670016 | tf_op jit(solution)/shard_map/all_to_all | solution.py:471
  44.8 0.2 shard_map.167
  45.1 8.6 %all_to_all.34.parts = bf16[4,56,512]{2,1,0:T(8,128)(2,1)S(1)} all-to-all(bf16[4,56,512]{2,1,0:T(8,128)(2,1)S(1)} %bitcast.7), channel_id=1, replica_groups={{0,8,128,136},{1,9,129,137},{2,10,130,138},{3,11,131,139},{4,12,132,140..., dimensions={0} | all-to-all | bytes 458752 | tf_op jit(solution)/shard_map/all_to_all | solution.py:471
  53.6 0.7 shard_map.168
  54.4 3.6 %all-to-all-start.2 = ((bf16[4,56,512]{2,1,0:T(8,128)(2,1)}), bf16[4,56,512]{2,1,0:T(8,128)(2,1)S(1)}, u32[]{:S(2)}, u32[]{:S(2)}) async-start(bf16[4,56,512]{2,1,0:T(8,128)(2,1)} %get-tuple-element.103), calls=%async_computation.2 | async-start | bytes 458752 | tf_op jit(solution)/shard_map/all_to_all | solution.py:471
  58.0 2.7 %collective-permute-start.5 = (bf16[16,512]{1,0:T(8,128)(2,1)S(1)}, bf16[16,512]{1,0:T(8,128)(2,1)S(1)}, u32[]{:S(2)}, u32[]{:S(2)}) collective-permute-start(bf16[16,512]{1,0:T(8,128)(2,1)S(1)} %get-tuple-element.104), channel_id=1, source_target_pairs={{1,2},{2,1},{3,4},{4,3},{5,6},{6,5},{7,8},{8,7},{9,10},{10,9},{11,... | collective-permute-start | bytes 49160 | tf_op jit(solution)/shard_map/ppermute | solution.py:465
  60.7 1.9 %collective-permute-start.6 = (bf16[16,512]{1,0:T(8,128)(2,1)S(1)}, bf16[16,512]{1,0:T(8,128)(2,1)S(1)}, u32[]{:S(2)}, u32[]{:S(2)}) collective-permute-start(bf16[16,512]{1,0:T(8,128)(2,1)S(1)} %get-tuple-element.105), channel_id=1, source_target_pairs={{16,32},{32,16},{48,64},{64,48},{80,96},{96,80},{112,128},{128,112... | collective-permute-start | bytes 49160 | tf_op jit(solution)/shard_map/ppermute | solution.py:465
  62.6 3.2 %collective-permute-done.5.refs_0_ = bf16[16,512]{1,0:T(8,128)(2,1)S(1)} collective-permute-done((bf16[16,512]{1,0:T(8,128)(2,1)S(1)}, bf16[16,512]{1,0:T(8,128)(2,1)S(1)}, u32[]{:S(2)}, u32[]{:S(2)}) %collective-permute-start.5) | collective-permute-done | bytes 16416 | tf_op jit(solution)/shard_map/ppermute | solution.py:465
  66.0 9.6 %all_to_all.35 = bf16[4,56,512]{2,1,0:T(8,128)(2,1)S(1)} all-to-all(bf16[4,56,512]{2,1,0:T(8,128)(2,1)S(1)} %get-tuple-element.107), channel_id=1, replica_groups={{0,8,128,136},{1,9,129,137},{2,10,130,138},{3,11,131,139},{4,12,132,140..., dimensions={0} | all-to-all | bytes 458752 | tf_op jit(solution)/shard_map/all_to_all | solution.py:471
  75.7 19.2 %all_to_all.36 = bf16[8,224,512]{2,1,0:T(8,128)(2,1)S(1)} all-to-all(bf16[8,224,512]{2,1,0:T(8,128)(2,1)S(1)} %shard_map.170), channel_id=1, replica_groups={{0,1,32,33,64,65,96,97},{2,3,34,35,66,67,98,99},{4,5,36,37,68,69,100,10..., dimensions={0} | all-to-all | bytes 3670016 | tf_op jit(solution)/shard_map/all_to_all | solution.py:471
  95.0 2.3 %collective-permute-start.8 = (bf16[1792,512]{1,0:T(8,128)(2,1)S(1)}, bf16[1792,512]{1,0:T(8,128)(2,1)S(1)}, u32[]{:S(2)}, u32[]{:S(2)}) collective-permute-start(bf16[1792,512]{1,0:T(8,128)(2,1)S(1)} %bitcast.4), channel_id=1, source_target_pairs={{0,16},{16,0},{1,17},{17,1},{2,18},{18,2},{3,19},{19,3},{4,20},{20... | collective-permute-start | bytes 5505032 | tf_op jit(solution)/shard_map/ppermute | solution.py:588
  97.2 1.9 %shard_map.171 = (bf16[1536,512]{1,0:T(8,128)(2,1)}, bf16[512,512]{1,0:T(8,128)(2,1)}, bf16[1024,512]{1,0:T(8,128)(2,1)}, bf16[512,512]{1,0:T(8,128)(2,1)}, bf16[1,1,64,512]{3,2,1,0:T(8,128)(2,1)}) custom-call(bf16[1792,512]{1,0:T(8,128)(2,1)S(1)} %bitcast.5, f32[64,512]{1,0:T(8,128)S(1)} %get-tuple-element.108.d_node, s32[1,1,4,16]{3,2,1,0:T(4,128)S(1)} %copy-done, ...), custom_call_target="tpu_custom_call" | custom-call | tf_op jit(solution)/shard_map/pallas_call | solution.py:592
  99.2 1.5 %collective-permute-done.8.half = bf16[1792,512]{1,0:T(8,128)(2,1)S(1)} collective-permute-done((bf16[1792,512]{1,0:T(8,128)(2,1)S(1)}, bf16[1792,512]{1,0:T(8,128)(2,1)S(1)}, u32[]{:S(2)}, u32[]{:S(2)}) %collective-permute-start.8) | collective-permute-done | bytes 1835040 | tf_op jit(solution)/shard_map/ppermute | solution.py:588
  100.6 1.3 %shard_map.172 = (bf16[1536,512]{1,0:T(8,128)(2,1)}, bf16[512,512]{1,0:T(8,128)(2,1)}, bf16[1024,512]{1,0:T(8,128)(2,1)}, bf16[512,512]{1,0:T(8,128)(2,1)}) custom-call(bf16[1792,512]{1,0:T(8,128)(2,1)S(1)} %collective-permute-done.8.half, ...), custom_call_target="tpu_custom_call", output_to_operand_aliasing={{0}: (1, {}), {1}: (2, {}), {2}: (3, {}), {3}: (4, {})} | custom-call | tf_op jit(solution)/shard_map/pallas_call | solution.py:600
  (13 shorter events, 0.3 us)
Async XLA Ops:
  1.7 15.1 %collective-permute-start = (bf16[16,512]{1,0:T(8,128)(2,1)S(1)}, bf16[16,512]{1,0:T(8,128)(2,1)S(1)}, u32[]{:S(2)}, u32[]{:S(2)}) collective-permute-start(bf16[16,512]{1,0:T(8,128)(2,1)S(1)} %get-tuple-element.69), channel_id=1, source_target_pairs={{1,2},{2,1},{3,4},{4,3},{5,6},{6,5},{7,8},{8,7},{9,10},{10,9},{11,... | collective-permute-start | bytes 49160 | tf_op jit(solution)/shard_map/ppermute | solution.py:465
  9.2 7.6 %collective-permute-start.1 = (bf16[16,512]{1,0:T(8,128)(2,1)S(1)}, bf16[16,512]{1,0:T(8,128)(2,1)S(1)}, u32[]{:S(2)}, u32[]{:S(2)}) collective-permute-start(bf16[16,512]{1,0:T(8,128)(2,1)S(1)} %get-tuple-element.70), channel_id=1, source_target_pairs={{16,32},{32,16},{48,64},{64,48},{80,96},{96,80},{112,128},{128,112... | collective-permute-start | bytes 49160 | tf_op jit(solution)/shard_map/ppermute | solution.py:465
  11.3 5.6 %collective-permute-start.2 = (bf16[16,512]{1,0:T(8,128)(2,1)S(1)}, bf16[16,512]{1,0:T(8,128)(2,1)S(1)}, u32[]{:S(2)}, u32[]{:S(2)}) collective-permute-start(bf16[16,512]{1,0:T(8,128)(2,1)S(1)} %get-tuple-element.71), channel_id=1, source_target_pairs={{0,16},{16,0},{32,48},{48,32},{64,80},{80,64},{96,112},{112,96},{1... | collective-permute-start | bytes 49160 | tf_op jit(solution)/shard_map/ppermute | solution.py:465
  14.4 2.6 %collective-permute-start.3 = (bf16[16,512]{1,0:T(8,128)(2,1)S(1)}, bf16[16,512]{1,0:T(8,128)(2,1)S(1)}, u32[]{:S(2)}, u32[]{:S(2)}) collective-permute-start(bf16[16,512]{1,0:T(8,128)(2,1)S(1)} %get-tuple-element.65.packs), channel_id=1, source_target_pairs={{0,1},{1,0},{2,3},{3,2},{4,5},{5,4},{6,7},{7,6},{8,9},{9,8},{10,11... | collective-permute-start | bytes 49160 | tf_op jit(solution)/shard_map/ppermute | solution.py:465
  21.1 4.7 %collective-permute-start.4 = (bf16[1808,512]{1,0:T(8,128)(2,1)S(1)}, bf16[1808,512]{1,0:T(8,128)(2,1)S(1)}, u32[]{:S(2)}, u32[]{:S(2)}) collective-permute-start(bf16[1808,512]{1,0:T(8,128)(2,1)S(1)} %get-tuple-element.98), channel_id=1, source_target_pairs={{0,16},{16,0},{1,17},{17,1},{2,18},{18,2},{3,19},{19,3},{4,20},{20... | collective-permute-start | bytes 5554184 | tf_op jit(solution)/shard_map/ppermute | solution.py:561
  54.4 11.5 %all-to-all-start.2 = ((bf16[4,56,512]{2,1,0:T(8,128)(2,1)}), bf16[4,56,512]{2,1,0:T(8,128)(2,1)S(1)}, u32[]{:S(2)}, u32[]{:S(2)}) async-start(bf16[4,56,512]{2,1,0:T(8,128)(2,1)} %get-tuple-element.103), calls=%async_computation.2 | async-start | bytes 458752 | tf_op jit(solution)/shard_map/all_to_all | solution.py:471
  58.0 7.9 %collective-permute-start.5 = (bf16[16,512]{1,0:T(8,128)(2,1)S(1)}, bf16[16,512]{1,0:T(8,128)(2,1)S(1)}, u32[]{:S(2)}, u32[]{:S(2)}) collective-permute-start(bf16[16,512]{1,0:T(8,128)(2,1)S(1)} %get-tuple-element.104), channel_id=1, source_target_pairs={{1,2},{2,1},{3,4},{4,3},{5,6},{6,5},{7,8},{8,7},{9,10},{10,9},{11,... | collective-permute-start | bytes 49160 | tf_op jit(solution)/shard_map/ppermute | solution.py:465
  60.7 5.2 %collective-permute-start.6 = (bf16[16,512]{1,0:T(8,128)(2,1)S(1)}, bf16[16,512]{1,0:T(8,128)(2,1)S(1)}, u32[]{:S(2)}, u32[]{:S(2)}) collective-permute-start(bf16[16,512]{1,0:T(8,128)(2,1)S(1)} %get-tuple-element.105), channel_id=1, source_target_pairs={{16,32},{32,16},{48,64},{64,48},{80,96},{96,80},{112,128},{128,112... | collective-permute-start | bytes 49160 | tf_op jit(solution)/shard_map/ppermute | solution.py:465
  62.6 3.3 %collective-permute-start.7 = (bf16[16,512]{1,0:T(8,128)(2,1)S(1)}, bf16[16,512]{1,0:T(8,128)(2,1)S(1)}, u32[]{:S(2)}, u32[]{:S(2)}) collective-permute-start(bf16[16,512]{1,0:T(8,128)(2,1)S(1)} %get-tuple-element.106), channel_id=1, source_target_pairs={{0,1},{1,0},{2,3},{3,2},{4,5},{5,4},{6,7},{7,6},{8,9},{9,8},{10,11... | collective-permute-start | bytes 49160 | tf_op jit(solution)/shard_map/ppermute | solution.py:465
  75.7 21.5 %copy-start = (s32[1,1,4,16]{3,2,1,0:T(4,128)S(1)}, s32[1,1,4,16]{3,2,1,0:T(4,128)}, u32[]{:S(2)}) copy-start(s32[1,1,4,16]{3,2,1,0:T(4,128)} %lists.1) | copy-start | bytes 772
  95.0 5.7 %collective-permute-start.8 = (bf16[1792,512]{1,0:T(8,128)(2,1)S(1)}, bf16[1792,512]{1,0:T(8,128)(2,1)S(1)}, u32[]{:S(2)}, u32[]{:S(2)}) collective-permute-start(bf16[1792,512]{1,0:T(8,128)(2,1)S(1)} %bitcast.4), channel_id=1, source_target_pairs={{0,16},{16,0},{1,17},{17,1},{2,18},{18,2},{3,19},{19,3},{4,20},{20... | collective-permute-start | bytes 5505032 | tf_op jit(solution)/shard_map/ppermute | solution.py:588

commit v9 on v8

--- a/solution.py
+++ b/solution.py
@@ -218,7 +218,6 @@
     w_edge2,
     w_node1,
     w_node2,
-    to_ext,
     to_node,
     from_node,
     from_halo,
@@ -230,14 +229,11 @@
     a_one,
     agg,
     a_three,
-    dz_one,
     dz_two,
     dz_three,
     dz_four,
-    sum_send,
-    sum_recv,
     de_new,
-    dn_part,
+    slope_one,
 ):
     odd = parities()
     count, width = node.shape
@@ -254,7 +250,7 @@
 
     terms = hi_lo(dot(ext_twice[count:reach, :], w_edge1[width : 2 * width, :]))
     z_one = z_part[...] + dot(from_halo[...], terms)
-    act, slope_one = silu_and_slope(z_one)
+    act, slope_one[...] = silu_and_slope(z_one)
     a_one[...] = act.astype(BF)
     n_two, s_two = layer_norm(dot(a_one[...], w_edge2[...]))
     e_new = (edge[...].astype(F32) + n_two).astype(BF)
@@ -268,15 +264,40 @@
     g_node = cot_node[...].astype(F32)
     dz_four[...] = norm_back(g_node, n_four, s_four).astype(BF)
     dz_three[...] = (dot_cols(dz_four[...], w_node2[...]) * slope_three).astype(BF)
-    dn_part[...] = g_node + dot_cols(dz_three[...], w_node1[:width, :])
     dy_agg = dot_cols(dz_three[...], w_node1[width:, :])
 
     de = cot_edge[...].astype(F32) + dot(from_node[...], hi_lo(dy_agg))
     de_new[...] = de
     dz_two[...] = norm_back(de, n_two, s_two).astype(BF)
-    dz_one[...] = (dot_cols(dz_two[...], w_edge2[...]) * slope_one).astype(BF)
+    put_half(
+        send,
+        1 - odd[0],
+        ((a_one, dz_two), (node, dz_three), (agg, dz_three), (a_three, dz_four)),
+    )
+
+
+def first_kernel(
+    edge,
+    w_edge1,
+    w_edge2,
+    to_ext,
+    to_node,
+    ext_twice,
+    node_twice,
+    dz_two,
+    slope_one,
+    send,
+    dz_one,
+    sum_send,
+    sum_recv,
+):
+    odd = parities()
+    width = edge.shape[1]
+    reach, count = to_ext.shape[0], to_node.shape[0]
+    dz_one[...] = (dot_cols(dz_two[...], w_edge2[...]) * slope_one[...]).astype(BF)
     sum_send[...] = hi_lo(dot(to_ext[...], dz_one[...]))
     sum_recv[...] = hi_lo(dot(to_node[...], dz_one[...]))
+    rows = (reach - count) // 4
     first = count + side_of(CORE_STEP, *odd) * rows
     ride = jnp.concatenate(
         [
@@ -287,38 +308,29 @@
     )
     send[send.shape[0] - rows :, :] = fold(dot_cols(ride, w_edge1[width : 2 * width, :])).astype(BF)
     put_half(
-        send,
-        1 - odd[0],
-        (
-            (edge, dz_one),
-            (ext_twice, sum_send),
-            (node_twice, sum_recv),
-            (a_one, dz_two),
-            (node, dz_three),
-            (agg, dz_three),
-            (a_three, dz_four),
-        ),
+        send, 1 - odd[0], ((edge, dz_one), (ext_twice, sum_send), (node_twice, sum_recv))
     )
 
 
 def rest_kernel(
     node,
     edge,
+    cot_node,
     w_edge1,
+    w_node1,
     next_node,
     ext_twice,
     node_twice,
     a_one,
     agg,
     a_three,
-    dz_one,
     dz_two,
     dz_three,
     dz_four,
+    de_new,
+    dz_one,
     sum_send,
     sum_recv,
-    de_new,
-    dn_part,
     keep,
     node_next,
     grad_edges,
@@ -348,16 +360,18 @@
     grad_edges[0, 0] = (de_new[...] + dot_cols(dz_one[...], w_edge1[:width, :])).astype(BF)
     d_ext[...] = fold(dot_cols(sum_send[...], w_edge1[width : 2 * width, :]))
     d_recv = fold(dot_cols(sum_recv[...], w_edge1[2 * width :, :]))
-    d_node[...] = dn_part[...] + d_recv + d_ext[:count, :]
+    dy_node = dot_cols(dz_three[...], w_node1[:width, :])
+    d_node[...] = cot_node[...].astype(F32) + dy_node + d_recv + d_ext[:count, :]
     for step, back in zip(CHIP_STEPS, (back0, back1, back2), strict=True):
         place = count + side_of(step, *odd) * rows
         back[...] = d_ext[pl.ds(pl.multiple_of(place, rows), rows), :].astype(BF)
 
 
-def pair_sum_kernel(mine, other, out, ret):
-    rows = mine.shape[0]
-    out[...] = (mine[...].astype(F32) + other[:rows, :].astype(F32)).astype(BF)
-    ret[...] = other[rows:, :]
+def pair_sum_kernel(mine, first, later, out, ret):
+    rows = later.shape[0] - ret.shape[0]
+    out[:rows, :] = (mine[:rows, :].astype(F32) + later[:rows, :].astype(F32)).astype(BF)
+    out[rows:, :] = (mine[rows:, :].astype(F32) + first[...].astype(F32)).astype(BF)
+    ret[...] = later[rows:, :]
 
 
 def sum_parts(parts):
@@ -492,37 +506,51 @@
     )(packs, *in_hbm(nodes, edges, senders, segments, cot_nodes, cot_edges, *weights))
 
 
+def cost(flops):
+    return pl.CostEstimate(flops=flops, bytes_accessed=12 << 20, transcendentals=0)
+
+
 def layer(halos, loaded):
-    node, edge, w_edge1 = loaded[0], loaded[1], loaded[4]
+    node, edge, cot_node, _, w_edge1, w_edge2, w_node1, _, to_ext, to_node = loaded[:10]
     (count, width), lines, rows = node.shape, edge.shape[0], halos[0].shape[0]
     reach = count + 4 * rows
+    later = w_edge1.shape[0] // 2
     half = sum(w.shape[0] for w in loaded[4:8]) // 2
     on_edges, on_nodes = shape((lines, width)), shape((count, width))
-    send, *state = call(
+    on_sums = [shape((2 * reach, width)), shape((2 * count, width))]
+    send_first, *state, slope_one = call(
         layer_kernel,
-        [shape((half + rows, width)), on_nodes]
-        + [shape((2 * reach, width)), shape((2 * count, width)), on_edges, on_nodes, on_nodes]
-        + [on_edges, on_edges, on_nodes, on_nodes]
-        + [shape((2 * reach, width)), shape((2 * count, width))]
-        + [shape((lines, width), F32), shape((count, width), F32)],
-        [VMEM] * (4 + len(loaded)),
+        [shape((half - later, width)), on_nodes]
+        + on_sums
+        + [on_edges, on_nodes, on_nodes, on_edges, on_nodes, on_nodes]
+        + [shape((lines, width), F32)] * 2,
+        [VMEM] * (3 + len(loaded)),
         limit=16,
-    )(*halos, *loaded)
+    )(*halos, *loaded[:8], *loaded[9:])
+    got_first = lax.ppermute(send_first, "c", pairs(2, 0))
+    _, ext_twice, node_twice, _, _, _, dz_two, *_ = state
+    send_later, *more = call(
+        first_kernel,
+        [shape((later + rows, width)), on_edges] + on_sums,
+        [VMEM] * 9,
+        limit=12,
+        cost_estimate=cost(2 * width * width * (2 * lines + 4 * reach)),
+    )(edge, w_edge1, w_edge2, to_ext, to_node, ext_twice, node_twice, dz_two, slope_one)
+    got_later = lax.ppermute(send_later, "c", pairs(2, 0))
     keep, node_next, grad_edges, d_node, *backs = call(
         rest_kernel,
         [shape((half, width)), shape((1, 1, count, width)), shape((1, 1, lines, width))]
         + [shape((count, width), F32)]
         + [shape((rows, width))] * 3,
-        [VMEM] * (3 + len(state)),
+        [VMEM] * (5 + len(state) + len(more)),
         limit=12,
         scratch=[pltpu.VMEM((reach, width), F32)],
-        cost_estimate=pl.CostEstimate(
-            flops=2 * width * width * (4 * lines + 8 * reach),
-            bytes_accessed=12 << 20,
-            transcendentals=0,
-        ),
-    )(node, edge, w_edge1, *state)
-    return node_next, send, keep, grad_edges, d_node, backs
+        cost_estimate=cost(2 * width * width * (4 * lines + 8 * reach)),
+    )(node, edge, cot_node, w_edge1, w_node1, *state, *more)
+    pair, core_back = call(
+        pair_sum_kernel, [shape((half, width)), shape((rows, width))], [VMEM] * 3, limit=8
+    )(keep, got_first, got_later)
+    return node_next, grad_edges, d_node, backs, pair, core_back
 
 
 def local(
@@ -556,12 +584,7 @@
     )(*in_hbm(nodes, send_lists))
     halos = exchange(packs, range(4))
     loaded = load(packs[3], nodes, edges, senders, segments, cot_nodes, cot_edges, weights)
-    node_next, send, keep, grad_edges, d_node, backs = layer(halos, loaded)
-
-    got = lax.ppermute(send, "c", pairs(2, 0))
-    pair, core_back = call(
-        pair_sum_kernel, [shape(keep.shape), shape((rows, width))], [VMEM] * 2, limit=8
-    )(keep, got)
+    node_next, grad_edges, d_node, backs, pair, core_back = layer(halos, loaded)
 
     near, ring, far = groups()
     n_near, n_ring, n_far = len(near[0]), len(ring[0]), len(far[0])

time: 102 us -> 101 us (level)
  waiting for transfers between devices: 6.38 us -> 5.2 us
    ppermute x1 -> x2, waiting for transfers between devices: 1.49 us -> 0.31 us  [the longest x1 0.31 us: layer(): got_later = lax.ppermute(send_later, 'c', pairs(2, 0))]
    pallas_call x2 -> x3, Pallas kernels: 4.53 us -> 4.77 us  [the longest x1 3.27 us: layer(): call(layer_kernel, [shape((half - later, width)), on_nodes] + on_sums + [...]
  transfers between devices with their start and end apart: 10 -> 11, of which waited for: 4 -> 4; matrix products, arithmetic and copies ran while one was open for 0% -> 0% of each run, Pallas kernels for 6% -> 7%
where the time goes in v9:
time: 101 us
  blocking collectives  56 us (55%)
  starting transfers between devices  24.7 us (24%)
  Pallas kernels  14.5 us (14%)
  waiting for transfers between devices  5.2 us (5%)
    all_to_all x4, blocking collectives, swap(): return lax.all_to_all(rows, ALL, 0, 0, axis_index_groups=groups, tiled=True)  56 us
    ppermute x7, starting transfers between devices, exchange(): lax.ppermute(block, axes[step], pairs(lax.axis_size(axes[step]), first[st...  17.4 us
    all_to_all x1, starting transfers between devices, swap(): return lax.all_to_all(rows, ALL, 0, 0, axis_index_groups=groups, tiled=True)  3.63 us
    ppermute x7, waiting for transfers between devices, exchange(): lax.ppermute(block, axes[step], pairs(lax.axis_size(axes[step]), first[st...  3.41 us
    pallas_call x1, Pallas kernels, layer(): call(layer_kernel, [shape((half - later, width)), on_nodes] + on_sums + [...  3.27 us
    pallas_call x1, Pallas kernels, load(): call(load_kernel, [shape((count, width)), shape((lines, width))] * 2 + [s...  2.39 us
    ppermute x1, starting transfers between devices, local(): other = lax.ppermute(mine, 'c', pairs(2, 0))  2.27 us
  transfers between devices with their start and end apart: 11, of which 4 were waited for; matrix products, arithmetic and copies ran while one was open for 0% of the time, Pallas kernels for 7%

profile of v9, /device:TPU:1, one launch (start us, length us, event | category | flops | bytes accessed | tf_op | source)
XLA Modules:
  0.0 101.1 jit_solution(7016602146299614552)
XLA Ops:
  0.6 1.1 %shard_map.162 = (bf16[16,512]{1,0:T(8,128)(2,1)S(1)}, bf16[16,512]{1,0:T(8,128)(2,1)S(1)}, bf16[16,512]{1,0:T(8,128)(2,1)S(1)}, bf16[16,512]{1,0:T(8,128)(2,1)S(1)}) custom-call(bf16[1,1,64,512]{3,2,1,0:T(8,128)(2,1)} %nodes_hbm.3, s32[1,1,4,16]{3,2,1,0:T(4,128)} %lists.1), custom_call_target="tpu_custom_call" | custom-call | tf_op jit(solution)/shard_map/pallas_call | solution.py:575
  1.7 7.5 %collective-permute-start = (bf16[16,512]{1,0:T(8,128)(2,1)S(1)}, bf16[16,512]{1,0:T(8,128)(2,1)S(1)}, u32[]{:S(2)}, u32[]{:S(2)}) collective-permute-start(bf16[16,512]{1,0:T(8,128)(2,1)S(1)} %get-tuple-element.72), channel_id=1, source_target_pairs={{1,2},{2,1},{3,4},{4,3},{5,6},{6,5},{7,8},{8,7},{9,10},{10,9},{11,... | collective-permute-start | bytes 49160 | tf_op jit(solution)/shard_map/ppermute | solution.py:479
  9.2 2.1 %collective-permute-start.1 = (bf16[16,512]{1,0:T(8,128)(2,1)S(1)}, bf16[16,512]{1,0:T(8,128)(2,1)S(1)}, u32[]{:S(2)}, u32[]{:S(2)}) collective-permute-start(bf16[16,512]{1,0:T(8,128)(2,1)S(1)} %get-tuple-element.73), channel_id=1, source_target_pairs={{16,32},{32,16},{48,64},{64,48},{80,96},{96,80},{112,128},{128,112... | collective-permute-start | bytes 49160 | tf_op jit(solution)/shard_map/ppermute | solution.py:479
  11.3 3.2 %collective-permute-start.2 = (bf16[16,512]{1,0:T(8,128)(2,1)S(1)}, bf16[16,512]{1,0:T(8,128)(2,1)S(1)}, u32[]{:S(2)}, u32[]{:S(2)}) collective-permute-start(bf16[16,512]{1,0:T(8,128)(2,1)S(1)} %get-tuple-element.74), channel_id=1, source_target_pairs={{0,16},{16,0},{32,48},{48,32},{64,80},{80,64},{96,112},{112,96},{1... | collective-permute-start | bytes 49160 | tf_op jit(solution)/shard_map/ppermute | solution.py:479
  14.4 2.4 %shard_map.163 = (bf16[64,512]{1,0:T(8,128)(2,1)S(1)}, bf16[384,512]{1,0:T(8,128)(2,1)S(1)}, bf16[64,512]{1,0:T(8,128)(2,1)S(1)}, bf16[384,512]{1,0:T(8,128)(2,1...) custom-call(bf16[16,512]{1,0:T(8,128)(2,1)S(1)} %get-tuple-element.6, ...), custom_call_target="tpu_custom_call" | custom-call | tf_op jit(solution)/shard_map/pallas_call | solution.py:492
  17.0 3.3 %shard_map.164 = (bf16[1024,512]{1,0:T(8,128)(2,1)S(1)}, bf16[64,512]{1,0:T(8,128)(2,1)S(1)}, bf16[256,512]{1,0:T(8,128)(2,1)S(1)}, bf16[128,512]{1,0:T(8,128)(2...) custom-call(bf16[16,512]{1,0:T(8,128)(2,1)S(1)} %collective-permute-, ...), custom_call_target="tpu_custom_call" | custom-call | tf_op jit(solution)/shard_map/pallas_call | solution.py:521
  20.3 1.2 %collective-permute-start.4 = (bf16[1024,512]{1,0:T(8,128)(2,1)S(1)}, bf16[1024,512]{1,0:T(8,128)(2,1)S(1)}, u32[]{:S(2)}, u32[]{:S(2)}) collective-permute-start(bf16[1024,512]{1,0:T(8,128)(2,1)S(1)} %get-tuple-element.99), channel_id=1, source_target_pairs={{0,16},{16,0},{1,17},{17,1},{2,18},{18,2},{3,19},{19,3},{4,20},{20... | collective-permute-start | bytes 3145736 | tf_op jit(solution)/shard_map/ppermute | solution.py:530
  21.5 1.1 %shard_map.165 = (bf16[784,512]{1,0:T(8,128)(2,1)S(1)}, bf16[384,512]{1,0:T(8,128)(2,1)S(1)}, bf16[256,512]{1,0:T(8,128)(2,1)S(1)}, bf16[128,512]{1,0:T(8,128)(2,1)S(1)}) custom-call(bf16[384,512]{1,0:T(8,128)(2,1)S(1)} %get-tuple-element.68.edge, bf16[1536,512]{1,0:T(8,128)(2,1)S(1)} %get-tuple-element.70.w_edge1, ...), custom_call_target="tpu_custom_call" | custom-call | flops 671088640 | bytes 12582912 | tf_op jit(solution)/shard_map/pallas_call | solution.py:532
  22.7 2.0 %shard_map.166 = (bf16[1792,512]{1,0:T(8,128)(2,1)S(1)}, bf16[1,1,64,512]{3,2,1,0:T(8,128)(2,1)}, bf16[1,1,384,512]{3,2,1,0:T(8,128)(2,1)}, f32[64,512]{1,0:T(8,...) custom-call(bf16[64,512]{1,0:T(8,128)(2,1)S(1)} %get-tuple-element.67.node, ...), custom_call_target="tpu_custom_call" | custom-call | flops 1342177280 | bytes 12582912 | tf_op jit(solution)/shard_map/pallas_call | solution.py:540
  24.7 0.3 collective-permute-done.5.later
  25.0 0.4 shard_map.167
  25.5 18.5 %all_to_all.33.parts = bf16[8,224,512]{2,1,0:T(8,128)(2,1)S(1)} all-to-all(bf16[8,224,512]{2,1,0:T(8,128)(2,1)S(1)} %bitcast.6), channel_id=1, replica_groups={{0,1,32,33,64,65,96,97},{2,3,34,35,66,67,98,99},{4,5,36,37,68,69,100,10..., dimensions={0} | all-to-all | bytes 3670016 | tf_op jit(solution)/shard_map/all_to_all | solution.py:485
  44.2 8.6 %all_to_all.34.parts = bf16[4,56,512]{2,1,0:T(8,128)(2,1)S(1)} all-to-all(bf16[4,56,512]{2,1,0:T(8,128)(2,1)S(1)} %bitcast.7), channel_id=1, replica_groups={{0,8,128,136},{1,9,129,137},{2,10,130,138},{3,11,131,139},{4,12,132,140..., dimensions={0} | all-to-all | bytes 458752 | tf_op jit(solution)/shard_map/all_to_all | solution.py:485
  52.8 0.7 shard_map.169
  53.5 3.6 %all-to-all-start.2 = ((bf16[4,56,512]{2,1,0:T(8,128)(2,1)}), bf16[4,56,512]{2,1,0:T(8,128)(2,1)S(1)}, u32[]{:S(2)}, u32[]{:S(2)}) async-start(bf16[4,56,512]{2,1,0:T(8,128)(2,1)} %get-tuple-element.105), calls=%async_computation.2 | async-start | bytes 458752 | tf_op jit(solution)/shard_map/all_to_all | solution.py:485
  57.1 2.7 %collective-permute-start.6 = (bf16[16,512]{1,0:T(8,128)(2,1)S(1)}, bf16[16,512]{1,0:T(8,128)(2,1)S(1)}, u32[]{:S(2)}, u32[]{:S(2)}) collective-permute-start(bf16[16,512]{1,0:T(8,128)(2,1)S(1)} %get-tuple-element.106), channel_id=1, source_target_pairs={{1,2},{2,1},{3,4},{4,3},{5,6},{6,5},{7,8},{8,7},{9,10},{10,9},{11,... | collective-permute-start | bytes 49160 | tf_op jit(solution)/shard_map/ppermute | solution.py:479
  59.9 2.0 %collective-permute-start.7 = (bf16[16,512]{1,0:T(8,128)(2,1)S(1)}, bf16[16,512]{1,0:T(8,128)(2,1)S(1)}, u32[]{:S(2)}, u32[]{:S(2)}) collective-permute-start(bf16[16,512]{1,0:T(8,128)(2,1)S(1)} %get-tuple-element.107), channel_id=1, source_target_pairs={{16,32},{32,16},{48,64},{64,48},{80,96},{96,80},{112,128},{128,112... | collective-permute-start | bytes 49160 | tf_op jit(solution)/shard_map/ppermute | solution.py:479
  61.8 3.2 %collective-permute-done.6.refs_0_ = bf16[16,512]{1,0:T(8,128)(2,1)S(1)} collective-permute-done((bf16[16,512]{1,0:T(8,128)(2,1)S(1)}, bf16[16,512]{1,0:T(8,128)(2,1)S(1)}, u32[]{:S(2)}, u32[]{:S(2)}) %collective-permute-start.6) | collective-permute-done | bytes 16416 | tf_op jit(solution)/shard_map/ppermute | solution.py:479
  65.1 9.6 %all_to_all.35 = bf16[4,56,512]{2,1,0:T(8,128)(2,1)S(1)} all-to-all(bf16[4,56,512]{2,1,0:T(8,128)(2,1)S(1)} %get-tuple-element.109), channel_id=1, replica_groups={{0,8,128,136},{1,9,129,137},{2,10,130,138},{3,11,131,139},{4,12,132,140..., dimensions={0} | all-to-all | bytes 458752 | tf_op jit(solution)/shard_map/all_to_all | solution.py:485
  74.9 19.2 %all_to_all.36 = bf16[8,224,512]{2,1,0:T(8,128)(2,1)S(1)} all-to-all(bf16[8,224,512]{2,1,0:T(8,128)(2,1)S(1)} %shard_map.171), channel_id=1, replica_groups={{0,1,32,33,64,65,96,97},{2,3,34,35,66,67,98,99},{4,5,36,37,68,69,100,10..., dimensions={0} | all-to-all | bytes 3670016 | tf_op jit(solution)/shard_map/all_to_all | solution.py:485
  94.2 2.3 %collective-permute-start.9 = (bf16[1792,512]{1,0:T(8,128)(2,1)S(1)}, bf16[1792,512]{1,0:T(8,128)(2,1)S(1)}, u32[]{:S(2)}, u32[]{:S(2)}) collective-permute-start(bf16[1792,512]{1,0:T(8,128)(2,1)S(1)} %bitcast.4), channel_id=1, source_target_pairs={{0,16},{16,0},{1,17},{17,1},{2,18},{18,2},{3,19},{19,3},{4,20},{20... | collective-permute-start | bytes 5505032 | tf_op jit(solution)/shard_map/ppermute | solution.py:611
  96.4 1.9 %shard_map.172 = (bf16[1536,512]{1,0:T(8,128)(2,1)}, bf16[512,512]{1,0:T(8,128)(2,1)}, bf16[1024,512]{1,0:T(8,128)(2,1)}, bf16[512,512]{1,0:T(8,128)(2,1)}, bf16[1,1,64,512]{3,2,1,0:T(8,128)(2,1)}) custom-call(bf16[1792,512]{1,0:T(8,128)(2,1)S(1)} %bitcast.5, f32[64,512]{1,0:T(8,128)S(1)} %get-tuple-element.110.d_node, s32[1,1,4,16]{3,2,1,0:T(4,128)S(1)} %copy-done, ...), custom_call_target="tpu_custom_call" | custom-call | tf_op jit(solution)/shard_map/pallas_call | solution.py:615
  98.4 1.5 %collective-permute-done.9.half = bf16[1792,512]{1,0:T(8,128)(2,1)S(1)} collective-permute-done((bf16[1792,512]{1,0:T(8,128)(2,1)S(1)}, bf16[1792,512]{1,0:T(8,128)(2,1)S(1)}, u32[]{:S(2)}, u32[]{:S(2)}) %collective-permute-start.9) | collective-permute-done | bytes 1835040 | tf_op jit(solution)/shard_map/ppermute | solution.py:611
  99.8 1.3 %shard_map.173 = (bf16[1536,512]{1,0:T(8,128)(2,1)}, bf16[512,512]{1,0:T(8,128)(2,1)}, bf16[1024,512]{1,0:T(8,128)(2,1)}, bf16[512,512]{1,0:T(8,128)(2,1)}) custom-call(bf16[1792,512]{1,0:T(8,128)(2,1)S(1)} %collective-permute-done.9.half, ...), custom_call_target="tpu_custom_call", output_to_operand_aliasing={{0}: (1, {}), {1}: (2, {}), {2}: (3, {}), {3}: (4, {})} | custom-call | tf_op jit(solution)/shard_map/pallas_call | solution.py:623
  (16 shorter events, 0.7 us)
Async XLA Ops:
  1.7 15.1 %collective-permute-start = (bf16[16,512]{1,0:T(8,128)(2,1)S(1)}, bf16[16,512]{1,0:T(8,128)(2,1)S(1)}, u32[]{:S(2)}, u32[]{:S(2)}) collective-permute-start(bf16[16,512]{1,0:T(8,128)(2,1)S(1)} %get-tuple-element.72), channel_id=1, source_target_pairs={{1,2},{2,1},{3,4},{4,3},{5,6},{6,5},{7,8},{8,7},{9,10},{10,9},{11,... | collective-permute-start | bytes 49160 | tf_op jit(solution)/shard_map/ppermute | solution.py:479
  9.2 7.6 %collective-permute-start.1 = (bf16[16,512]{1,0:T(8,128)(2,1)S(1)}, bf16[16,512]{1,0:T(8,128)(2,1)S(1)}, u32[]{:S(2)}, u32[]{:S(2)}) collective-permute-start(bf16[16,512]{1,0:T(8,128)(2,1)S(1)} %get-tuple-element.73), channel_id=1, source_target_pairs={{16,32},{32,16},{48,64},{64,48},{80,96},{96,80},{112,128},{128,112... | collective-permute-start | bytes 49160 | tf_op jit(solution)/shard_map/ppermute | solution.py:479
  11.3 5.6 %collective-permute-start.2 = (bf16[16,512]{1,0:T(8,128)(2,1)S(1)}, bf16[16,512]{1,0:T(8,128)(2,1)S(1)}, u32[]{:S(2)}, u32[]{:S(2)}) collective-permute-start(bf16[16,512]{1,0:T(8,128)(2,1)S(1)} %get-tuple-element.74), channel_id=1, source_target_pairs={{0,16},{16,0},{32,48},{48,32},{64,80},{80,64},{96,112},{112,96},{1... | collective-permute-start | bytes 49160 | tf_op jit(solution)/shard_map/ppermute | solution.py:479
  14.4 2.6 %collective-permute-start.3 = (bf16[16,512]{1,0:T(8,128)(2,1)S(1)}, bf16[16,512]{1,0:T(8,128)(2,1)S(1)}, u32[]{:S(2)}, u32[]{:S(2)}) collective-permute-start(bf16[16,512]{1,0:T(8,128)(2,1)S(1)} %get-tuple-element.66.packs), channel_id=1, source_target_pairs={{0,1},{1,0},{2,3},{3,2},{4,5},{5,4},{6,7},{7,6},{8,9},{9,8},{10,11... | collective-permute-start | bytes 49160 | tf_op jit(solution)/shard_map/ppermute | solution.py:479
  20.3 4.7 %collective-permute-start.4 = (bf16[1024,512]{1,0:T(8,128)(2,1)S(1)}, bf16[1024,512]{1,0:T(8,128)(2,1)S(1)}, u32[]{:S(2)}, u32[]{:S(2)}) collective-permute-start(bf16[1024,512]{1,0:T(8,128)(2,1)S(1)} %get-tuple-element.99), channel_id=1, source_target_pairs={{0,16},{16,0},{1,17},{17,1},{2,18},{18,2},{3,19},{19,3},{4,20},{20... | collective-permute-start | bytes 3145736 | tf_op jit(solution)/shard_map/ppermute | solution.py:530
  22.6 2.4 %collective-permute-start.5 = (bf16[784,512]{1,0:T(8,128)(2,1)S(1)}, bf16[784,512]{1,0:T(8,128)(2,1)S(1)}, u32[]{:S(2)}, u32[]{:S(2)}) collective-permute-start(bf16[784,512]{1,0:T(8,128)(2,1)S(1)} %get-tuple-element.100), channel_id=1, source_target_pairs={{0,16},{16,0},{1,17},{17,1},{2,18},{18,2},{3,19},{19,3},{4,20},{20... | collective-permute-start | bytes 2408456 | tf_op jit(solution)/shard_map/ppermute | solution.py:539
  53.5 11.6 %all-to-all-start.2 = ((bf16[4,56,512]{2,1,0:T(8,128)(2,1)}), bf16[4,56,512]{2,1,0:T(8,128)(2,1)S(1)}, u32[]{:S(2)}, u32[]{:S(2)}) async-start(bf16[4,56,512]{2,1,0:T(8,128)(2,1)} %get-tuple-element.105), calls=%async_computation.2 | async-start | bytes 458752 | tf_op jit(solution)/shard_map/all_to_all | solution.py:485
  57.1 7.9 %collective-permute-start.6 = (bf16[16,512]{1,0:T(8,128)(2,1)S(1)}, bf16[16,512]{1,0:T(8,128)(2,1)S(1)}, u32[]{:S(2)}, u32[]{:S(2)}) collective-permute-start(bf16[16,512]{1,0:T(8,128)(2,1)S(1)} %get-tuple-element.106), channel_id=1, source_target_pairs={{1,2},{2,1},{3,4},{4,3},{5,6},{6,5},{7,8},{8,7},{9,10},{10,9},{11,... | collective-permute-start | bytes 49160 | tf_op jit(solution)/shard_map/ppermute | solution.py:479
  59.9 5.2 %collective-permute-start.7 = (bf16[16,512]{1,0:T(8,128)(2,1)S(1)}, bf16[16,512]{1,0:T(8,128)(2,1)S(1)}, u32[]{:S(2)}, u32[]{:S(2)}) collective-permute-start(bf16[16,512]{1,0:T(8,128)(2,1)S(1)} %get-tuple-element.107), channel_id=1, source_target_pairs={{16,32},{32,16},{48,64},{64,48},{80,96},{96,80},{112,128},{128,112... | collective-permute-start | bytes 49160 | tf_op jit(solution)/shard_map/ppermute | solution.py:479
  61.8 3.3 %collective-permute-start.8 = (bf16[16,512]{1,0:T(8,128)(2,1)S(1)}, bf16[16,512]{1,0:T(8,128)(2,1)S(1)}, u32[]{:S(2)}, u32[]{:S(2)}) collective-permute-start(bf16[16,512]{1,0:T(8,128)(2,1)S(1)} %get-tuple-element.108), channel_id=1, source_target_pairs={{0,1},{1,0},{2,3},{3,2},{4,5},{5,4},{6,7},{7,6},{8,9},{9,8},{10,11... | collective-permute-start | bytes 49160 | tf_op jit(solution)/shard_map/ppermute | solution.py:479
  74.9 21.5 %copy-start = (s32[1,1,4,16]{3,2,1,0:T(4,128)S(1)}, s32[1,1,4,16]{3,2,1,0:T(4,128)}, u32[]{:S(2)}) copy-start(s32[1,1,4,16]{3,2,1,0:T(4,128)} %lists.1) | copy-start | bytes 772
  94.2 5.7 %collective-permute-start.9 = (bf16[1792,512]{1,0:T(8,128)(2,1)S(1)}, bf16[1792,512]{1,0:T(8,128)(2,1)S(1)}, u32[]{:S(2)}, u32[]{:S(2)}) collective-permute-start(bf16[1792,512]{1,0:T(8,128)(2,1)S(1)} %bitcast.4), channel_id=1, source_target_pairs={{0,16},{16,0},{1,17},{17,1},{2,18},{18,2},{3,19},{19,3},{4,20},{20... | collective-permute-start | bytes 5505032 | tf_op jit(solution)/shard_map/ppermute | solution.py:611

commit v10 on v9

--- a/solution.py
+++ b/solution.py
@@ -21,10 +21,12 @@
 
 def groups():
     four, lines = range(4), [(o, k) for o in range(4) for k in range(4)]
-    near = [[place(k, o, 0, 2 * p + b) for k in four for b in (0, 1)] for o, p in lines]
-    near += [[place(o, k, 1, 2 * p + 1 + b) for k in four for b in (0, 1)] for o, p in lines]
-    ring = [[place(o, k, 0, z) for k in four] for o in four for z in range(8)]
-    ring += [[place(k, o, 1, z) for k in four] for o in four for z in range(8)]
+    both = ((0, 0), (2, 1), (1, 1), (3, 0), (0, 1), (2, 0), (1, 0), (3, 1))
+    turn = (0, 1, 3, 2)
+    near = [[place(k, o, 0, 2 * p + b) for k, b in both] for o, p in lines]
+    near += [[place(o, k, 1, 2 * p + 1 + b) for k, b in both] for o, p in lines]
+    ring = [[place(o, k, 0, z) for k in turn] for o in four for z in range(8)]
+    ring += [[place(k, o, 1, z) for k in turn] for o in four for z in range(8)]
     far = [[place(x, y, c, 2 * p + b + c) for p in four] for x, y in lines for c in (0, 1) for b in (0, 1)]
     return near, ring, far
 VMEM = pl.BlockSpec(memory_space=pltpu.VMEM)

time: 101 us -> 100 us (0.990)
  blocking collectives: 56 us -> 53.9 us
    all_to_all x4, blocking collectives: 56 us -> 53.9 us  [swap(): return lax.all_to_all(rows, ALL, 0, 0, axis_index_groups=groups, tiled=True)]
where the time goes in v10:
time: 100 us; the launch traced here: 99.9 us
  blocking collectives  53.9 us (54%)
  starting transfers between devices  24.8 us (25%)
  Pallas kernels  14.5 us (14%)
  waiting for transfers between devices  5.93 us (6%)
    all_to_all x4, blocking collectives, swap(): return lax.all_to_all(rows, ALL, 0, 0, axis_index_groups=groups, tiled=True)  53.9 us
    ppermute x7, starting transfers between devices, exchange(): lax.ppermute(block, axes[step], pairs(lax.axis_size(axes[step]), first[st...  17.6 us
    ppermute x7, waiting for transfers between devices, exchange(): lax.ppermute(block, axes[step], pairs(lax.axis_size(axes[step]), first[st...  4.14 us
    all_to_all x1, starting transfers between devices, swap(): return lax.all_to_all(rows, ALL, 0, 0, axis_index_groups=groups, tiled=True)  3.63 us
    pallas_call x1, Pallas kernels, layer(): call(layer_kernel, [shape((half - later, width)), on_nodes] + on_sums + [...  3.27 us
    pallas_call x1, Pallas kernels, load(): call(load_kernel, [shape((count, width)), shape((lines, width))] * 2 + [s...  2.39 us
    ppermute x1, starting transfers between devices, local(): other = lax.ppermute(mine, 'c', pairs(2, 0))  2.21 us
  transfers between devices with their start and end apart: 11, of which 4 were waited for; matrix products, arithmetic and copies ran while one was open for 0% of the time, Pallas kernels for 7%

profile of v10, /device:TPU:1, one launch (start us, length us, event | category | flops | bytes accessed | tf_op | source)
XLA Modules:
  0.0 99.9 jit_solution(15679331925422377067)
XLA Ops:
  0.6 1.1 %shard_map.162 = (bf16[16,512]{1,0:T(8,128)(2,1)S(1)}, bf16[16,512]{1,0:T(8,128)(2,1)S(1)}, bf16[16,512]{1,0:T(8,128)(2,1)S(1)}, bf16[16,512]{1,0:T(8,128)(2,1)S(1)}) custom-call(bf16[1,1,64,512]{3,2,1,0:T(8,128)(2,1)} %nodes_hbm.3, s32[1,1,4,16]{3,2,1,0:T(4,128)} %lists.1), custom_call_target="tpu_custom_call" | custom-call | tf_op jit(solution)/shard_map/pallas_call | solution.py:577
  1.7 7.5 %collective-permute-start = (bf16[16,512]{1,0:T(8,128)(2,1)S(1)}, bf16[16,512]{1,0:T(8,128)(2,1)S(1)}, u32[]{:S(2)}, u32[]{:S(2)}) collective-permute-start(bf16[16,512]{1,0:T(8,128)(2,1)S(1)} %get-tuple-element.72), channel_id=1, source_target_pairs={{1,2},{2,1},{3,4},{4,3},{5,6},{6,5},{7,8},{8,7},{9,10},{10,9},{11,... | collective-permute-start | bytes 49160 | tf_op jit(solution)/shard_map/ppermute | solution.py:481
  9.2 2.1 %collective-permute-start.1 = (bf16[16,512]{1,0:T(8,128)(2,1)S(1)}, bf16[16,512]{1,0:T(8,128)(2,1)S(1)}, u32[]{:S(2)}, u32[]{:S(2)}) collective-permute-start(bf16[16,512]{1,0:T(8,128)(2,1)S(1)} %get-tuple-element.73), channel_id=1, source_target_pairs={{16,32},{32,16},{48,64},{64,48},{80,96},{96,80},{112,128},{128,112... | collective-permute-start | bytes 49160 | tf_op jit(solution)/shard_map/ppermute | solution.py:481
  11.3 3.2 %collective-permute-start.2 = (bf16[16,512]{1,0:T(8,128)(2,1)S(1)}, bf16[16,512]{1,0:T(8,128)(2,1)S(1)}, u32[]{:S(2)}, u32[]{:S(2)}) collective-permute-start(bf16[16,512]{1,0:T(8,128)(2,1)S(1)} %get-tuple-element.74), channel_id=1, source_target_pairs={{0,16},{16,0},{32,48},{48,32},{64,80},{80,64},{96,112},{112,96},{1... | collective-permute-start | bytes 49160 | tf_op jit(solution)/shard_map/ppermute | solution.py:481
  14.4 2.4 %shard_map.163 = (bf16[64,512]{1,0:T(8,128)(2,1)S(1)}, bf16[384,512]{1,0:T(8,128)(2,1)S(1)}, bf16[64,512]{1,0:T(8,128)(2,1)S(1)}, bf16[384,512]{1,0:T(8,128)(2,1...) custom-call(bf16[16,512]{1,0:T(8,128)(2,1)S(1)} %get-tuple-element.6, ...), custom_call_target="tpu_custom_call" | custom-call | tf_op jit(solution)/shard_map/pallas_call | solution.py:494
  17.0 3.3 %shard_map.164 = (bf16[1024,512]{1,0:T(8,128)(2,1)S(1)}, bf16[64,512]{1,0:T(8,128)(2,1)S(1)}, bf16[256,512]{1,0:T(8,128)(2,1)S(1)}, bf16[128,512]{1,0:T(8,128)(2...) custom-call(bf16[16,512]{1,0:T(8,128)(2,1)S(1)} %collective-permute-, ...), custom_call_target="tpu_custom_call" | custom-call | tf_op jit(solution)/shard_map/pallas_call | solution.py:523
  20.3 1.2 %collective-permute-start.4 = (bf16[1024,512]{1,0:T(8,128)(2,1)S(1)}, bf16[1024,512]{1,0:T(8,128)(2,1)S(1)}, u32[]{:S(2)}, u32[]{:S(2)}) collective-permute-start(bf16[1024,512]{1,0:T(8,128)(2,1)S(1)} %get-tuple-element.99), channel_id=1, source_target_pairs={{0,16},{16,0},{1,17},{17,1},{2,18},{18,2},{3,19},{19,3},{4,20},{20... | collective-permute-start | bytes 3145736 | tf_op jit(solution)/shard_map/ppermute | solution.py:532
  21.5 1.1 %shard_map.165 = (bf16[784,512]{1,0:T(8,128)(2,1)S(1)}, bf16[384,512]{1,0:T(8,128)(2,1)S(1)}, bf16[256,512]{1,0:T(8,128)(2,1)S(1)}, bf16[128,512]{1,0:T(8,128)(2,1)S(1)}) custom-call(bf16[384,512]{1,0:T(8,128)(2,1)S(1)} %get-tuple-element.68.edge, bf16[1536,512]{1,0:T(8,128)(2,1)S(1)} %get-tuple-element.70.w_edge1, ...), custom_call_target="tpu_custom_call" | custom-call | flops 671088640 | bytes 12582912 | tf_op jit(solution)/shard_map/pallas_call | solution.py:534
  22.7 2.0 %shard_map.166 = (bf16[1792,512]{1,0:T(8,128)(2,1)S(1)}, bf16[1,1,64,512]{3,2,1,0:T(8,128)(2,1)}, bf16[1,1,384,512]{3,2,1,0:T(8,128)(2,1)}, f32[64,512]{1,0:T(8,...) custom-call(bf16[64,512]{1,0:T(8,128)(2,1)S(1)} %get-tuple-element.67.node, ...), custom_call_target="tpu_custom_call" | custom-call | flops 1342177280 | bytes 12582912 | tf_op jit(solution)/shard_map/pallas_call | solution.py:542
  24.7 0.3 collective-permute-done.5.later
  25.0 0.4 shard_map.167
  25.5 18.3 %all_to_all.33.parts = bf16[8,224,512]{2,1,0:T(8,128)(2,1)S(1)} all-to-all(bf16[8,224,512]{2,1,0:T(8,128)(2,1)S(1)} %bitcast.6), channel_id=1, replica_groups={{0,65,33,96,1,64,32,97},{2,67,35,98,3,66,34,99},{4,69,37,100,5,68,36,10..., dimensions={0} | all-to-all | bytes 3670016 | tf_op jit(solution)/shard_map/all_to_all | solution.py:487
  43.9 8.3 %all_to_all.34.parts = bf16[4,56,512]{2,1,0:T(8,128)(2,1)S(1)} all-to-all(bf16[4,56,512]{2,1,0:T(8,128)(2,1)S(1)} %bitcast.7), channel_id=1, replica_groups={{0,8,136,128},{1,9,137,129},{2,10,138,130},{3,11,139,131},{4,12,140,132..., dimensions={0} | all-to-all | bytes 458752 | tf_op jit(solution)/shard_map/all_to_all | solution.py:487
  52.2 0.7 shard_map.169
  53.0 3.6 %all-to-all-start.2 = ((bf16[4,56,512]{2,1,0:T(8,128)(2,1)}), bf16[4,56,512]{2,1,0:T(8,128)(2,1)S(1)}, u32[]{:S(2)}, u32[]{:S(2)}) async-start(bf16[4,56,512]{2,1,0:T(8,128)(2,1)} %get-tuple-element.105), calls=%async_computation.2 | async-start | bytes 458752 | tf_op jit(solution)/shard_map/all_to_all | solution.py:487
  56.6 2.9 %collective-permute-start.6 = (bf16[16,512]{1,0:T(8,128)(2,1)S(1)}, bf16[16,512]{1,0:T(8,128)(2,1)S(1)}, u32[]{:S(2)}, u32[]{:S(2)}) collective-permute-start(bf16[16,512]{1,0:T(8,128)(2,1)S(1)} %get-tuple-element.106), channel_id=1, source_target_pairs={{1,2},{2,1},{3,4},{4,3},{5,6},{6,5},{7,8},{8,7},{9,10},{10,9},{11,... | collective-permute-start | bytes 49160 | tf_op jit(solution)/shard_map/ppermute | solution.py:481
  59.5 2.0 %collective-permute-start.7 = (bf16[16,512]{1,0:T(8,128)(2,1)S(1)}, bf16[16,512]{1,0:T(8,128)(2,1)S(1)}, u32[]{:S(2)}, u32[]{:S(2)}) collective-permute-start(bf16[16,512]{1,0:T(8,128)(2,1)S(1)} %get-tuple-element.107), channel_id=1, source_target_pairs={{16,32},{32,16},{48,64},{64,48},{80,96},{96,80},{112,128},{128,112... | collective-permute-start | bytes 49160 | tf_op jit(solution)/shard_map/ppermute | solution.py:481
  61.5 4.0 %collective-permute-done.6.refs_0_ = bf16[16,512]{1,0:T(8,128)(2,1)S(1)} collective-permute-done((bf16[16,512]{1,0:T(8,128)(2,1)S(1)}, bf16[16,512]{1,0:T(8,128)(2,1)S(1)}, u32[]{:S(2)}, u32[]{:S(2)}) %collective-permute-start.6) | collective-permute-done | bytes 16416 | tf_op jit(solution)/shard_map/ppermute | solution.py:481
  65.5 8.5 %all_to_all.35 = bf16[4,56,512]{2,1,0:T(8,128)(2,1)S(1)} all-to-all(bf16[4,56,512]{2,1,0:T(8,128)(2,1)S(1)} %get-tuple-element.109), channel_id=1, replica_groups={{0,8,136,128},{1,9,137,129},{2,10,138,130},{3,11,139,131},{4,12,140,132..., dimensions={0} | all-to-all | bytes 458752 | tf_op jit(solution)/shard_map/all_to_all | solution.py:487
  74.1 18.9 %all_to_all.36 = bf16[8,224,512]{2,1,0:T(8,128)(2,1)S(1)} all-to-all(bf16[8,224,512]{2,1,0:T(8,128)(2,1)S(1)} %shard_map.171), channel_id=1, replica_groups={{0,65,33,96,1,64,32,97},{2,67,35,98,3,66,34,99},{4,69,37,100,5,68,36,10..., dimensions={0} | all-to-all | bytes 3670016 | tf_op jit(solution)/shard_map/all_to_all | solution.py:487
  93.0 2.2 %collective-permute-start.9 = (bf16[1792,512]{1,0:T(8,128)(2,1)S(1)}, bf16[1792,512]{1,0:T(8,128)(2,1)S(1)}, u32[]{:S(2)}, u32[]{:S(2)}) collective-permute-start(bf16[1792,512]{1,0:T(8,128)(2,1)S(1)} %bitcast.4), channel_id=1, source_target_pairs={{0,16},{16,0},{1,17},{17,1},{2,18},{18,2},{3,19},{19,3},{4,20},{20... | collective-permute-start | bytes 5505032 | tf_op jit(solution)/shard_map/ppermute | solution.py:613
  95.3 1.9 %shard_map.172 = (bf16[1536,512]{1,0:T(8,128)(2,1)}, bf16[512,512]{1,0:T(8,128)(2,1)}, bf16[1024,512]{1,0:T(8,128)(2,1)}, bf16[512,512]{1,0:T(8,128)(2,1)}, bf16[1,1,64,512]{3,2,1,0:T(8,128)(2,1)}) custom-call(bf16[1792,512]{1,0:T(8,128)(2,1)S(1)} %bitcast.5, f32[64,512]{1,0:T(8,128)S(1)} %get-tuple-element.110.d_node, s32[1,1,4,16]{3,2,1,0:T(4,128)S(1)} %copy-done, ...), custom_call_target="tpu_custom_call" | custom-call | tf_op jit(solution)/shard_map/pallas_call | solution.py:617
  97.2 1.5 %collective-permute-done.9.half = bf16[1792,512]{1,0:T(8,128)(2,1)S(1)} collective-permute-done((bf16[1792,512]{1,0:T(8,128)(2,1)S(1)}, bf16[1792,512]{1,0:T(8,128)(2,1)S(1)}, u32[]{:S(2)}, u32[]{:S(2)}) %collective-permute-start.9) | collective-permute-done | bytes 1835040 | tf_op jit(solution)/shard_map/ppermute | solution.py:613
  98.7 1.3 %shard_map.173 = (bf16[1536,512]{1,0:T(8,128)(2,1)}, bf16[512,512]{1,0:T(8,128)(2,1)}, bf16[1024,512]{1,0:T(8,128)(2,1)}, bf16[512,512]{1,0:T(8,128)(2,1)}) custom-call(bf16[1792,512]{1,0:T(8,128)(2,1)S(1)} %collective-permute-done.9.half, ...), custom_call_target="tpu_custom_call", output_to_operand_aliasing={{0}: (1, {}), {1}: (2, {}), {2}: (3, {}), {3}: (4, {})} | custom-call | tf_op jit(solution)/shard_map/pallas_call | solution.py:625
  (16 shorter events, 0.7 us)
Async XLA Ops:
  1.7 15.1 %collective-permute-start = (bf16[16,512]{1,0:T(8,128)(2,1)S(1)}, bf16[16,512]{1,0:T(8,128)(2,1)S(1)}, u32[]{:S(2)}, u32[]{:S(2)}) collective-permute-start(bf16[16,512]{1,0:T(8,128)(2,1)S(1)} %get-tuple-element.72), channel_id=1, source_target_pairs={{1,2},{2,1},{3,4},{4,3},{5,6},{6,5},{7,8},{8,7},{9,10},{10,9},{11,... | collective-permute-start | bytes 49160 | tf_op jit(solution)/shard_map/ppermute | solution.py:481
  9.2 7.6 %collective-permute-start.1 = (bf16[16,512]{1,0:T(8,128)(2,1)S(1)}, bf16[16,512]{1,0:T(8,128)(2,1)S(1)}, u32[]{:S(2)}, u32[]{:S(2)}) collective-permute-start(bf16[16,512]{1,0:T(8,128)(2,1)S(1)} %get-tuple-element.73), channel_id=1, source_target_pairs={{16,32},{32,16},{48,64},{64,48},{80,96},{96,80},{112,128},{128,112... | collective-permute-start | bytes 49160 | tf_op jit(solution)/shard_map/ppermute | solution.py:481
  11.3 5.6 %collective-permute-start.2 = (bf16[16,512]{1,0:T(8,128)(2,1)S(1)}, bf16[16,512]{1,0:T(8,128)(2,1)S(1)}, u32[]{:S(2)}, u32[]{:S(2)}) collective-permute-start(bf16[16,512]{1,0:T(8,128)(2,1)S(1)} %get-tuple-element.74), channel_id=1, source_target_pairs={{0,16},{16,0},{32,48},{48,32},{64,80},{80,64},{96,112},{112,96},{1... | collective-permute-start | bytes 49160 | tf_op jit(solution)/shard_map/ppermute | solution.py:481
  14.4 2.6 %collective-permute-start.3 = (bf16[16,512]{1,0:T(8,128)(2,1)S(1)}, bf16[16,512]{1,0:T(8,128)(2,1)S(1)}, u32[]{:S(2)}, u32[]{:S(2)}) collective-permute-start(bf16[16,512]{1,0:T(8,128)(2,1)S(1)} %get-tuple-element.66.packs), channel_id=1, source_target_pairs={{0,1},{1,0},{2,3},{3,2},{4,5},{5,4},{6,7},{7,6},{8,9},{9,8},{10,11... | collective-permute-start | bytes 49160 | tf_op jit(solution)/shard_map/ppermute | solution.py:481
  20.3 4.7 %collective-permute-start.4 = (bf16[1024,512]{1,0:T(8,128)(2,1)S(1)}, bf16[1024,512]{1,0:T(8,128)(2,1)S(1)}, u32[]{:S(2)}, u32[]{:S(2)}) collective-permute-start(bf16[1024,512]{1,0:T(8,128)(2,1)S(1)} %get-tuple-element.99), channel_id=1, source_target_pairs={{0,16},{16,0},{1,17},{17,1},{2,18},{18,2},{3,19},{19,3},{4,20},{20... | collective-permute-start | bytes 3145736 | tf_op jit(solution)/shard_map/ppermute | solution.py:532
  22.6 2.4 %collective-permute-start.5 = (bf16[784,512]{1,0:T(8,128)(2,1)S(1)}, bf16[784,512]{1,0:T(8,128)(2,1)S(1)}, u32[]{:S(2)}, u32[]{:S(2)}) collective-permute-start(bf16[784,512]{1,0:T(8,128)(2,1)S(1)} %get-tuple-element.100), channel_id=1, source_target_pairs={{0,16},{16,0},{1,17},{17,1},{2,18},{18,2},{3,19},{19,3},{4,20},{20... | collective-permute-start | bytes 2408456 | tf_op jit(solution)/shard_map/ppermute | solution.py:541
  53.0 12.5 %all-to-all-start.2 = ((bf16[4,56,512]{2,1,0:T(8,128)(2,1)}), bf16[4,56,512]{2,1,0:T(8,128)(2,1)S(1)}, u32[]{:S(2)}, u32[]{:S(2)}) async-start(bf16[4,56,512]{2,1,0:T(8,128)(2,1)} %get-tuple-element.105), calls=%async_computation.2 | async-start | bytes 458752 | tf_op jit(solution)/shard_map/all_to_all | solution.py:487
  56.6 8.9 %collective-permute-start.6 = (bf16[16,512]{1,0:T(8,128)(2,1)S(1)}, bf16[16,512]{1,0:T(8,128)(2,1)S(1)}, u32[]{:S(2)}, u32[]{:S(2)}) collective-permute-start(bf16[16,512]{1,0:T(8,128)(2,1)S(1)} %get-tuple-element.106), channel_id=1, source_target_pairs={{1,2},{2,1},{3,4},{4,3},{5,6},{6,5},{7,8},{8,7},{9,10},{10,9},{11,... | collective-permute-start | bytes 49160 | tf_op jit(solution)/shard_map/ppermute | solution.py:481
  59.5 6.0 %collective-permute-start.7 = (bf16[16,512]{1,0:T(8,128)(2,1)S(1)}, bf16[16,512]{1,0:T(8,128)(2,1)S(1)}, u32[]{:S(2)}, u32[]{:S(2)}) collective-permute-start(bf16[16,512]{1,0:T(8,128)(2,1)S(1)} %get-tuple-element.107), channel_id=1, source_target_pairs={{16,32},{32,16},{48,64},{64,48},{80,96},{96,80},{112,128},{128,112... | collective-permute-start | bytes 49160 | tf_op jit(solution)/shard_map/ppermute | solution.py:481
  61.5 4.0 %collective-permute-start.8 = (bf16[16,512]{1,0:T(8,128)(2,1)S(1)}, bf16[16,512]{1,0:T(8,128)(2,1)S(1)}, u32[]{:S(2)}, u32[]{:S(2)}) collective-permute-start(bf16[16,512]{1,0:T(8,128)(2,1)S(1)} %get-tuple-element.108), channel_id=1, source_target_pairs={{0,1},{1,0},{2,3},{3,2},{4,5},{5,4},{6,7},{7,6},{8,9},{9,8},{10,11... | collective-permute-start | bytes 49160 | tf_op jit(solution)/shard_map/ppermute | solution.py:481
  74.1 21.2 %copy-start = (s32[1,1,4,16]{3,2,1,0:T(4,128)S(1)}, s32[1,1,4,16]{3,2,1,0:T(4,128)}, u32[]{:S(2)}) copy-start(s32[1,1,4,16]{3,2,1,0:T(4,128)} %lists.1) | copy-start | bytes 772
  93.0 5.6 %collective-permute-start.9 = (bf16[1792,512]{1,0:T(8,128)(2,1)S(1)}, bf16[1792,512]{1,0:T(8,128)(2,1)S(1)}, u32[]{:S(2)}, u32[]{:S(2)}) collective-permute-start(bf16[1792,512]{1,0:T(8,128)(2,1)S(1)} %bitcast.4), channel_id=1, source_target_pairs={{0,16},{16,0},{1,17},{17,1},{2,18},{18,2},{3,19},{19,3},{4,20},{20... | collective-permute-start | bytes 5505032 | tf_op jit(solution)/shard_map/ppermute | solution.py:613

commit v11 on v10

--- a/solution.py
+++ b/solution.py
@@ -21,7 +21,7 @@
 
 def groups():
     four, lines = range(4), [(o, k) for o in range(4) for k in range(4)]
-    both = ((0, 0), (2, 1), (1, 1), (3, 0), (0, 1), (2, 0), (1, 0), (3, 1))
+    both = ((0, 0), (3, 1), (2, 0), (1, 1), (0, 1), (3, 0), (2, 1), (1, 0))
     turn = (0, 1, 3, 2)
     near = [[place(k, o, 0, 2 * p + b) for k, b in both] for o, p in lines]
     near += [[place(o, k, 1, 2 * p + 1 + b) for k, b in both] for o, p in lines]

time: 100 us -> 101 us (1.010)
  blocking collectives: 53.9 us -> 55 us
    all_to_all x4, blocking collectives: 53.9 us -> 55 us  [swap(): return lax.all_to_all(rows, ALL, 0, 0, axis_index_groups=groups, tiled=True)]
where the time goes in v11:
time: 101 us; the launch traced here: 100 us
  blocking collectives  55 us (54%)
  starting transfers between devices  24.3 us (24%)
  Pallas kernels  14.5 us (14%)
  waiting for transfers between devices  5.62 us (6%)
    all_to_all x4, blocking collectives, swap(): return lax.all_to_all(rows, ALL, 0, 0, axis_index_groups=groups, tiled=True)  55 us
    ppermute x7, starting transfers between devices, exchange(): lax.ppermute(block, axes[step], pairs(lax.axis_size(axes[step]), first[st...  17.5 us
    ppermute x7, waiting for transfers between devices, exchange(): lax.ppermute(block, axes[step], pairs(lax.axis_size(axes[step]), first[st...  3.83 us
    all_to_all x1, starting transfers between devices, swap(): return lax.all_to_all(rows, ALL, 0, 0, axis_index_groups=groups, tiled=True)  3.63 us
    pallas_call x1, Pallas kernels, layer(): call(layer_kernel, [shape((half - later, width)), on_nodes] + on_sums + [...  3.27 us
    pallas_call x1, Pallas kernels, load(): call(load_kernel, [shape((count, width)), shape((lines, width))] * 2 + [s...  2.39 us
  transfers between devices with their start and end apart: 11, of which 4 were waited for; matrix products, arithmetic and copies ran while one was open for 0% of the time, Pallas kernels for 7%

profile of v11, /device:TPU:1, one launch (start us, length us, event | category | flops | bytes accessed | tf_op | source)
XLA Modules:
  0.0 100.2 jit_solution(2266174598229892547)
XLA Ops:
  0.6 1.1 %shard_map.162 = (bf16[16,512]{1,0:T(8,128)(2,1)S(1)}, bf16[16,512]{1,0:T(8,128)(2,1)S(1)}, bf16[16,512]{1,0:T(8,128)(2,1)S(1)}, bf16[16,512]{1,0:T(8,128)(2,1)S(1)}) custom-call(bf16[1,1,64,512]{3,2,1,0:T(8,128)(2,1)} %nodes_hbm.3, s32[1,1,4,16]{3,2,1,0:T(4,128)} %lists.1), custom_call_target="tpu_custom_call" | custom-call | tf_op jit(solution)/shard_map/pallas_call | solution.py:577
  1.7 7.5 %collective-permute-start = (bf16[16,512]{1,0:T(8,128)(2,1)S(1)}, bf16[16,512]{1,0:T(8,128)(2,1)S(1)}, u32[]{:S(2)}, u32[]{:S(2)}) collective-permute-start(bf16[16,512]{1,0:T(8,128)(2,1)S(1)} %get-tuple-element.72), channel_id=1, source_target_pairs={{1,2},{2,1},{3,4},{4,3},{5,6},{6,5},{7,8},{8,7},{9,10},{10,9},{11,... | collective-permute-start | bytes 49160 | tf_op jit(solution)/shard_map/ppermute | solution.py:481
  9.2 2.1 %collective-permute-start.1 = (bf16[16,512]{1,0:T(8,128)(2,1)S(1)}, bf16[16,512]{1,0:T(8,128)(2,1)S(1)}, u32[]{:S(2)}, u32[]{:S(2)}) collective-permute-start(bf16[16,512]{1,0:T(8,128)(2,1)S(1)} %get-tuple-element.73), channel_id=1, source_target_pairs={{16,32},{32,16},{48,64},{64,48},{80,96},{96,80},{112,128},{128,112... | collective-permute-start | bytes 49160 | tf_op jit(solution)/shard_map/ppermute | solution.py:481
  11.3 3.2 %collective-permute-start.2 = (bf16[16,512]{1,0:T(8,128)(2,1)S(1)}, bf16[16,512]{1,0:T(8,128)(2,1)S(1)}, u32[]{:S(2)}, u32[]{:S(2)}) collective-permute-start(bf16[16,512]{1,0:T(8,128)(2,1)S(1)} %get-tuple-element.74), channel_id=1, source_target_pairs={{0,16},{16,0},{32,48},{48,32},{64,80},{80,64},{96,112},{112,96},{1... | collective-permute-start | bytes 49160 | tf_op jit(solution)/shard_map/ppermute | solution.py:481
  14.4 2.4 %shard_map.163 = (bf16[64,512]{1,0:T(8,128)(2,1)S(1)}, bf16[384,512]{1,0:T(8,128)(2,1)S(1)}, bf16[64,512]{1,0:T(8,128)(2,1)S(1)}, bf16[384,512]{1,0:T(8,128)(2,1...) custom-call(bf16[16,512]{1,0:T(8,128)(2,1)S(1)} %get-tuple-element.6, ...), custom_call_target="tpu_custom_call" | custom-call | tf_op jit(solution)/shard_map/pallas_call | solution.py:494
  17.0 3.3 %shard_map.164 = (bf16[1024,512]{1,0:T(8,128)(2,1)S(1)}, bf16[64,512]{1,0:T(8,128)(2,1)S(1)}, bf16[256,512]{1,0:T(8,128)(2,1)S(1)}, bf16[128,512]{1,0:T(8,128)(2...) custom-call(bf16[16,512]{1,0:T(8,128)(2,1)S(1)} %collective-permute-, ...), custom_call_target="tpu_custom_call" | custom-call | tf_op jit(solution)/shard_map/pallas_call | solution.py:523
  20.3 1.2 %collective-permute-start.4 = (bf16[1024,512]{1,0:T(8,128)(2,1)S(1)}, bf16[1024,512]{1,0:T(8,128)(2,1)S(1)}, u32[]{:S(2)}, u32[]{:S(2)}) collective-permute-start(bf16[1024,512]{1,0:T(8,128)(2,1)S(1)} %get-tuple-element.99), channel_id=1, source_target_pairs={{0,16},{16,0},{1,17},{17,1},{2,18},{18,2},{3,19},{19,3},{4,20},{20... | collective-permute-start | bytes 3145736 | tf_op jit(solution)/shard_map/ppermute | solution.py:532
  21.5 1.1 %shard_map.165 = (bf16[784,512]{1,0:T(8,128)(2,1)S(1)}, bf16[384,512]{1,0:T(8,128)(2,1)S(1)}, bf16[256,512]{1,0:T(8,128)(2,1)S(1)}, bf16[128,512]{1,0:T(8,128)(2,1)S(1)}) custom-call(bf16[384,512]{1,0:T(8,128)(2,1)S(1)} %get-tuple-element.68.edge, bf16[1536,512]{1,0:T(8,128)(2,1)S(1)} %get-tuple-element.70.w_edge1, ...), custom_call_target="tpu_custom_call" | custom-call | flops 671088640 | bytes 12582912 | tf_op jit(solution)/shard_map/pallas_call | solution.py:534
  22.7 2.0 %shard_map.166 = (bf16[1792,512]{1,0:T(8,128)(2,1)S(1)}, bf16[1,1,64,512]{3,2,1,0:T(8,128)(2,1)}, bf16[1,1,384,512]{3,2,1,0:T(8,128)(2,1)}, f32[64,512]{1,0:T(8,...) custom-call(bf16[64,512]{1,0:T(8,128)(2,1)S(1)} %get-tuple-element.67.node, ...), custom_call_target="tpu_custom_call" | custom-call | flops 1342177280 | bytes 12582912 | tf_op jit(solution)/shard_map/pallas_call | solution.py:542
  24.7 0.3 collective-permute-done.5.later
  25.0 0.4 shard_map.167
  25.5 18.5 %all_to_all.33.parts = bf16[8,224,512]{2,1,0:T(8,128)(2,1)S(1)} all-to-all(bf16[8,224,512]{2,1,0:T(8,128)(2,1)S(1)} %bitcast.6), channel_id=1, replica_groups={{0,97,64,33,1,96,65,32},{2,99,66,35,3,98,67,34},{4,101,68,37,5,100,69,3..., dimensions={0} | all-to-all | bytes 3670016 | tf_op jit(solution)/shard_map/all_to_all | solution.py:487
  44.2 8.1 %all_to_all.34.parts = bf16[4,56,512]{2,1,0:T(8,128)(2,1)S(1)} all-to-all(bf16[4,56,512]{2,1,0:T(8,128)(2,1)S(1)} %bitcast.7), channel_id=1, replica_groups={{0,8,136,128},{1,9,137,129},{2,10,138,130},{3,11,139,131},{4,12,140,132..., dimensions={0} | all-to-all | bytes 458752 | tf_op jit(solution)/shard_map/all_to_all | solution.py:487
  52.4 0.7 shard_map.169
  53.1 3.6 %all-to-all-start.2 = ((bf16[4,56,512]{2,1,0:T(8,128)(2,1)}), bf16[4,56,512]{2,1,0:T(8,128)(2,1)S(1)}, u32[]{:S(2)}, u32[]{:S(2)}) async-start(bf16[4,56,512]{2,1,0:T(8,128)(2,1)} %get-tuple-element.105), calls=%async_computation.2 | async-start | bytes 458752 | tf_op jit(solution)/shard_map/all_to_all | solution.py:487
  56.7 2.9 %collective-permute-start.6 = (bf16[16,512]{1,0:T(8,128)(2,1)S(1)}, bf16[16,512]{1,0:T(8,128)(2,1)S(1)}, u32[]{:S(2)}, u32[]{:S(2)}) collective-permute-start(bf16[16,512]{1,0:T(8,128)(2,1)S(1)} %get-tuple-element.106), channel_id=1, source_target_pairs={{1,2},{2,1},{3,4},{4,3},{5,6},{6,5},{7,8},{8,7},{9,10},{10,9},{11,... | collective-permute-start | bytes 49160 | tf_op jit(solution)/shard_map/ppermute | solution.py:481
  59.6 1.9 %collective-permute-start.7 = (bf16[16,512]{1,0:T(8,128)(2,1)S(1)}, bf16[16,512]{1,0:T(8,128)(2,1)S(1)}, u32[]{:S(2)}, u32[]{:S(2)}) collective-permute-start(bf16[16,512]{1,0:T(8,128)(2,1)S(1)} %get-tuple-element.107), channel_id=1, source_target_pairs={{16,32},{32,16},{48,64},{64,48},{80,96},{96,80},{112,128},{128,112... | collective-permute-start | bytes 49160 | tf_op jit(solution)/shard_map/ppermute | solution.py:481
  61.5 3.7 %collective-permute-done.6.refs_0_ = bf16[16,512]{1,0:T(8,128)(2,1)S(1)} collective-permute-done((bf16[16,512]{1,0:T(8,128)(2,1)S(1)}, bf16[16,512]{1,0:T(8,128)(2,1)S(1)}, u32[]{:S(2)}, u32[]{:S(2)}) %collective-permute-start.6) | collective-permute-done | bytes 16416 | tf_op jit(solution)/shard_map/ppermute | solution.py:481
  65.2 9.1 %all_to_all.35 = bf16[4,56,512]{2,1,0:T(8,128)(2,1)S(1)} all-to-all(bf16[4,56,512]{2,1,0:T(8,128)(2,1)S(1)} %get-tuple-element.109), channel_id=1, replica_groups={{0,8,136,128},{1,9,137,129},{2,10,138,130},{3,11,139,131},{4,12,140,132..., dimensions={0} | all-to-all | bytes 458752 | tf_op jit(solution)/shard_map/all_to_all | solution.py:487
  74.4 19.2 %all_to_all.36 = bf16[8,224,512]{2,1,0:T(8,128)(2,1)S(1)} all-to-all(bf16[8,224,512]{2,1,0:T(8,128)(2,1)S(1)} %shard_map.171), channel_id=1, replica_groups={{0,97,64,33,1,96,65,32},{2,99,66,35,3,98,67,34},{4,101,68,37,5,100,69,3..., dimensions={0} | all-to-all | bytes 3670016 | tf_op jit(solution)/shard_map/all_to_all | solution.py:487
  93.6 1.9 %collective-permute-start.9 = (bf16[1792,512]{1,0:T(8,128)(2,1)S(1)}, bf16[1792,512]{1,0:T(8,128)(2,1)S(1)}, u32[]{:S(2)}, u32[]{:S(2)}) collective-permute-start(bf16[1792,512]{1,0:T(8,128)(2,1)S(1)} %bitcast.4), channel_id=1, source_target_pairs={{0,16},{16,0},{1,17},{17,1},{2,18},{18,2},{3,19},{19,3},{4,20},{20... | collective-permute-start | bytes 5505032 | tf_op jit(solution)/shard_map/ppermute | solution.py:613
  95.5 1.9 %shard_map.172 = (bf16[1536,512]{1,0:T(8,128)(2,1)}, bf16[512,512]{1,0:T(8,128)(2,1)}, bf16[1024,512]{1,0:T(8,128)(2,1)}, bf16[512,512]{1,0:T(8,128)(2,1)}, bf16[1,1,64,512]{3,2,1,0:T(8,128)(2,1)}) custom-call(bf16[1792,512]{1,0:T(8,128)(2,1)S(1)} %bitcast.5, f32[64,512]{1,0:T(8,128)S(1)} %get-tuple-element.110.d_node, s32[1,1,4,16]{3,2,1,0:T(4,128)S(1)} %copy-done, ...), custom_call_target="tpu_custom_call" | custom-call | tf_op jit(solution)/shard_map/pallas_call | solution.py:617
  97.4 1.5 %collective-permute-done.9.half = bf16[1792,512]{1,0:T(8,128)(2,1)S(1)} collective-permute-done((bf16[1792,512]{1,0:T(8,128)(2,1)S(1)}, bf16[1792,512]{1,0:T(8,128)(2,1)S(1)}, u32[]{:S(2)}, u32[]{:S(2)}) %collective-permute-start.9) | collective-permute-done | bytes 1835040 | tf_op jit(solution)/shard_map/ppermute | solution.py:613
  98.9 1.3 %shard_map.173 = (bf16[1536,512]{1,0:T(8,128)(2,1)}, bf16[512,512]{1,0:T(8,128)(2,1)}, bf16[1024,512]{1,0:T(8,128)(2,1)}, bf16[512,512]{1,0:T(8,128)(2,1)}) custom-call(bf16[1792,512]{1,0:T(8,128)(2,1)S(1)} %collective-permute-done.9.half, ...), custom_call_target="tpu_custom_call", output_to_operand_aliasing={{0}: (1, {}), {1}: (2, {}), {2}: (3, {}), {3}: (4, {})} | custom-call | tf_op jit(solution)/shard_map/pallas_call | solution.py:625
  (16 shorter events, 0.7 us)
Async XLA Ops:
  1.7 15.1 %collective-permute-start = (bf16[16,512]{1,0:T(8,128)(2,1)S(1)}, bf16[16,512]{1,0:T(8,128)(2,1)S(1)}, u32[]{:S(2)}, u32[]{:S(2)}) collective-permute-start(bf16[16,512]{1,0:T(8,128)(2,1)S(1)} %get-tuple-element.72), channel_id=1, source_target_pairs={{1,2},{2,1},{3,4},{4,3},{5,6},{6,5},{7,8},{8,7},{9,10},{10,9},{11,... | collective-permute-start | bytes 49160 | tf_op jit(solution)/shard_map/ppermute | solution.py:481
  9.2 7.6 %collective-permute-start.1 = (bf16[16,512]{1,0:T(8,128)(2,1)S(1)}, bf16[16,512]{1,0:T(8,128)(2,1)S(1)}, u32[]{:S(2)}, u32[]{:S(2)}) collective-permute-start(bf16[16,512]{1,0:T(8,128)(2,1)S(1)} %get-tuple-element.73), channel_id=1, source_target_pairs={{16,32},{32,16},{48,64},{64,48},{80,96},{96,80},{112,128},{128,112... | collective-permute-start | bytes 49160 | tf_op jit(solution)/shard_map/ppermute | solution.py:481
  11.3 5.6 %collective-permute-start.2 = (bf16[16,512]{1,0:T(8,128)(2,1)S(1)}, bf16[16,512]{1,0:T(8,128)(2,1)S(1)}, u32[]{:S(2)}, u32[]{:S(2)}) collective-permute-start(bf16[16,512]{1,0:T(8,128)(2,1)S(1)} %get-tuple-element.74), channel_id=1, source_target_pairs={{0,16},{16,0},{32,48},{48,32},{64,80},{80,64},{96,112},{112,96},{1... | collective-permute-start | bytes 49160 | tf_op jit(solution)/shard_map/ppermute | solution.py:481
  14.4 2.6 %collective-permute-start.3 = (bf16[16,512]{1,0:T(8,128)(2,1)S(1)}, bf16[16,512]{1,0:T(8,128)(2,1)S(1)}, u32[]{:S(2)}, u32[]{:S(2)}) collective-permute-start(bf16[16,512]{1,0:T(8,128)(2,1)S(1)} %get-tuple-element.66.packs), channel_id=1, source_target_pairs={{0,1},{1,0},{2,3},{3,2},{4,5},{5,4},{6,7},{7,6},{8,9},{9,8},{10,11... | collective-permute-start | bytes 49160 | tf_op jit(solution)/shard_map/ppermute | solution.py:481
  20.3 4.7 %collective-permute-start.4 = (bf16[1024,512]{1,0:T(8,128)(2,1)S(1)}, bf16[1024,512]{1,0:T(8,128)(2,1)S(1)}, u32[]{:S(2)}, u32[]{:S(2)}) collective-permute-start(bf16[1024,512]{1,0:T(8,128)(2,1)S(1)} %get-tuple-element.99), channel_id=1, source_target_pairs={{0,16},{16,0},{1,17},{17,1},{2,18},{18,2},{3,19},{19,3},{4,20},{20... | collective-permute-start | bytes 3145736 | tf_op jit(solution)/shard_map/ppermute | solution.py:532
  22.6 2.4 %collective-permute-start.5 = (bf16[784,512]{1,0:T(8,128)(2,1)S(1)}, bf16[784,512]{1,0:T(8,128)(2,1)S(1)}, u32[]{:S(2)}, u32[]{:S(2)}) collective-permute-start(bf16[784,512]{1,0:T(8,128)(2,1)S(1)} %get-tuple-element.100), channel_id=1, source_target_pairs={{0,16},{16,0},{1,17},{17,1},{2,18},{18,2},{3,19},{19,3},{4,20},{20... | collective-permute-start | bytes 2408456 | tf_op jit(solution)/shard_map/ppermute | solution.py:541
  53.1 12.1 %all-to-all-start.2 = ((bf16[4,56,512]{2,1,0:T(8,128)(2,1)}), bf16[4,56,512]{2,1,0:T(8,128)(2,1)S(1)}, u32[]{:S(2)}, u32[]{:S(2)}) async-start(bf16[4,56,512]{2,1,0:T(8,128)(2,1)} %get-tuple-element.105), calls=%async_computation.2 | async-start | bytes 458752 | tf_op jit(solution)/shard_map/all_to_all | solution.py:487
  56.7 8.4 %collective-permute-start.6 = (bf16[16,512]{1,0:T(8,128)(2,1)S(1)}, bf16[16,512]{1,0:T(8,128)(2,1)S(1)}, u32[]{:S(2)}, u32[]{:S(2)}) collective-permute-start(bf16[16,512]{1,0:T(8,128)(2,1)S(1)} %get-tuple-element.106), channel_id=1, source_target_pairs={{1,2},{2,1},{3,4},{4,3},{5,6},{6,5},{7,8},{8,7},{9,10},{10,9},{11,... | collective-permute-start | bytes 49160 | tf_op jit(solution)/shard_map/ppermute | solution.py:481
  59.6 5.6 %collective-permute-start.7 = (bf16[16,512]{1,0:T(8,128)(2,1)S(1)}, bf16[16,512]{1,0:T(8,128)(2,1)S(1)}, u32[]{:S(2)}, u32[]{:S(2)}) collective-permute-start(bf16[16,512]{1,0:T(8,128)(2,1)S(1)} %get-tuple-element.107), channel_id=1, source_target_pairs={{16,32},{32,16},{48,64},{64,48},{80,96},{96,80},{112,128},{128,112... | collective-permute-start | bytes 49160 | tf_op jit(solution)/shard_map/ppermute | solution.py:481
  61.5 3.7 %collective-permute-start.8 = (bf16[16,512]{1,0:T(8,128)(2,1)S(1)}, bf16[16,512]{1,0:T(8,128)(2,1)S(1)}, u32[]{:S(2)}, u32[]{:S(2)}) collective-permute-start(bf16[16,512]{1,0:T(8,128)(2,1)S(1)} %get-tuple-element.108), channel_id=1, source_target_pairs={{0,1},{1,0},{2,3},{3,2},{4,5},{5,4},{6,7},{7,6},{8,9},{9,8},{10,11... | collective-permute-start | bytes 49160 | tf_op jit(solution)/shard_map/ppermute | solution.py:481
  74.4 21.1 %copy-start = (s32[1,1,4,16]{3,2,1,0:T(4,128)S(1)}, s32[1,1,4,16]{3,2,1,0:T(4,128)}, u32[]{:S(2)}) copy-start(s32[1,1,4,16]{3,2,1,0:T(4,128)} %lists.1) | copy-start | bytes 772
  93.6 5.3 %collective-permute-start.9 = (bf16[1792,512]{1,0:T(8,128)(2,1)S(1)}, bf16[1792,512]{1,0:T(8,128)(2,1)S(1)}, u32[]{:S(2)}, u32[]{:S(2)}) collective-permute-start(bf16[1792,512]{1,0:T(8,128)(2,1)S(1)} %bitcast.4), channel_id=1, source_target_pairs={{0,16},{16,0},{1,17},{17,1},{2,18},{18,2},{3,19},{19,3},{4,20},{20... | collective-permute-start | bytes 5505032 | tf_op jit(solution)/shard_map/ppermute | solution.py:613
